TPU v7x, 32 devices: a whole 2x2x4 slice. The times are simulated.
32 devices in a mesh: seg: 16 (over z, y, core), item: 2 (over x).
Axes of the slice: x: 2, y: 2, z: 4, core: 2. Of those that a mesh axis runs over, the one named last changes fastest.
Arguments:
- hidden: bfloat16 [4, 2, 16, 522, 256], P(None, 'item', 'seg'), may hold values from -6 to 6
- write_cotangent: bfloat16 [4, 2, 16, 10, 256], P(None, 'item', 'seg'), may hold values from -6 to 6
- targets: bfloat16 [4, 2, 16, 80, 256], P(None, 'item', 'seg'), may hold values from -6 to 6
- positions: int32 [4, 2, 16, 80], P(None, 'item', 'seg'), may hold values from 0 to 501, as said below
- counts: int32 [4, 2, 16], P(None, 'item', 'seg'), may hold values from 40 to 80, as said below
- w_query: bfloat16 [2, 256, 256], replicated, may hold values from -0.375 to 0.375
- b_query: float32 [2, 256], replicated, may hold values from -3 to 3
- w_key: bfloat16 [2, 256, 256], replicated, may hold values from -0.375 to 0.375
- w_value: bfloat16 [2, 256, 256], replicated, may hold values from -0.375 to 0.375
- b_value: float32 [2, 256], replicated, may hold values from -3 to 3
- w_out: bfloat16 [2, 256, 256], replicated, may hold values from -6 to 6
- b_out: float32 [2, 256], replicated, may hold values from -3 to 3
- gain_attn: float32 [2, 256], replicated, may hold values from 0.5 to 1.5
- shift_attn: float32 [2, 256], replicated, may hold values from -2 to 2
- w_up: bfloat16 [2, 256, 1024], replicated, may hold values from -0.375 to 0.375
- b_up: float32 [2, 1024], replicated, may hold values from -3 to 3
- w_down: bfloat16 [2, 1024, 256], replicated, may hold values from -0.1875 to 0.1875
- b_down: float32 [2, 256], replicated, may hold values from -3 to 3
- gain_ffn: float32 [2, 256], replicated, may hold values from 0.5 to 1.5
- shift_ffn: float32 [2, 256], replicated, may hold values from -2 to 2
Outputs:
- output: bfloat16 [4, 2, 16, 522, 256], P(None, 'item', 'seg')
- hidden_grad: bfloat16 [4, 2, 16, 522, 256], P(None, 'item', 'seg')
- grad_w_query: float32 [2, 256, 256], replicated
- grad_b_query: float32 [2, 256], replicated
- grad_w_key: float32 [2, 256, 256], replicated
- grad_w_value: float32 [2, 256, 256], replicated
- grad_b_value: float32 [2, 256], replicated
- grad_w_out: float32 [2, 256, 256], replicated
- grad_b_out: float32 [2, 256], replicated
- grad_gain_attn: float32 [2, 256], replicated
- grad_shift_attn: float32 [2, 256], replicated
- grad_w_up: float32 [2, 256, 1024], replicated
- grad_b_up: float32 [2, 1024], replicated
- grad_w_down: float32 [2, 1024, 256], replicated
- grad_b_down: float32 [2, 256], replicated
- grad_gain_ffn: float32 [2, 256], replicated
- grad_shift_ffn: float32 [2, 256], replicated
Inputs may be any that keep to these rules, and one draw needn't show every extreme that they name: Within one segment the 80 positions are distinct; slots at or after the segment's count are unused. `counts`: some segment uses all 80 slots.
All inputs are finite; a program needn't handle non-finite values.
Results may differ from a plain program's by a relative error of at most 0.018.
The roundings to bfloat16 on the way count: a program that leaves them out, or rounds other values in their place, can miss the bound.
Values may be sent and summed in bfloat16 or wider, within the bound.
No kernel may reach another device: no remote copies, remote signals or barrier semaphores. Data moves between devices by JAX's collectives and lax.ppermute only.
A program may use at most 128 MiB of HBM per device.

v0:
```python
import functools

import jax
import jax.numpy as jnp
from jax import lax
from jax.experimental import pallas as pl
from jax.experimental.pallas import tpu as pltpu
from jax.sharding import PartitionSpec as P

EPSILON = 1e-12
DENSITY = 0.3989422804014327
HEADS = 4
TILE = 16
LOW = -1e30
F32, BF16 = jnp.float32, jnp.bfloat16
WEIGHTS = (
    "w_query", "b_query", "w_key", "w_value", "b_value", "w_out", "b_out", "gain_attn",
    "shift_attn", "w_up", "b_up", "w_down", "b_down", "gain_ffn", "shift_ffn",
)
VECTORS = ("b_query", "b_value", "b_out", "gain_attn", "shift_attn", "b_down", "gain_ffn", "shift_ffn")
STASH = ("query", "key", "value", "prob", "prob_rest", "context_t", "context", "inverse", "normed_attn",
         "middle", "active", "slope", "normed_ffn")


def dot(a, b):
    return jnp.dot(a, b, preferred_element_type=F32)


def dot_nt(a, b):
    return lax.dot_general(a, b, (((1,), (1,)), ((), ())), preferred_element_type=F32)


def dot_tn(a, b):
    return lax.dot_general(a, b, (((0,), (0,)), ((), ())), preferred_element_type=F32)


def mean(v):
    return jnp.mean(v, axis=-1, keepdims=True)


def column_sum(v):
    return jnp.sum(v.astype(F32), axis=0, keepdims=True)


def normalize(v):
    centred = v - mean(v)
    inverse = lax.rsqrt(mean(centred * centred) + EPSILON)
    return centred * inverse, inverse


def norm_back(grad, normed, inverse):
    return inverse * (grad - mean(grad) - normed * mean(grad * normed))


def gelu_and_slope(u):
    bell = jnp.exp(u * u * -0.5)
    t = 1.0 / (1.0 + 0.23164188826 * jnp.abs(u))
    tail = t * (0.127414796 + t * (-0.142248368 + t * (0.7107068705 + t * (-0.7265760135 + t * 0.5307027145))))
    tail = tail * bell
    phi = jnp.where(u < 0.0, tail, 1.0 - tail)
    return u * phi, phi + u * bell * DENSITY


def spread_heads(rest, width):
    tiled = jnp.concatenate([rest] * HEADS, axis=0)
    return jnp.where(head_block(tiled.shape, width), tiled, jnp.zeros_like(tiled))


def head_block(shape, width):
    rows = lax.broadcasted_iota(jnp.int32, shape, 0) // TILE
    lanes = lax.broadcasted_iota(jnp.int32, shape, 1) // width
    return rows == lanes


def fold_heads(spread, width):
    own = jnp.where(head_block(spread.shape, width), spread, 0.0)
    return own[:TILE] + own[TILE : 2 * TILE] + own[2 * TILE : 3 * TILE] + own[3 * TILE :]


def own_half(pair, h, width):
    lanes = lax.broadcasted_iota(jnp.int32, pair.shape, 1) // width
    return jnp.where(lanes == h % 2, pair, jnp.zeros_like(pair))


def layer_forward(x, layer, w, st, rows):
    full, features = x.shape
    main = full - TILE
    width = features // HEADS
    row = lambda name: w[name][layer : layer + 1, :]
    q = ((dot(x, w["w_query"][0]) + row("b_query")) * 0.125).astype(BF16)
    k = dot(x, w["w_key"][0]).astype(BF16)
    v = (dot(x, w["w_value"][0]) + row("b_value")).astype(BF16)
    st["query"][...] = q
    st["key"][...] = k
    st["value"][...] = v
    q_t = q[:main].T
    v_t = v[:main].T
    live_rest = lax.broadcasted_iota(jnp.int32, (TILE, 1), 0) < rows - main
    s = dot_nt(k, spread_heads(q[main:], width))
    top, bottom = s[:main], jnp.where(live_rest, s[main:], LOW)
    peak = jnp.maximum(jnp.max(top, axis=0, keepdims=True), jnp.max(bottom, axis=0, keepdims=True))
    top, bottom = jnp.exp(top - peak), jnp.exp(bottom - peak)
    scale = 1.0 / (jnp.sum(top, axis=0, keepdims=True) + jnp.sum(bottom, axis=0, keepdims=True))
    p_rest = jnp.concatenate([(top * scale).astype(BF16), (bottom * scale).astype(BF16)], axis=0)
    st["prob_rest"][...] = p_rest
    context_rest = fold_heads(dot_tn(p_rest, v), width).astype(BF16)
    parts, bottoms = [], []
    for h in range(HEADS):
        pair = slice(2 * width * (h // 2), 2 * width * (h // 2 + 1))
        s = dot(own_half(k[:, pair], h, width), q_t[pair, :])
        top, bottom = s[:main], jnp.where(live_rest, s[main:], LOW)
        peak = jnp.maximum(jnp.max(top, axis=0, keepdims=True), jnp.max(bottom, axis=0, keepdims=True))
        top, bottom = jnp.exp(top - peak), jnp.exp(bottom - peak)
        scale = 1.0 / (jnp.sum(top, axis=0, keepdims=True) + jnp.sum(bottom, axis=0, keepdims=True))
        top, bottom = (top * scale).astype(BF16), (bottom * scale).astype(BF16)
        st["prob"][h, :main, :] = top
        st["prob"][h, main:, :] = bottom
        bottoms.append(bottom)
        parts.append(dot(v_t[h * width : (h + 1) * width, :], top))
    context_t = jnp.concatenate(parts, axis=0)
    context_t = context_t + dot_tn(spread_heads(v[main:], width), jnp.concatenate(bottoms, axis=0))
    context_t = context_t.astype(BF16)
    st["context_t"][...] = context_t
    context = jnp.concatenate([context_t.T, context_rest], axis=0)
    st["context"][...] = context
    normed_attn, inverse_attn = normalize(x.astype(F32) + dot(context, w["w_out"][0]) + row("b_out"))
    st["normed_attn"][...] = normed_attn
    middle = normed_attn * row("gain_attn") + row("shift_attn")
    middle_low = middle.astype(BF16)
    st["middle"][...] = middle_low
    total = middle + row("b_down")
    hidden_units = w["w_up"].shape[2]
    for c in range(hidden_units // features):
        part = slice(c * features, (c + 1) * features)
        u = dot(middle_low, w["w_up"][0, :, part]) + w["b_up"][layer : layer + 1, part]
        active, slope = gelu_and_slope(u)
        active = active.astype(BF16)
        st["active"][:, part] = active
        st["slope"][:, part] = slope.astype(BF16)
        total = total + dot(active, w["w_down"][0, part, :])
    normed_ffn, inverse_ffn = normalize(total)
    st["normed_ffn"][...] = normed_ffn
    st["inverse"][:, 0:1] = inverse_attn
    st["inverse"][:, 1:2] = inverse_ffn
    return normed_ffn * row("gain_ffn") + row("shift_ffn")


def layer_backward(x, grad_out, layer, w, st, g, rest, step, steps):
    full, features = x.shape
    main = full - TILE
    width = features // HEADS
    row = lambda name: w[name][layer : layer + 1, :]
    place = pl.ds(pl.multiple_of(step * TILE, TILE), TILE)

    def add(name, value):
        g[name][...] += value

    normed_ffn = st["normed_ffn"][...]
    add("gain_ffn", column_sum(grad_out * normed_ffn))
    add("shift_ffn", column_sum(grad_out))
    grad_sum = norm_back(grad_out * row("gain_ffn"), normed_ffn, st["inverse"][:, 1:2])
    grad_branch = grad_sum.astype(BF16)
    rest["branch"][place, :] = grad_branch[main:]
    add("b_down", column_sum(grad_branch))
    grad_middle = grad_sum
    middle = st["middle"][...]
    rest["middle"][place, :] = middle[main:]
    hidden_units = w["w_up"].shape[2]
    for c in range(hidden_units // features):
        part = slice(c * features, (c + 1) * features)
        grad_up = dot_nt(grad_branch, w["w_down"][0, part, :]) * st["slope"][:, part].astype(F32)
        grad_up = grad_up.astype(BF16)
        active = st["active"][:, part]
        rest["up"][place, part] = grad_up[main:]
        rest["active"][place, part] = active[main:]
        g["b_up"][:, part] += column_sum(grad_up)
        g["w_down"][part, :] += dot_tn(active[:main], grad_branch[:main])
        g["w_up"][:, part] += dot_tn(middle[:main], grad_up[:main])
        grad_middle = grad_middle + dot_nt(grad_up, w["w_up"][0, :, part])
    normed_attn = st["normed_attn"][...]
    add("gain_attn", column_sum(grad_middle * normed_attn))
    add("shift_attn", column_sum(grad_middle))
    grad_resid = norm_back(grad_middle * row("gain_attn"), normed_attn, st["inverse"][:, 0:1])
    grad_attn = grad_resid.astype(BF16)
    rest["attn"][place, :] = grad_attn[main:]
    rest["context"][place, :] = st["context"][main:, :]
    add("b_out", column_sum(grad_attn))
    context_t = st["context_t"][...]
    add("w_out", dot(context_t, grad_attn[:main]))
    grad_context = dot_nt(grad_attn, w["w_out"][0]).astype(BF16)
    grad_context_t = grad_context[:main].T
    product = grad_context_t.astype(F32) * context_t.astype(F32)
    q, k, v = st["query"][...], st["key"][...], st["value"][...]
    k_t = k[:main].T
    grad_spread = spread_heads(grad_context[main:], width)
    p_rest = st["prob_rest"][...]
    p_rest_wide = p_rest.astype(F32)
    grad_p = dot_nt(v, grad_spread)
    grad_s = p_rest_wide * (grad_p - jnp.sum(p_rest_wide * grad_p, axis=0, keepdims=True))
    grad_s = grad_s.astype(BF16)
    grad_v = dot(p_rest, grad_spread)
    grad_k = dot(grad_s, spread_heads(q[main:], width))
    grad_q_rest = fold_heads(dot_tn(grad_s, k), width).astype(BF16)
    q_parts, k_parts, v_parts, bottoms = [], [], [], []
    for h in range(HEADS):
        pair = slice(2 * width * (h // 2), 2 * width * (h // 2 + 1))
        own = slice(h * width, (h + 1) * width)
        p = st["prob"][h]
        grad_p = dot(own_half(v[:, pair], h, width), grad_context_t[pair, :])
        grad_s = p.astype(F32) * (grad_p - jnp.sum(product[own, :], axis=0, keepdims=True))
        grad_s = grad_s.astype(BF16)
        v_parts.append(dot(p, grad_context[:main, pair]))
        k_parts.append(dot(grad_s, q[:main, pair]))
        q_parts.append(dot(k_t[own, :], grad_s[:main]))
        bottoms.append(grad_s[main:])
    left = lax.broadcasted_iota(jnp.int32, (full, 2 * width), 1) < width

    def join(parts):
        return jnp.concatenate(
            [jnp.where(left, parts[i], parts[i + 1]) for i in range(0, HEADS, 2)], axis=1
        )

    grad_v = (grad_v + join(v_parts)).astype(BF16)
    grad_k = (grad_k + join(k_parts)).astype(BF16)
    grad_q_t = jnp.concatenate(q_parts, axis=0)
    grad_q_t = grad_q_t + dot_tn(spread_heads(k[main:], width), jnp.concatenate(bottoms, axis=0))
    grad_q = jnp.concatenate([grad_q_t.astype(BF16).T, grad_q_rest], axis=0) * BF16(0.125)
    rest["input"][place, :] = x[main:]
    rest["query"][place, :] = grad_q[main:]
    rest["key"][place, :] = grad_k[main:]
    rest["value"][place, :] = grad_v[main:]
    add("b_query", column_sum(grad_q))
    add("b_value", column_sum(grad_v))
    x_main = x[:main]
    add("w_query", dot_tn(x_main, grad_q[:main]))
    add("w_key", dot_tn(x_main, grad_k[:main]))
    add("w_value", dot_tn(x_main, grad_v[:main]))

    @pl.when(step == steps - 1)
    def _():
        add("w_query", dot_tn(rest["input"][...], rest["query"][...]))
        add("w_key", dot_tn(rest["input"][...], rest["key"][...]))
        add("w_value", dot_tn(rest["input"][...], rest["value"][...]))
        add("w_out", dot_tn(rest["context"][...], rest["attn"][...]))
        add("w_up", dot_tn(rest["middle"][...], rest["up"][...]))
        add("w_down", dot_tn(rest["active"][...], rest["branch"][...]))

    return (
        grad_resid
        + dot_nt(grad_q, w["w_query"][0])
        + dot_nt(grad_k, w["w_key"][0])
        + dot_nt(grad_v, w["w_value"][0])
    )


def packed_rows(features, hidden_units):
    used = 4 * features + 2 * hidden_units + len(VECTORS) + hidden_units // features
    return -(-used // 64) * 64


def emit(g, packed, features, hidden_units):
    at = 0
    for name in ("w_query", "w_key", "w_value", "w_out"):
        packed[at : at + features, :] = g[name][...].astype(BF16)
        at += features
    for c in range(hidden_units // features):
        packed[at : at + features, :] = g["w_up"][:, c * features : (c + 1) * features].astype(BF16)
        at += features
    packed[at : at + hidden_units, :] = g["w_down"][...].astype(BF16)
    at += hidden_units
    lines = [g[name][...] for name in VECTORS]
    lines += [g["b_up"][:, c * features : (c + 1) * features] for c in range(hidden_units // features)]
    lines.append(jnp.zeros((packed.shape[0] - at - len(lines), features), F32))
    packed[at:, :] = jnp.concatenate(lines, axis=0).astype(BF16)


def unpack(packed, features, hidden_units):
    out, at = {}, 0
    wide = packed.astype(F32)
    for name in ("w_query", "w_key", "w_value", "w_out"):
        out[name] = wide[:, at : at + features]
        at += features
    chunks = hidden_units // features
    out["w_up"] = jnp.concatenate(
        [wide[:, at + c * features : at + (c + 1) * features] for c in range(chunks)], axis=-1
    )
    at += hidden_units
    out["w_down"] = wide[:, at : at + hidden_units]
    at += hidden_units
    for name in VECTORS:
        out[name] = wide[:, at]
        at += 1
    out["b_up"] = wide[:, at : at + chunks].reshape(wide.shape[0], hidden_units)
    return out


def stash_shapes(full, features, hidden_units):
    main = full - TILE
    square = ((full, features), BF16)
    return {
        "query": square,
        "key": square,
        "value": square,
        "prob": ((HEADS, full, main), BF16),
        "prob_rest": ((full, HEADS * TILE), BF16),
        "context_t": ((features, main), BF16),
        "context": square,
        "inverse": ((full, 2), F32),
        "normed_attn": ((full, features), F32),
        "middle": square,
        "active": ((full, hidden_units), BF16),
        "slope": ((full, hidden_units), BF16),
        "normed_ffn": ((full, features), F32),
    }


def grad_shapes(features, hidden_units):
    sizes = {name: (features, features) for name in ("w_query", "w_key", "w_value", "w_out")}
    sizes.update({name: (1, features) for name in VECTORS})
    sizes.update(w_up=(features, hidden_units), w_down=(hidden_units, features), b_up=(1, hidden_units))
    return sizes


def rest_shapes(steps, features, hidden_units):
    sizes = {name: features for name in ("input", "query", "key", "value", "context", "attn", "middle", "branch")}
    sizes.update(up=hidden_units, active=hidden_units)
    return {name: (steps * TILE, size) for name, size in sizes.items()}


def weight_specs(weights, layer):
    specs = []
    for name in WEIGHTS:
        shape = weights[name].shape
        if len(shape) == 3:
            specs.append(pl.BlockSpec((1,) + shape[1:], lambda m: (layer, 0, 0)))
        else:
            specs.append(pl.BlockSpec(shape, lambda m: (0, 0)))
    return specs


def by_micro(shape):
    rank = len(shape)
    return pl.BlockSpec((1,) + tuple(shape[1:]), lambda m: (m,) + (0,) * (rank - 1))


def fixed(shape):
    rank = len(shape)
    return pl.BlockSpec(tuple(shape), lambda m: (0,) * rank)


PARAMS = pltpu.CompilerParams(vmem_limit_bytes=60 * 2**20, dimension_semantics=("arbitrary",))


def lower_forward_kernel(rows, x_ref, *refs):
    w = dict(zip(WEIGHTS, refs[: len(WEIGHTS)]))
    out_ref, *stash = refs[len(WEIGHTS) :]
    st = {name: ref.at[0] for name, ref in zip(STASH, stash)}
    out_ref[0] = layer_forward(x_ref[0], 0, w, st, rows).astype(BF16)


def lower_forward(x, weights, rows):
    micro, full, features = x.shape
    shapes = stash_shapes(full, features, weights["w_up"].shape[2])
    outs = [jax.ShapeDtypeStruct(x.shape, BF16)]
    outs += [jax.ShapeDtypeStruct((micro,) + shapes[name][0], shapes[name][1]) for name in STASH]
    return pl.pallas_call(
        functools.partial(lower_forward_kernel, rows),
        grid=(micro,),
        in_specs=[by_micro(x.shape)] + weight_specs(weights, 0),
        out_specs=[by_micro(o.shape) for o in outs],
        out_shape=outs,
        compiler_params=PARAMS,
        name="lower_forward",
    )(x, *[weights[name] for name in WEIGHTS])


def zero_all(g):
    for ref in g.values():
        ref[...] = jnp.zeros_like(ref)


def upper_kernel(rows, memory, lead_ref, count_ref, x_ref, arrived_ref, cot_ref, target_ref, place_ref, *refs):
    step, steps = pl.program_id(0), pl.num_programs(0)
    w = dict(zip(WEIGHTS, refs[: len(WEIGHTS)]))
    refs = refs[len(WEIGHTS) :]
    out_ref, grad_ref, back_ref, packed_ref = refs[:4]
    refs = refs[4:]
    st = dict(zip(STASH, refs[: len(STASH)]))
    refs = refs[len(STASH) :]
    full, features = x_ref.shape[1:]
    hidden_units = w["w_up"].shape[2]
    main = full - TILE
    names = list(grad_shapes(features, hidden_units))
    g = dict(zip(names, refs[: len(names)]))
    rest = dict(zip(rest_shapes(1, 1, 1), refs[len(names) :]))

    @pl.when(step == 0)
    def _():
        zero_all(g)

    lead = lead_ref[0] != 0
    x = x_ref[0]
    is_read = lax.broadcasted_iota(jnp.int32, (TILE, features), 0) < memory
    head_rows = jnp.where(jnp.logical_and(is_read, jnp.logical_not(lead)), arrived_ref[0], x[:TILE])
    x = jnp.concatenate([head_rows, x[TILE:]], axis=0)
    y = layer_forward(x, 1, w, st, rows)
    out_ref[0] = y.astype(BF16)
    count = count_ref[step]
    slots = place_ref.shape[2]
    slot_row = lax.broadcasted_iota(jnp.int32, (main, slots), 0) - memory
    slot_at = lax.broadcasted_iota(jnp.int32, (main, slots), 1)
    hit = jnp.logical_and(slot_row == place_ref[0], slot_at < count)
    hit = jnp.where(hit, 1.0, 0.0).astype(BF16)
    used = dot(hit, jnp.ones((slots, features), BF16))
    wanted = dot(hit, target_ref[0])
    grad_main = (y[:main] * used - wanted) / count.astype(F32)
    grad_out = jnp.concatenate([grad_main, cot_ref[0].astype(F32)], axis=0)
    grad_in = layer_backward(x, grad_out, 1, w, st, g, rest, step, steps)
    back_ref[0] = grad_in[:TILE].astype(BF16)
    drop = jnp.logical_and(is_read, jnp.logical_not(lead))
    grad_ref[0, :TILE, :] = jnp.where(drop, 0.0, grad_in[:TILE])
    grad_ref[0, TILE:, :] = grad_in[TILE:]

    @pl.when(step == steps - 1)
    def _():
        emit(g, packed_ref, features, hidden_units)


def smem():
    return pl.BlockSpec(memory_space=pltpu.SMEM)


def scratches(micro, features, hidden_units):
    out = [pltpu.VMEM(size, F32) for size in grad_shapes(features, hidden_units).values()]
    return out + [pltpu.VMEM(size, BF16) for size in rest_shapes(micro, features, hidden_units).values()]


def upper_both(lead, counts, x, arrived, cotangent, targets, places, weights, rows, memory):
    micro, full, features = x.shape
    hidden_units = weights["w_up"].shape[2]
    shapes = stash_shapes(full, features, hidden_units)
    outs = [
        jax.ShapeDtypeStruct(x.shape, BF16),
        jax.ShapeDtypeStruct(x.shape, F32),
        jax.ShapeDtypeStruct((micro, TILE, features), BF16),
        jax.ShapeDtypeStruct((packed_rows(features, hidden_units), features), BF16),
    ]
    ins = (x, arrived, cotangent, targets, places)
    return pl.pallas_call(
        functools.partial(upper_kernel, rows, memory),
        grid=(micro,),
        in_specs=[smem(), smem()] + [by_micro(a.shape) for a in ins] + weight_specs(weights, 1),
        out_specs=[by_micro(o.shape) for o in outs[:3]] + [fixed(outs[3].shape)],
        out_shape=outs,
        scratch_shapes=[pltpu.VMEM(*shapes[name]) for name in STASH] + scratches(micro, features, hidden_units),
        compiler_params=PARAMS,
        name="upper_both",
    )(lead, counts, *ins, *[weights[name] for name in WEIGHTS])


def lower_backward_kernel(memory, x_ref, grad_ref, back_ref, *refs):
    step, steps = pl.program_id(0), pl.num_programs(0)
    w = dict(zip(WEIGHTS, refs[: len(WEIGHTS)]))
    refs = refs[len(WEIGHTS) :]
    st = {name: ref.at[0] for name, ref in zip(STASH, refs)}
    refs = refs[len(STASH) :]
    out_ref, packed_ref = refs[:2]
    refs = refs[2:]
    full, features = x_ref.shape[1:]
    hidden_units = w["w_up"].shape[2]
    main = full - TILE
    names = list(grad_shapes(features, hidden_units))
    g = dict(zip(names, refs[: len(names)]))
    rest = dict(zip(rest_shapes(1, 1, 1), refs[len(names) :]))

    @pl.when(step == 0)
    def _():
        zero_all(g)

    is_write = lax.broadcasted_iota(jnp.int32, (TILE, features), 0) < memory
    returned = jnp.where(is_write, back_ref[0].astype(F32), 0.0)
    grad_out = jnp.concatenate([grad_ref[0, :main, :], grad_ref[0, main:, :] + returned], axis=0)
    grad_in = layer_backward(x_ref[0], grad_out, 0, w, st, g, rest, step, steps)
    out_ref[0] = grad_in.astype(BF16)

    @pl.when(step == steps - 1)
    def _():
        emit(g, packed_ref, features, hidden_units)


def lower_backward(x, grad, back, weights, stash, memory):
    micro, full, features = x.shape
    hidden_units = weights["w_up"].shape[2]
    outs = [
        jax.ShapeDtypeStruct(x.shape, BF16),
        jax.ShapeDtypeStruct((packed_rows(features, hidden_units), features), BF16),
    ]
    ins = (x, grad, back)
    return pl.pallas_call(
        functools.partial(lower_backward_kernel, memory),
        grid=(micro,),
        in_specs=[by_micro(a.shape) for a in ins]
        + weight_specs(weights, 0)
        + [by_micro(a.shape) for a in stash],
        out_specs=[by_micro(outs[0].shape), fixed(outs[1].shape)],
        out_shape=outs,
        scratch_shapes=scratches(micro, features, hidden_units),
        compiler_params=PARAMS,
        name="lower_backward",
    )(*ins, *[weights[name] for name in WEIGHTS], *stash)


def from_behind(value, axis, steps):
    count = lax.axis_size(axis)
    initial, last = (max(0, -steps), min(count, count - steps))
    return lax.ppermute(value, axis, [(source, source + steps) for source in range(initial, last)])


def sum_all(value, axes):
    order = []
    for axis in axes:
        step = 1
        while step < lax.axis_size(axis):
            order.append((axis, step))
            step *= 2
    kept, halved = value, []
    for axis, step in order:
        swap = [(i, i ^ step) for i in range(lax.axis_size(axis))]
        half = kept.shape[0] // 2
        if half % (TILE // 2):
            kept = (kept.astype(F32) + lax.ppermute(kept, axis, swap).astype(F32)).astype(BF16)
            continue
        halved.append((axis, step))
        upper = (lax.axis_index(axis) // step) % 2
        low, high = kept[:half], kept[half:]
        got = lax.ppermute(jnp.where(upper == 0, high, low), axis, swap)
        own = jnp.where(upper == 0, low, high)
        kept = (own.astype(F32) + got.astype(F32)).astype(BF16)
    for axis, step in reversed(halved):
        upper = (lax.axis_index(axis) // step) % 2
        swap = [(i, i ^ step) for i in range(lax.axis_size(axis))]
        got = lax.ppermute(kept, axis, swap)
        kept = jnp.where(upper == 0, jnp.concatenate([kept, got]), jnp.concatenate([got, kept]))
    return kept


def local(hidden, write_cotangent, targets, positions, counts, *weights):
    weights = dict(zip(WEIGHTS, weights))
    micro, _, _, rows, features = hidden.shape
    memory = write_cotangent.shape[3]
    hidden_units = weights["w_up"].shape[2]
    full = -(-rows // TILE) * TILE
    lead = (lax.axis_index("seg") == 0).astype(jnp.int32).reshape(1)
    x = jnp.pad(hidden.reshape(micro, rows, features), ((0, 0), (0, full - rows), (0, 0)))
    cotangent = write_cotangent.reshape(micro, memory, features)
    cotangent = jnp.pad(cotangent, ((0, 0), (0, TILE - memory), (0, 0)))
    target = targets.reshape(micro, targets.shape[3], features)
    places = positions.reshape(micro, 1, positions.shape[3])

    lower_out, *stash = lower_forward(x, weights, rows)
    arrived = from_behind(lower_out[:, full - TILE :], "seg", 1)
    out, grad, back, upper_packed = upper_both(
        lead, counts.reshape(micro), lower_out, arrived, cotangent, target, places, weights, rows, memory
    )
    returned = from_behind(back, "seg", -1)
    grad_in, lower_packed = lower_backward(x, grad, returned, weights, stash, memory)
    packed = jnp.concatenate([lower_packed, upper_packed], axis=0)
    packed = sum_all(packed, ("seg", "item"))
    grads = unpack(packed.reshape(2, -1, features), features, hidden_units)
    output = out[:, :rows].reshape(hidden.shape)
    hidden_grad = grad_in[:, :rows].reshape(hidden.shape)
    return (output, hidden_grad) + tuple(grads[name] for name in WEIGHTS)


def solution(mesh):
    split = P(None, "item", "seg", None, None)
    placed = (split, split, split, P(None, "item", "seg", None), P(None, "item", "seg"))
    return jax.shard_map(
        local,
        mesh=mesh,
        in_specs=placed + (P(),) * len(WEIGHTS),
        out_specs=(split, split) + (P(),) * len(WEIGHTS),
        check_vma=False,
    )
```

profile of v0, /device:TPU:0, one launch (start us, length us, event | category | flops | bytes accessed | tf_op | source)
XLA Modules:
  0.0 233.9 jit_solution(917460627644600282)
XLA Ops:
  0.7 1.4 copy.63
  2.0 1.0 pad.8.x_ref
  3.1 27.6 %lower_forward.1 = (bf16[4,528,256]{2,1,0:T(8,128)(2,1)}, bf16[4,528,256]{2,1,0:T(8,128)(2,1)}, bf16[4,528,256]{2,1,0:T(8,128)(2,1)}, bf16[4,528,256]{2,1,0:T(8,...) custom-call(bf16[4,528,256]{2,1,0:T(8,128)(2,1)} %pad.8.x_ref, ...), custom_call_target="tpu_custom_call" | custom-call | tf_op jit(solution)/shard_map/lower_forward/pallas_call | solution.py:366
  30.7 0.8 slice.81
  31.4 2.5 %collective-permute-start = (bf16[4,16,256]{2,1,0:T(8,128)(2,1)S(1)}, bf16[4,16,256]{2,1,0:T(8,128)(2,1)S(1)}, u32[]{:S(2)}, u32[]{:S(2)}) collective-permute-start(bf16[4,16,256]{2,1,0:T(8,128)(2,1)S(1)} %slice.81), channel_id=1, source_target_pairs={{0,2},{2,4},{4,6},{6,8},{8,10},{10,12},{12,14},{14,16},{16,18},{18... | collective-permute-start | bytes 98312 | tf_op jit(solution)/shard_map/ppermute | solution.py:516
  34.0 0.6 pad.9.cot_ref
  34.6 0.6 copy-done.3
  35.2 51.7 %upper_both.1 = (bf16[4,528,256]{2,1,0:T(8,128)(2,1)}, f32[4,528,256]{2,1,0:T(8,128)}, bf16[4,16,256]{2,1,0:T(8,128)(2,1)}, bf16[3136,256]{1,0:T(8,128)(2,1)}) custom-call(s32[1]{0:T(128)} %bitcast.lead_ref, s32[4]{0:T(128)} %bitcast.44, bf16[4,528,256]{2,1,0:T(8,128)(2,1)} %get-tuple-element.37.x_ref, bf16[4,16,256]{2,1,0:T(8,128)(2,1)} %copy-done.3, ...), custom_call_target="tpu_custom_call" | custom-call | tf_op jit(solution)/shard_map/upper_both/pallas_call | solution.py:449
  87.0 1.5 collective-permute-start.1
  88.5 4.1 %collective-permute-done.1.back_ref = bf16[4,16,256]{2,1,0:T(8,128)(2,1)S(1)} collective-permute-done((bf16[4,16,256]{2,1,0:T(8,128)(2,1)}, bf16[4,16,256]{2,1,0:T(8,128)(2,1)S(1)}, u32[]{:S(2)}, u32[]{:S(2)}) %collective-permute-start.1) | collective-permute-done | bytes 32800 | tf_op jit(solution)/shard_map/ppermute | solution.py:516
  93.2 29.9 %lower_backward.1 = (bf16[4,528,256]{2,1,0:T(8,128)(2,1)}, bf16[3136,256]{1,0:T(8,128)(2,1)}) custom-call(bf16[4,528,256]{2,1,0:T(8,128)(2,1)} %pad.8.x_ref, f32[4,528,256]{2,1,0:T(8,128)} %get-tuple-element.39.grad_ref, bf16[4,16,256]{2,1,0:T(8,128)(2,1)} %copy-done.4, bf16[2,256,256]{2,1,0:T(8,128)(2,1)} %refs_0_.5, f32[2,256]{1,0:T(2,128)} %refs_1_.5, ...), custom_call_target="tpu_custom_call" | custom-call | tf_op jit(solution)/shard_map/lower_backward/pallas_call | solution.py:499
  123.3 4.7 %collective-permute-start.2 = (bf16[3136,256]{1,0:T(8,128)(2,1)S(1)}, bf16[3136,256]{1,0:T(8,128)(2,1)}, u32[]{:S(2)}, u32[]{:S(2)}) collective-permute-start(bf16[3136,256]{1,0:T(8,128)(2,1)S(1)} %broadcast_select_fusion), channel_id=1, source_target_pairs={{0,2},{2,0},{4,6},{6,4},{8,10},{10,8},{12,14},{14,12},{16,18},{18,... | collective-permute-start | bytes 4816904 | tf_op jit(solution)/shard_map/ppermute | solution.py:536
  128.0 3.2 %collective-permute-done.2 = bf16[3136,256]{1,0:T(8,128)(2,1)} collective-permute-done((bf16[3136,256]{1,0:T(8,128)(2,1)S(1)}, bf16[3136,256]{1,0:T(8,128)(2,1)}, u32[]{:S(2)}, u32[]{:S(2)}) %collective-permute-start.2) | collective-permute-done | bytes 1605664 | tf_op jit(solution)/shard_map/ppermute | solution.py:536
  131.2 2.5 %add_convert_fusion = bf16[3136,256]{1,0:T(8,128)(2,1)S(1)} fusion(bf16[3136,256]{1,0:T(8,128)(2,1)} %collective-permute-done.2, bf16[3136,256]{1,0:T(8,128)(2,1)} %get-tuple-element.55, bf16[3136,256]{1,0:T(8,128)(2,1)S(1)} %copy-done, pred[]{:T(512)S(6)} %eq.33), kind=kLoop, calls=%fused_computation.1 | loop fusion | flops 4014080 | bytes 6422529 | tf_op jit(solution)/shard_map/convert_element_type | solution.py:538
  133.8 2.5 %collective-permute-start.3 = (bf16[1568,256]{1,0:T(8,128)(2,1)S(1)}, bf16[1568,256]{1,0:T(8,128)(2,1)S(1)}, u32[]{:S(2)}, u32[]{:S(2)}) collective-permute-start(bf16[1568,256]{1,0:T(8,128)(2,1)S(1)} %broadcast_select_fusion.1), channel_id=1, source_target_pairs={{0,4},{2,6},{4,0},{6,2},{8,12},{10,14},{12,8},{14,10},{16,20},{18,... | collective-permute-start | bytes 2408456 | tf_op jit(solution)/shard_map/ppermute | solution.py:536
  136.3 17.9 %collective-permute-done.3 = bf16[1568,256]{1,0:T(8,128)(2,1)S(1)} collective-permute-done((bf16[1568,256]{1,0:T(8,128)(2,1)S(1)}, bf16[1568,256]{1,0:T(8,128)(2,1)S(1)}, u32[]{:S(2)}, u32[]{:S(2)}) %collective-permute-start.3) | collective-permute-done | bytes 802848 | tf_op jit(solution)/shard_map/ppermute | solution.py:536
  154.6 1.6 collective-permute-start.4
  156.2 9.0 %collective-permute-done.4 = bf16[784,256]{1,0:T(8,128)(2,1)S(1)} collective-permute-done((bf16[784,256]{1,0:T(8,128)(2,1)S(1)}, bf16[784,256]{1,0:T(8,128)(2,1)S(1)}, u32[]{:S(2)}, u32[]{:S(2)}) %collective-permute-start.4) | collective-permute-done | bytes 401440 | tf_op jit(solution)/shard_map/ppermute | solution.py:536
  165.4 2.6 %collective-permute-start.5 = (bf16[392,256]{1,0:T(8,128)(2,1)S(1)}, bf16[392,256]{1,0:T(8,128)(2,1)S(1)}, u32[]{:S(2)}, u32[]{:S(2)}) collective-permute-start(bf16[392,256]{1,0:T(8,128)(2,1)S(1)} %broadcast_select_fusion.3), channel_id=1, source_target_pairs={{0,16},{2,18},{4,20},{6,22},{8,24},{10,26},{12,28},{14,30},{16,0},... | collective-permute-start | bytes 602120 | tf_op jit(solution)/shard_map/ppermute | solution.py:536
  168.0 7.9 %collective-permute-done.5 = bf16[392,256]{1,0:T(8,128)(2,1)S(1)} collective-permute-done((bf16[392,256]{1,0:T(8,128)(2,1)S(1)}, bf16[392,256]{1,0:T(8,128)(2,1)S(1)}, u32[]{:S(2)}, u32[]{:S(2)}) %collective-permute-start.5) | collective-permute-done | bytes 200736 | tf_op jit(solution)/shard_map/ppermute | solution.py:536
  176.0 1.6 collective-permute-start.6
  177.6 4.3 %collective-permute-done.6 = bf16[392,256]{1,0:T(8,128)(2,1)S(1)} collective-permute-done((bf16[392,256]{1,0:T(8,128)(2,1)S(1)}, bf16[392,256]{1,0:T(8,128)(2,1)S(1)}, u32[]{:S(2)}, u32[]{:S(2)}) %collective-permute-start.6) | collective-permute-done | bytes 200736 | tf_op jit(solution)/shard_map/ppermute | solution.py:531
  182.1 9.2 %collective-permute-done.7 = bf16[392,256]{1,0:T(8,128)(2,1)S(1)} collective-permute-done((bf16[392,256]{1,0:T(8,128)(2,1)S(1)}, bf16[392,256]{1,0:T(8,128)(2,1)S(1)}, u32[]{:S(2)}, u32[]{:S(2)}) %collective-permute-start.7) | collective-permute-done | bytes 200736 | tf_op jit(solution)/shard_map/ppermute | solution.py:542
  191.5 10.2 %collective-permute-done.8 = bf16[784,256]{1,0:T(8,128)(2,1)S(1)} collective-permute-done((bf16[784,256]{1,0:T(8,128)(2,1)S(1)}, bf16[784,256]{1,0:T(8,128)(2,1)S(1)}, u32[]{:S(2)}, u32[]{:S(2)}) %collective-permute-start.8) | collective-permute-done | bytes 401440 | tf_op jit(solution)/shard_map/ppermute | solution.py:542
  202.0 2.5 %collective-permute-start.9 = (bf16[1568,256]{1,0:T(8,128)(2,1)S(1)}, bf16[1568,256]{1,0:T(8,128)(2,1)S(1)}, u32[]{:S(2)}, u32[]{:S(2)}) collective-permute-start(bf16[1568,256]{1,0:T(8,128)(2,1)S(1)} %maximum_select_fusion.2), channel_id=1, source_target_pairs={{0,4},{2,6},{4,0},{6,2},{8,12},{10,14},{12,8},{14,10},{16,20},{18,... | collective-permute-start | bytes 2408456 | tf_op jit(solution)/shard_map/ppermute | solution.py:542
  204.6 16.6 %collective-permute-done.9 = bf16[1568,256]{1,0:T(8,128)(2,1)S(1)} collective-permute-done((bf16[1568,256]{1,0:T(8,128)(2,1)S(1)}, bf16[1568,256]{1,0:T(8,128)(2,1)S(1)}, u32[]{:S(2)}, u32[]{:S(2)}) %collective-permute-start.9) | collective-permute-done | bytes 802848 | tf_op jit(solution)/shard_map/ppermute | solution.py:542
  221.7 1.5 copy.42
  223.3 1.5 copy.43
  225.1 0.9 maximum_select_fusion
  225.9 1.4 fusion.1
  227.9 1.5 slice.128
  232.3 1.6 pad_maximum_fusion
  (38 shorter events, 6.4 us)
Async XLA Ops:
  3.1 30.9 %copy-start.5 = (bf16[4,1,1,10,256]{4,0,3,2,1:T(4,128)(2,1)S(1)}, bf16[4,1,1,10,256]{4,0,3,2,1:T(4,128)(2,1)}, u32[]{:S(2)}) copy-start(bf16[4,1,1,10,256]{4,0,3,2,1:T(4,128)(2,1)} %param.21) | copy-start | bytes 61444
  31.4 3.2 %collective-permute-start = (bf16[4,16,256]{2,1,0:T(8,128)(2,1)S(1)}, bf16[4,16,256]{2,1,0:T(8,128)(2,1)S(1)}, u32[]{:S(2)}, u32[]{:S(2)}) collective-permute-start(bf16[4,16,256]{2,1,0:T(8,128)(2,1)S(1)} %slice.81), channel_id=1, source_target_pairs={{0,2},{2,4},{4,6},{6,8},{8,10},{10,12},{12,14},{14,16},{16,18},{18... | collective-permute-start | bytes 98312 | tf_op jit(solution)/shard_map/ppermute | solution.py:516
  34.6 0.6 copy-start.3
  87.0 5.6 %collective-permute-start.1 = (bf16[4,16,256]{2,1,0:T(8,128)(2,1)}, bf16[4,16,256]{2,1,0:T(8,128)(2,1)S(1)}, u32[]{:S(2)}, u32[]{:S(2)}) collective-permute-start(bf16[4,16,256]{2,1,0:T(8,128)(2,1)} %get-tuple-element.40), channel_id=1, source_target_pairs={{2,0},{4,2},{6,4},{8,6},{10,8},{12,10},{14,12},{16,14},{18,16},{20... | collective-permute-start | bytes 98312 | tf_op jit(solution)/shard_map/ppermute | solution.py:516
  92.6 0.6 copy-start.4
  93.2 29.9 %copy-start = (bf16[3136,256]{1,0:T(8,128)(2,1)S(1)}, bf16[3136,256]{1,0:T(8,128)(2,1)}, u32[]{:S(2)}) copy-start(bf16[3136,256]{1,0:T(8,128)(2,1)} %get-tuple-element.56) | copy-start | bytes 4816900
  123.3 7.9 %collective-permute-start.2 = (bf16[3136,256]{1,0:T(8,128)(2,1)S(1)}, bf16[3136,256]{1,0:T(8,128)(2,1)}, u32[]{:S(2)}, u32[]{:S(2)}) collective-permute-start(bf16[3136,256]{1,0:T(8,128)(2,1)S(1)} %broadcast_select_fusion), channel_id=1, source_target_pairs={{0,2},{2,0},{4,6},{6,4},{8,10},{10,8},{12,14},{14,12},{16,18},{18,... | collective-permute-start | bytes 4816904 | tf_op jit(solution)/shard_map/ppermute | solution.py:536
  133.8 20.4 %collective-permute-start.3 = (bf16[1568,256]{1,0:T(8,128)(2,1)S(1)}, bf16[1568,256]{1,0:T(8,128)(2,1)S(1)}, u32[]{:S(2)}, u32[]{:S(2)}) collective-permute-start(bf16[1568,256]{1,0:T(8,128)(2,1)S(1)} %broadcast_select_fusion.1), channel_id=1, source_target_pairs={{0,4},{2,6},{4,0},{6,2},{8,12},{10,14},{12,8},{14,10},{16,20},{18,... | collective-permute-start | bytes 2408456 | tf_op jit(solution)/shard_map/ppermute | solution.py:536
  154.6 10.6 %collective-permute-start.4 = (bf16[784,256]{1,0:T(8,128)(2,1)S(1)}, bf16[784,256]{1,0:T(8,128)(2,1)S(1)}, u32[]{:S(2)}, u32[]{:S(2)}) collective-permute-start(bf16[784,256]{1,0:T(8,128)(2,1)S(1)} %broadcast_select_fusion.2), channel_id=1, source_target_pairs={{0,8},{2,10},{4,12},{6,14},{8,0},{10,2},{12,4},{14,6},{16,24},{18,... | collective-permute-start | bytes 1204232 | tf_op jit(solution)/shard_map/ppermute | solution.py:536
  165.4 10.6 %collective-permute-start.5 = (bf16[392,256]{1,0:T(8,128)(2,1)S(1)}, bf16[392,256]{1,0:T(8,128)(2,1)S(1)}, u32[]{:S(2)}, u32[]{:S(2)}) collective-permute-start(bf16[392,256]{1,0:T(8,128)(2,1)S(1)} %broadcast_select_fusion.3), channel_id=1, source_target_pairs={{0,16},{2,18},{4,20},{6,22},{8,24},{10,26},{12,28},{14,30},{16,0},... | collective-permute-start | bytes 602120 | tf_op jit(solution)/shard_map/ppermute | solution.py:536
  176.0 5.9 %collective-permute-start.6 = (bf16[392,256]{1,0:T(8,128)(2,1)S(1)}, bf16[392,256]{1,0:T(8,128)(2,1)S(1)}, u32[]{:S(2)}, u32[]{:S(2)}) collective-permute-start(bf16[392,256]{1,0:T(8,128)(2,1)S(1)} %add_convert_fusion.4), channel_id=1, source_target_pairs={{0,1},{1,0},{2,3},{3,2},{4,5},{5,4},{6,7},{7,6},{8,9},{9,8},{10,11... | collective-permute-start | bytes 602120 | tf_op jit(solution)/shard_map/ppermute | solution.py:531
  182.0 9.3 %collective-permute-start.7 = (bf16[392,256]{1,0:T(8,128)(2,1)S(1)}, bf16[392,256]{1,0:T(8,128)(2,1)S(1)}, u32[]{:S(2)}, u32[]{:S(2)}) collective-permute-start(bf16[392,256]{1,0:T(8,128)(2,1)S(1)} %add_convert_fusion.3), channel_id=1, source_target_pairs={{0,16},{2,18},{4,20},{6,22},{8,24},{10,26},{12,28},{14,30},{16,0},... | collective-permute-start | bytes 602120 | tf_op jit(solution)/shard_map/ppermute | solution.py:542
  191.4 10.3 %collective-permute-start.8 = (bf16[784,256]{1,0:T(8,128)(2,1)S(1)}, bf16[784,256]{1,0:T(8,128)(2,1)S(1)}, u32[]{:S(2)}, u32[]{:S(2)}) collective-permute-start(bf16[784,256]{1,0:T(8,128)(2,1)S(1)} %maximum_select_fusion.3), channel_id=1, source_target_pairs={{0,8},{2,10},{4,12},{6,14},{8,0},{10,2},{12,4},{14,6},{16,24},{18,... | collective-permute-start | bytes 1204232 | tf_op jit(solution)/shard_map/ppermute | solution.py:542
  202.0 19.6 %copy-start.1 = (bf16[4,528,256]{2,1,0:T(8,128)(2,1)S(1)}, bf16[4,528,256]{2,1,0:T(8,128)(2,1)}, u32[]{:S(2)}) copy-start(bf16[4,528,256]{2,1,0:T(8,128)(2,1)} %get-tuple-element.38) | copy-start | bytes 3244036
  202.0 19.1 %collective-permute-start.9 = (bf16[1568,256]{1,0:T(8,128)(2,1)S(1)}, bf16[1568,256]{1,0:T(8,128)(2,1)S(1)}, u32[]{:S(2)}, u32[]{:S(2)}) collective-permute-start(bf16[1568,256]{1,0:T(8,128)(2,1)S(1)} %maximum_select_fusion.2), channel_id=1, source_target_pairs={{0,4},{2,6},{4,0},{6,2},{8,12},{10,14},{12,8},{14,10},{16,20},{18,... | collective-permute-start | bytes 2408456 | tf_op jit(solution)/shard_map/ppermute | solution.py:542
  221.5 3.5 %collective-permute-start.10 = (bf16[3136,256]{1,0:T(8,128)(2,1)S(1)}, bf16[3136,256]{1,0:T(8,128)(2,1)S(1)}, u32[]{:S(2)}, u32[]{:S(2)}) collective-permute-start(bf16[3136,256]{1,0:T(8,128)(2,1)S(1)} %maximum_select_fusion.1), channel_id=1, source_target_pairs={{0,2},{2,0},{4,6},{6,4},{8,10},{10,8},{12,14},{14,12},{16,18},{18,... | collective-permute-start | bytes 4816904 | tf_op jit(solution)/shard_map/ppermute | solution.py:542
  221.7 1.5 copy-start.2
where the time goes:
time: 234 us
  Pallas kernels  109 us (47%)
  waiting for transfers between devices  82.6 us (35%)
  starting transfers between devices  19.8 us (8%)
  local copies, waits for them, and re-layouts  14.1 us (6%)
  other arithmetic  7.18 us (3%)
    pallas_call x1, Pallas kernels, upper_both(): pl.pallas_call(functools.partial(upper_kernel, rows, memory), grid=(micro...  51.7 us
    ppermute x4, waiting for transfers between devices, sum_all(): got = lax.ppermute(jnp.where(upper == 0, high, low), axis, swap)  38.1 us
    ppermute x4, waiting for transfers between devices, sum_all(): got = lax.ppermute(kept, axis, swap)  36.2 us
    pallas_call x1, Pallas kernels, lower_backward(): pl.pallas_call(functools.partial(lower_backward_kernel, memory), grid=(mi...  29.9 us
    pallas_call x1, Pallas kernels, lower_forward(): pl.pallas_call(functools.partial(lower_forward_kernel, rows), grid=(micro...  27.6 us
    ppermute x4, starting transfers between devices, sum_all(): got = lax.ppermute(jnp.where(upper == 0, high, low), axis, swap)  11.5 us
    unnamed x20, local copies, waits for them, and re-layouts  7.46 us
  transfers between devices with their start and end apart: 11, of which 10 were waited for; matrix products, arithmetic and copies ran while one was open for 2% of the time, Pallas kernels for 0%

commit v1 on v0

v1 whole, which is shorter than its diff:
```python
import functools
from typing import Any, NamedTuple

import jax
import jax.numpy as jnp
from jax import lax
from jax.experimental import pallas as pl
from jax.experimental.pallas import tpu as pltpu
from jax.sharding import PartitionSpec as P

EPSILON = 1e-12
DENSITY = 0.3989422804014327
ROOT_HALF = 0.7071067811865476
HEADS = 4
TILE = 16
PIECES = 8
LOW = -1e30
F32, BF16 = jnp.float32, jnp.bfloat16


class Weights(NamedTuple):
    w_query: Any
    b_query: Any
    w_key: Any
    w_value: Any
    b_value: Any
    w_out: Any
    b_out: Any
    gain_attn: Any
    shift_attn: Any
    w_up: Any
    b_up: Any
    w_down: Any
    b_down: Any
    gain_ffn: Any
    shift_ffn: Any


class Stash(NamedTuple):
    x: Any
    query: Any
    key: Any
    value: Any
    prob: Any
    prob_rest: Any
    context_t: Any
    context: Any
    inverse: Any
    normed_attn: Any
    middle: Any
    active: Any
    slope: Any
    normed_ffn: Any


class Rest(NamedTuple):
    x: Any
    query: Any
    key: Any
    value: Any
    context: Any
    attn: Any
    middle: Any
    branch: Any
    up: Any
    active: Any


def dot(a, b):
    return jnp.dot(a, b, preferred_element_type=F32)


def dot_nt(a, b):
    return lax.dot_general(a, b, (((1,), (1,)), ((), ())), preferred_element_type=F32)


def dot_tn(a, b):
    return lax.dot_general(a, b, (((0,), (0,)), ((), ())), preferred_element_type=F32)


def mean(v):
    return jnp.mean(v, axis=-1, keepdims=True)


def column_sum(v):
    return jnp.sum(v.astype(F32), axis=0, keepdims=True)


def normalize(v):
    centred = v - mean(v)
    inverse = lax.rsqrt(mean(centred * centred) + EPSILON)
    return centred * inverse, inverse


def norm_back(grad, normed, inverse):
    return inverse * (grad - mean(grad) - normed * mean(grad * normed))


def gelu_and_slope(u):
    phi = 0.5 + 0.5 * lax.erf(u * ROOT_HALF)
    return u * phi, phi + u * (jnp.exp(u * u * -0.5) * DENSITY)


def head_block(shape, width):
    rows = lax.broadcasted_iota(jnp.int32, shape, 0) // TILE
    lanes = lax.broadcasted_iota(jnp.int32, shape, 1) // width
    return rows == lanes


def spread_heads(rest, width):
    tiled = jnp.concatenate([rest] * HEADS, axis=0)
    return jnp.where(head_block(tiled.shape, width), tiled, jnp.zeros_like(tiled))


def fold_heads(spread, width):
    own = jnp.where(head_block(spread.shape, width), spread, 0.0)
    return own[:TILE] + own[TILE : 2 * TILE] + own[2 * TILE : 3 * TILE] + own[3 * TILE :]


def own_half(pair, h, width):
    lanes = lax.broadcasted_iota(jnp.int32, pair.shape, 1) // width
    return jnp.where(lanes == h % 2, pair, jnp.zeros_like(pair))


def softmax_keys(s, live_rest):
    main = s.shape[0] - TILE
    top, bottom = s[:main], jnp.where(live_rest, s[main:], LOW)
    peak = jnp.maximum(jnp.max(top, axis=0, keepdims=True), jnp.max(bottom, axis=0, keepdims=True))
    top, bottom = jnp.exp(top - peak), jnp.exp(bottom - peak)
    scale = 1.0 / (jnp.sum(top, axis=0, keepdims=True) + jnp.sum(bottom, axis=0, keepdims=True))
    return (top * scale).astype(BF16), (bottom * scale).astype(BF16)


def layer_forward(x, layer, w, st, rows):
    full, features = x.shape
    main = full - TILE
    width = features // HEADS

    def row(ref):
        return ref[layer : layer + 1, :]

    st.x[...] = x
    q = ((dot(x, w.w_query[0]) + row(w.b_query)) * 0.125).astype(BF16)
    k = dot(x, w.w_key[0]).astype(BF16)
    v = (dot(x, w.w_value[0]) + row(w.b_value)).astype(BF16)
    st.query[...] = q
    st.key[...] = k
    st.value[...] = v
    q_t = q[:main].T
    v_t = v[:main].T
    live_rest = lax.broadcasted_iota(jnp.int32, (TILE, 1), 0) < rows - main
    top, bottom = softmax_keys(dot_nt(k, spread_heads(q[main:], width)), live_rest)
    p_rest = jnp.concatenate([top, bottom], axis=0)
    st.prob_rest[...] = p_rest
    context_rest = fold_heads(dot_tn(p_rest, v), width).astype(BF16)
    parts, bottoms, totals = [], [], []
    ones = jnp.ones((TILE, main), BF16)
    for h in range(HEADS):
        pair = slice(2 * width * (h // 2), 2 * width * (h // 2 + 1))
        top, bottom = softmax_keys(dot(own_half(k[:, pair], h, width), q_t[pair, :]), live_rest)
        st.prob[h, :main, :] = top
        st.prob[h, main:, :] = bottom
        bottoms.append(bottom)
        part = dot(jnp.concatenate([v_t[h * width : (h + 1) * width, :], ones], axis=0), top)
        parts.append(part[:width])
        totals.append(jnp.broadcast_to(1.0 / (part[width : width + 1] + column_sum(bottom)), (width, main)))
    context_t = jnp.concatenate(parts, axis=0)
    context_t = context_t + dot_tn(spread_heads(v[main:], width), jnp.concatenate(bottoms, axis=0))
    st.context_t[...] = context_t * jnp.concatenate(totals, axis=0)
    context = jnp.concatenate([context_t.astype(BF16).T, context_rest], axis=0)
    st.context[...] = context
    normed_attn, inverse_attn = normalize(x.astype(F32) + dot(context, w.w_out[0]) + row(w.b_out))
    st.normed_attn[...] = normed_attn
    middle = normed_attn * row(w.gain_attn) + row(w.shift_attn)
    middle_low = middle.astype(BF16)
    st.middle[...] = middle_low
    total = middle + row(w.b_down)
    for c in range(w.w_up.shape[2] // features):
        part = slice(c * features, (c + 1) * features)
        u = dot(middle_low, w.w_up[0, :, part]) + w.b_up[layer : layer + 1, part]
        active, slope = gelu_and_slope(u)
        active = active.astype(BF16)
        st.active[:, part] = active
        st.slope[:, part] = slope.astype(BF16)
        total = total + dot(active, w.w_down[0, part, :])
    normed_ffn, inverse_ffn = normalize(total)
    st.normed_ffn[...] = normed_ffn
    st.inverse[:, 0:1] = inverse_attn
    st.inverse[:, 1:2] = inverse_ffn
    return normed_ffn * row(w.gain_ffn) + row(w.shift_ffn)


def layer_backward(grad_out, layer, w, st, g, rest, grad_up_ref, grad_s_ref, step, steps):
    full, features = st.x.shape
    main = full - TILE
    width = features // HEADS
    place = pl.ds(pl.multiple_of(step * TILE, TILE), TILE)

    def row(ref):
        return ref[layer : layer + 1, :]

    def add(ref, value):
        ref[...] += value

    normed_ffn = st.normed_ffn[...]
    add(g.gain_ffn, column_sum(grad_out * normed_ffn))
    add(g.shift_ffn, column_sum(grad_out))
    grad_sum = norm_back(grad_out * row(w.gain_ffn), normed_ffn, st.inverse[:, 1:2])
    grad_branch = grad_sum.astype(BF16)
    rest.branch[place, :] = grad_branch[main:]
    add(g.b_down, column_sum(grad_branch))
    grad_middle = grad_sum
    for c in range(w.w_up.shape[2] // features):
        part = slice(c * features, (c + 1) * features)
        grad_up = dot_nt(grad_branch, w.w_down[0, part, :]) * st.slope[:, part].astype(F32)
        grad_up = grad_up.astype(BF16)
        grad_up_ref[:, part] = grad_up
        g.b_up[:, part] += column_sum(grad_up)
        grad_middle = grad_middle + dot_nt(grad_up, w.w_up[0, :, part])
    add(g.w_down, dot_tn(st.active[:main, :], grad_branch[:main]))
    add(g.w_up, dot_tn(grad_up_ref[:main, :], st.middle[:main, :]))
    rest.middle[place, :] = st.middle[main:, :]
    rest.up[place, :] = grad_up_ref[main:, :]
    rest.active[place, :] = st.active[main:, :]
    normed_attn = st.normed_attn[...]
    add(g.gain_attn, column_sum(grad_middle * normed_attn))
    add(g.shift_attn, column_sum(grad_middle))
    grad_resid = norm_back(grad_middle * row(w.gain_attn), normed_attn, st.inverse[:, 0:1])
    grad_attn = grad_resid.astype(BF16)
    rest.attn[place, :] = grad_attn[main:]
    rest.context[place, :] = st.context[main:, :]
    add(g.b_out, column_sum(grad_attn))
    add(g.w_out, dot_tn(st.context[:main, :], grad_attn[:main]))
    grad_context = dot_nt(grad_attn, w.w_out[0]).astype(BF16)
    grad_context_t = grad_context[:main].T
    product = grad_context_t.astype(F32) * st.context_t[...]
    q, k, v = st.query[...], st.key[...], st.value[...]
    k_t = k[:main].T
    grad_spread = spread_heads(grad_context[main:], width)
    p_rest = st.prob_rest[...]
    p_rest_wide = p_rest.astype(F32)
    grad_p = dot_nt(v, grad_spread)
    centre = jnp.sum(p_rest_wide * grad_p, axis=0, keepdims=True) / jnp.sum(p_rest_wide, axis=0, keepdims=True)
    grad_s = p_rest_wide * (grad_p - centre)
    grad_s = grad_s.astype(BF16)
    grad_v = dot(p_rest, grad_spread)
    grad_k = dot(grad_s, spread_heads(q[main:], width))
    grad_q_rest = fold_heads(dot_tn(grad_s, k), width).astype(BF16)
    left = lax.broadcasted_iota(jnp.int32, (full, 2 * width), 1) < width
    q_parts, k_parts, v_parts, bottoms = [], [], [], []
    for h in range(0, HEADS, 2):
        pair = slice(width * h, width * (h + 2))
        for i in (h, h + 1):
            own = slice(i * width, (i + 1) * width)
            grad_p = dot(own_half(v[:, pair], i, width), grad_context_t[pair, :])
            grad_s = st.prob[i].astype(F32) * (grad_p - jnp.sum(product[own, :], axis=0, keepdims=True))
            grad_s = grad_s.astype(BF16)
            grad_s_ref[i] = grad_s
            q_parts.append(dot(k_t[own, :], grad_s[:main]))
            bottoms.append(grad_s[main:])
        both = dot(st.prob[h : h + 2].reshape(2 * full, main), grad_context[:main, pair])
        v_parts.append(jnp.where(left, both[:full], both[full:]))
        both = dot(grad_s_ref[h : h + 2].reshape(2 * full, main), q[:main, pair])
        k_parts.append(jnp.where(left, both[:full], both[full:]))
    grad_v = (grad_v + jnp.concatenate(v_parts, axis=1)).astype(BF16)
    grad_k = (grad_k + jnp.concatenate(k_parts, axis=1)).astype(BF16)
    grad_q_t = jnp.concatenate(q_parts, axis=0)
    grad_q_t = grad_q_t + dot_tn(spread_heads(k[main:], width), jnp.concatenate(bottoms, axis=0))
    grad_q = jnp.concatenate([grad_q_t.astype(BF16).T, grad_q_rest], axis=0) * BF16(0.125)
    rest.x[place, :] = st.x[main:, :]
    rest.query[place, :] = grad_q[main:]
    rest.key[place, :] = grad_k[main:]
    rest.value[place, :] = grad_v[main:]
    add(g.b_query, column_sum(grad_q))
    add(g.b_value, column_sum(grad_v))
    x_main = st.x[:main, :]
    add(g.w_query, dot_tn(x_main, grad_q[:main]))
    add(g.w_key, dot_tn(x_main, grad_k[:main]))
    add(g.w_value, dot_tn(x_main, grad_v[:main]))

    @pl.when(step == steps - 1)
    def _():
        x_rest = rest.x[...]
        add(g.w_query, dot_tn(x_rest, rest.query[...]))
        add(g.w_key, dot_tn(x_rest, rest.key[...]))
        add(g.w_value, dot_tn(x_rest, rest.value[...]))
        add(g.w_out, dot_tn(rest.context[...], rest.attn[...]))
        add(g.w_up, dot_tn(rest.up[...], rest.middle[...]))
        add(g.w_down, dot_tn(rest.active[...], rest.branch[...]))

    return (
        grad_resid
        + dot_nt(grad_q, w.w_query[0])
        + dot_nt(grad_k, w.w_key[0])
        + dot_nt(grad_v, w.w_value[0])
    )


def squares(g):
    return (g.w_query, g.w_key, g.w_value, g.w_out)


def lines(g):
    return (g.b_query, g.b_value, g.b_out, g.gain_attn, g.shift_attn, g.b_down, g.gain_ffn, g.shift_ffn)


def packed_rows(features, units):
    used = 4 * features + 2 * units + len(lines(Weights(*range(len(Weights._fields))))) + units // features
    return -(-used // (PIECES * TILE)) * PIECES * TILE


def spans(sizes, rows):
    piece = rows // PIECES
    out, at = [], 0
    for index, size in enumerate(sizes):
        done = 0
        while done < size:
            take = min(size - done, piece - at % piece)
            out.append((index, done, at // piece, at % piece, take))
            done, at = done + take, at + take
    return out


def emit(g, keep, send, ordered, me):
    units, features = g.w_down.shape
    rows = ordered.shape[0]
    piece = rows // PIECES
    chunks = units // features
    arrays = squares(g) + (g.w_up, g.w_down)
    last = [ref[...] for ref in lines(g)]
    last += [g.b_up[:, c * features : (c + 1) * features] for c in range(chunks)]
    sizes = [ref.shape[0] for ref in arrays]
    left = rows - sum(sizes)
    last.append(jnp.zeros((left - len(last), features), F32))
    tail = jnp.concatenate(last, axis=0).astype(BF16)
    for index, start, which, offset, take in spans(sizes + [left], rows):
        if index < len(arrays):
            value = arrays[index][start : start + take, :].astype(BF16)
        else:
            value = tail[start : start + take]
        at = pl.multiple_of((which ^ me) * piece, TILE) + offset
        ordered[pl.ds(pl.multiple_of(at, TILE), take), :] = value
    half = rows // 2
    keep[...] = ordered[:half, :]
    send[...] = ordered[half:, :]


def stash_shapes(full, features, units):
    main = full - TILE
    square = ((full, features), BF16)
    wide = ((full, units), BF16)
    exact = ((full, features), F32)
    return Stash(
        x=square,
        query=square,
        key=square,
        value=square,
        prob=((HEADS, full, main), BF16),
        prob_rest=((full, HEADS * TILE), BF16),
        context_t=((features, main), F32),
        context=square,
        inverse=((full, 2), F32),
        normed_attn=exact,
        middle=square,
        active=wide,
        slope=wide,
        normed_ffn=exact,
    )


def scratch(micro, full, features, units):
    square, line = (features, features), (1, features)
    sums = Weights(
        w_query=square, b_query=line, w_key=square, w_value=square, b_value=line, w_out=square, b_out=line,
        gain_attn=line, shift_attn=line, w_up=(units, features), b_up=(1, units), w_down=(units, features),
        b_down=line, gain_ffn=line, shift_ffn=line,
    )
    rest = Rest(*[(micro * TILE, features)] * 8, up=(micro * TILE, units), active=(micro * TILE, units))
    out = [pltpu.VMEM(size, F32) for size in sums] + [pltpu.VMEM(size, BF16) for size in rest]
    out.append(pltpu.VMEM((full, units), BF16))
    out.append(pltpu.VMEM((HEADS, full, full - TILE), BF16))
    out.append(pltpu.VMEM((packed_rows(features, units), features), BF16))
    return out


def take_scratch(refs):
    count = len(Weights._fields)
    g, refs = Weights(*refs[:count]), refs[count:]
    count = len(Rest._fields)
    return g, Rest(*refs[:count]), *refs[count:]


def weight_specs(weights, layer):
    specs = []
    for weight in weights:
        if weight.ndim == 3:
            specs.append(pl.BlockSpec((1,) + weight.shape[1:], lambda m: (layer, 0, 0)))
        else:
            specs.append(pl.BlockSpec(weight.shape, lambda m: (0, 0)))
    return specs


def by_micro(shape):
    rank = len(shape)
    return pl.BlockSpec((1,) + tuple(shape[1:]), lambda m: (m,) + (0,) * (rank - 1))


def fixed(shape):
    rank = len(shape)
    return pl.BlockSpec(tuple(shape), lambda m: (0,) * rank)


def smem():
    return pl.BlockSpec(memory_space=pltpu.SMEM)


PARAMS = pltpu.CompilerParams(vmem_limit_bytes=60 * 2**20)


def lower_forward_kernel(x_ref, *refs):
    w, refs = Weights(*refs[: len(Weights._fields)]), refs[len(Weights._fields) :]
    out_ref, sent_ref, *refs = refs
    st = Stash(*[ref.at[0] for ref in refs[:-1]])
    padded = refs[-1]
    rows = x_ref.shape[1]
    main = padded.shape[0] - TILE
    padded[main:, :] = jnp.zeros((TILE, padded.shape[1]), BF16)
    padded[:rows, :] = x_ref[0]
    y = layer_forward(padded[...], 0, w, st, rows).astype(BF16)
    out_ref[0] = y
    sent_ref[0] = y[main:]


def lower_forward(hidden, weights, full):
    micro, rows, features = hidden.shape
    outs = [jax.ShapeDtypeStruct((micro, full, features), BF16), jax.ShapeDtypeStruct((micro, TILE, features), BF16)]
    shapes = stash_shapes(full, features, weights.w_up.shape[2])
    outs += [jax.ShapeDtypeStruct((micro,) + shape, kind) for shape, kind in shapes]
    out, sent, *stash = pl.pallas_call(
        lower_forward_kernel,
        grid=(micro,),
        in_specs=[by_micro(hidden.shape)] + weight_specs(weights, 0),
        out_specs=[by_micro(o.shape) for o in outs],
        out_shape=outs,
        scratch_shapes=[pltpu.VMEM((full, features), BF16)],
        compiler_params=PARAMS,
        name="lower_forward",
    )(hidden, *weights)
    return out, sent, Stash(*stash)


def zero_sums(g):
    for ref in g:
        ref[...] = jnp.zeros_like(ref)


def upper_kernel(rows, place_ref, count_ref, x_ref, arrived_ref, cot_ref, target_ref, slot_ref, *refs):
    step, steps = pl.program_id(0), pl.num_programs(0)
    w, refs = Weights(*refs[: len(Weights._fields)]), refs[len(Weights._fields) :]
    out_ref, grad_ref, back_ref, keep_ref, send_ref = refs[:5]
    refs = refs[5:]
    st, refs = Stash(*refs[: len(Stash._fields)]), refs[len(Stash._fields) :]
    cot_wide, *refs = refs
    g, rest, grad_up_ref, grad_s_ref, ordered = take_scratch(refs)
    full, features = x_ref.shape[1:]
    memory = cot_ref.shape[1]
    main = full - TILE

    @pl.when(step == 0)
    def _():
        zero_sums(g)
        cot_wide[...] = jnp.zeros_like(cot_wide)

    lead = place_ref[1] != 0
    x = x_ref[0]
    is_read = lax.broadcasted_iota(jnp.int32, (TILE, features), 0) < memory
    moved = jnp.logical_and(is_read, jnp.logical_not(lead))
    x = jnp.concatenate([jnp.where(moved, arrived_ref[0], x[:TILE]), x[TILE:]], axis=0)
    y = layer_forward(x, 1, w, st, rows)
    out_ref[0] = y[:rows].astype(BF16)
    count = count_ref[step]
    slots = slot_ref.shape[2]
    slot_row = lax.broadcasted_iota(jnp.int32, (main, slots), 0) - memory
    slot_at = lax.broadcasted_iota(jnp.int32, (main, slots), 1)
    hit = jnp.logical_and(slot_row == slot_ref[0], slot_at < count)
    hit = jnp.where(hit, 1.0, 0.0).astype(BF16)
    used = dot(hit, jnp.ones((slots, features), BF16))
    wanted = dot(hit, target_ref[0])
    grad_main = (y[:main] * used - wanted) / count.astype(F32)
    cot_wide[:memory, :] = cot_ref[0].astype(F32)
    grad_out = jnp.concatenate([grad_main, cot_wide[...]], axis=0)
    grad_in = layer_backward(grad_out, 1, w, st, g, rest, grad_up_ref, grad_s_ref, step, steps)
    back_ref[0] = grad_in[:TILE].astype(BF16)
    grad_ref[0, :TILE, :] = jnp.where(moved, 0.0, grad_in[:TILE])
    grad_ref[0, TILE:, :] = grad_in[TILE:]

    @pl.when(step == steps - 1)
    def _():
        emit(g, keep_ref, send_ref, ordered, place_ref[0])


def half_packed(features, units):
    return jax.ShapeDtypeStruct((packed_rows(features, units) // 2, features), BF16)


def upper_both(place, counts, x, arrived, cotangent, targets, slots, weights, rows):
    micro, full, features = x.shape
    units = weights.w_up.shape[2]
    outs = [
        jax.ShapeDtypeStruct((micro, rows, features), BF16),
        jax.ShapeDtypeStruct(x.shape, F32),
        jax.ShapeDtypeStruct((micro, TILE, features), BF16),
        half_packed(features, units),
        half_packed(features, units),
    ]
    ins = (x, arrived, cotangent, targets, slots)
    return pl.pallas_call(
        functools.partial(upper_kernel, rows),
        grid=(micro,),
        in_specs=[smem(), smem()] + [by_micro(a.shape) for a in ins] + weight_specs(weights, 1),
        out_specs=[by_micro(o.shape) for o in outs[:3]] + [fixed(o.shape) for o in outs[3:]],
        out_shape=outs,
        scratch_shapes=[pltpu.VMEM(*shape) for shape in stash_shapes(full, features, units)]
        + [pltpu.VMEM((TILE, features), F32)]
        + scratch(micro, full, features, units),
        compiler_params=PARAMS,
        name="upper_both",
    )(place, counts, *ins, *weights)


def lower_backward_kernel(memory, place_ref, grad_ref, back_ref, *refs):
    step, steps = pl.program_id(0), pl.num_programs(0)
    w, refs = Weights(*refs[: len(Weights._fields)]), refs[len(Weights._fields) :]
    st, refs = Stash(*[ref.at[0] for ref in refs[: len(Stash._fields)]]), refs[len(Stash._fields) :]
    out_ref, keep_ref, send_ref, *refs = refs
    g, rest, grad_up_ref, grad_s_ref, ordered = take_scratch(refs)
    full, features = grad_ref.shape[1:]
    main = full - TILE

    @pl.when(step == 0)
    def _():
        zero_sums(g)

    is_write = lax.broadcasted_iota(jnp.int32, (TILE, features), 0) < memory
    returned = jnp.where(is_write, back_ref[0].astype(F32), 0.0)
    grad_out = jnp.concatenate([grad_ref[0, :main, :], grad_ref[0, main:, :] + returned], axis=0)
    grad_in = layer_backward(grad_out, 0, w, st, g, rest, grad_up_ref, grad_s_ref, step, steps)
    out_ref[0] = grad_in[: out_ref.shape[1]].astype(BF16)

    @pl.when(step == steps - 1)
    def _():
        emit(g, keep_ref, send_ref, ordered, place_ref[0])


def lower_backward(place, grad, back, weights, stash, rows, memory):
    micro, full, features = grad.shape
    units = weights.w_up.shape[2]
    outs = [
        jax.ShapeDtypeStruct((micro, rows, features), BF16),
        half_packed(features, units),
        half_packed(features, units),
    ]
    return pl.pallas_call(
        functools.partial(lower_backward_kernel, memory),
        grid=(micro,),
        in_specs=[smem(), by_micro(grad.shape), by_micro(back.shape)]
        + weight_specs(weights, 0)
        + [by_micro(a.shape) for a in stash],
        out_specs=[by_micro(outs[0].shape)] + [fixed(o.shape) for o in outs[1:]],
        out_shape=outs,
        scratch_shapes=scratch(micro, full, features, units),
        compiler_params=PARAMS,
        name="lower_backward",
    )(place, grad, back, *weights, *stash)


def unpack_kernel(place_ref, lower_keep, lower_got, upper_keep, upper_got, *refs):
    out, ordered = Weights(*refs[: len(Weights._fields)]), refs[-1]
    features, units = out.w_up.shape[1:]
    chunks = units // features
    half = lower_keep.shape[0]
    rows, piece = 2 * half, 2 * half // PIECES
    for layer, (keep, got) in enumerate(((lower_keep, lower_got), (upper_keep, upper_got))):
        me = place_ref[layer]
        ordered[:half, :] = keep[...]
        ordered[half:, :] = got[...]
        sizes = [features] * 4 + [units, units]
        sizes.append(rows - sum(sizes))
        arrays = squares(out) + (out.w_up, out.w_down)
        for index, start, which, offset, take in spans(sizes, rows):
            at = pl.multiple_of((which ^ me) * piece, TILE) + offset
            value = ordered[pl.ds(pl.multiple_of(at, TILE), take), :].astype(F32)
            if index == 4:
                out.w_up[layer, :, start : start + take] = value.T
            elif index < 6:
                arrays[index][layer, start : start + take, :] = value
            else:
                names = lines(out)
                for i, ref in enumerate(names):
                    ref[layer : layer + 1, :] = value[i : i + 1]
                for c in range(chunks):
                    i = len(names) + c
                    out.b_up[layer : layer + 1, c * features : (c + 1) * features] = value[i : i + 1]


def unpack(places, parts, weights):
    outs = [jax.ShapeDtypeStruct(weight.shape, F32) for weight in weights]
    return pl.pallas_call(
        unpack_kernel,
        in_specs=[smem()] + [pl.BlockSpec(memory_space=pltpu.VMEM)] * 4,
        out_specs=[pl.BlockSpec(memory_space=pltpu.VMEM)] * len(outs),
        out_shape=outs,
        scratch_shapes=[pltpu.VMEM((2 * parts[0].shape[0], parts[0].shape[1]), BF16)],
        compiler_params=PARAMS,
        name="unpack",
    )(places, *parts)


def from_behind(value, axis, steps):
    count = lax.axis_size(axis)
    initial, last = (max(0, -steps), min(count, count - steps))
    return lax.ppermute(value, axis, [(source, source + steps) for source in range(initial, last)])


def swap(value, bit):
    axis, step = bit
    return lax.ppermute(value, axis, [(i, i ^ step) for i in range(lax.axis_size(axis))])


def plus(a, b):
    return (a.astype(F32) + b.astype(F32)).astype(BF16)


def place_of(bits):
    me = jnp.int32(0)
    for axis, step in bits:
        me = me * 2 + (lax.axis_index(axis) // step) % 2
    return me


def sum_rest(value, bits):
    kept, halved = value, []
    for axis, step in bits:
        half = kept.shape[0] // 2
        if half % (TILE // 2):
            kept = plus(kept, swap(kept, (axis, step)))
            continue
        halved.append((axis, step))
        upper = (lax.axis_index(axis) // step) % 2
        low, high = kept[:half], kept[half:]
        got = swap(jnp.where(upper == 0, high, low), (axis, step))
        kept = plus(jnp.where(upper == 0, low, high), got)
    for axis, step in reversed(halved):
        upper = (lax.axis_index(axis) // step) % 2
        got = swap(kept, (axis, step))
        kept = jnp.where(upper == 0, jnp.concatenate([kept, got]), jnp.concatenate([got, kept]))
    return kept


def sum_all(lower, upper, lower_bits, upper_bits, rest_bits):
    chains = []
    for (keep, send), bits in ((lower, lower_bits), (upper, upper_bits)):
        chains.append((plus(keep, swap(send, bits[0])), bits))
    for level in (1, 2):
        sent = [swap(kept[kept.shape[0] // 2 :], bits[level]) for kept, bits in chains]
        chains = [(plus(kept[: kept.shape[0] // 2], got), bits) for got, (kept, bits) in zip(sent, chains)]
    size = chains[0][0].shape[0]
    both = sum_rest(jnp.concatenate([kept for kept, _ in chains], axis=0), rest_bits)
    chains = [(both[:size], lower_bits), (both[size:], upper_bits)]
    for level in (2, 1):
        sent = [swap(kept, bits[level]) for kept, bits in chains]
        chains = [(jnp.concatenate([kept, got], axis=0), bits) for got, (kept, bits) in zip(sent, chains)]
    out = []
    for kept, bits in chains:
        out += [kept, swap(kept, bits[0])]
    return out


def local(hidden, write_cotangent, targets, positions, counts, *weights):
    weights = Weights(*weights)
    micro, _, _, rows, features = hidden.shape
    memory = write_cotangent.shape[3]
    full = -(-rows // TILE) * TILE
    bits = [(axis, 1 << i) for axis in ("seg", "item") for i in range(lax.axis_size(axis).bit_length() - 1)]
    core, along, across = ("seg", 1), ("seg", 2), ("item", 1)
    lower_bits, upper_bits = (core, across, along), (core, along, across)
    rest_bits = [bit for bit in bits if bit not in lower_bits]
    lead = (lax.axis_index("seg") == 0).astype(jnp.int32)
    places = [place_of(lower_bits), place_of(upper_bits)]
    lower_place, upper_place = (jnp.stack([place, lead]) for place in places)

    hidden_rows = hidden.reshape(micro, rows, features)
    lower_out, sent, stash = lower_forward(hidden_rows, weights, full)
    arrived = from_behind(sent, "seg", 1)
    out, grad, back, *upper = upper_both(
        upper_place,
        counts.reshape(micro),
        lower_out,
        arrived,
        write_cotangent.reshape(micro, memory, features),
        targets.reshape(micro, targets.shape[3], features),
        positions.reshape(micro, 1, positions.shape[3]),
        weights,
        rows,
    )
    returned = from_behind(back, "seg", -1)
    grad_in, *lower = lower_backward(lower_place, grad, returned, weights, stash, rows, memory)
    parts = sum_all(lower, upper, lower_bits, upper_bits, rest_bits)
    grads = unpack(jnp.stack(places), parts, weights)
    return (out.reshape(hidden.shape), grad_in.reshape(hidden.shape)) + tuple(grads)


def solution(mesh):
    split = P(None, "item", "seg", None, None)
    placed = (split, split, split, P(None, "item", "seg", None), P(None, "item", "seg"))
    count = len(Weights._fields)
    return jax.shard_map(
        local,
        mesh=mesh,
        in_specs=placed + (P(),) * count,
        out_specs=(split, split) + (P(),) * count,
        check_vma=False,
    )
```

time: 234 us -> 199 us (0.85)
  waiting for transfers between devices: 82.6 us -> 39 us
  starting transfers between devices: 19.8 us -> 36.6 us
  local copies, waits for them, and re-layouts: 14.1 us -> 9.19 us
  other arithmetic: 7.18 us -> 3.26 us
    ppermute x9 -> x16, waiting for transfers between devices: 78.6 us -> 37.8 us  [swap(): lax.ppermute(value, axis, [(i, i ^ step) for i in range(lax.axis_size(axi...]
    ppermute x9 -> x16, starting transfers between devices: 15.8 us -> 32.6 us  [swap(): lax.ppermute(value, axis, [(i, i ^ step) for i in range(lax.axis_size(axi...]
    slice x4 -> x5, local copies, waits for them, and re-layouts: 3.7 us -> 0.12 us  [the longest x4 0.09 us: sum_all(): kept[kept.shape[0] // 2:]]
    ppermute x2, waiting for transfers between devices: 4.06 us -> 1.2 us  [from_behind(): lax.ppermute(value, axis, [(source, source + steps) for source in range(i...]
    convert_element_type x6, other arithmetic: 3.55 us -> 0.8 us  [plus(): return (a.astype(F32) + b.astype(F32)).astype(BF16)]
    unnamed x20 -> x26, local copies, waits for them, and re-layouts: 7.46 us -> 9.07 us
    pallas_call x2 -> x3, Pallas kernels: 79.3 us -> 78.1 us  [the longest x1 48.5 us: upper_both(): pl.pallas_call(functools.partial(upper_kernel, rows), grid=(micro,), in_s...]
  transfers between devices with their start and end apart: 11 -> 18, of which waited for: 10 -> 12; matrix products, arithmetic and copies ran while one was open for 2% -> 3% of each run, Pallas kernels for 0% -> 16%
where the time goes in v1:
time: 199 us
  Pallas kernels  109 us (55%)
  waiting for transfers between devices  39 us (20%)
  starting transfers between devices  36.6 us (18%)
  local copies, waits for them, and re-layouts  9.19 us (5%)
  other arithmetic  3.26 us (2%)
    pallas_call x1, Pallas kernels, upper_both(): pl.pallas_call(functools.partial(upper_kernel, rows), grid=(micro,), in_s...  48.5 us
    ppermute x16, waiting for transfers between devices, swap(): lax.ppermute(value, axis, [(i, i ^ step) for i in range(lax.axis_size(axi...  37.8 us
    ppermute x16, starting transfers between devices, swap(): lax.ppermute(value, axis, [(i, i ^ step) for i in range(lax.axis_size(axi...  32.6 us
    pallas_call x1, Pallas kernels, lower_backward(): pl.pallas_call(functools.partial(lower_backward_kernel, memory), grid=(mi...  31.4 us
    pallas_call x1, Pallas kernels, lower_forward(): pl.pallas_call(lower_forward_kernel, grid=(micro,), in_specs=[by_micro(hi...  24 us
    unnamed x26, local copies, waits for them, and re-layouts  9.07 us
    pallas_call x1, Pallas kernels, unpack(): pl.pallas_call(unpack_kernel, in_specs=[smem()] + [pl.BlockSpec(memory_sp...  5.62 us
    ppermute x2, starting transfers between devices, from_behind(): lax.ppermute(value, axis, [(source, source + steps) for source in range(i...  4.04 us
  transfers between devices with their start and end apart: 18, of which 12 were waited for; matrix products, arithmetic and copies ran while one was open for 3% of the time, Pallas kernels for 16%

profile of v1, /device:TPU:0, one launch (start us, length us, event | category | flops | bytes accessed | tf_op | source)
XLA Modules:
  0.0 198.6 jit_solution(7977406753342052403)
XLA Ops:
  0.7 2.4 %copy.43 = bf16[4,1,1,522,256]{4,3,0,2,1:T(8,128)(2,1)} copy(bf16[4,1,1,522,256]{4,0,3,2,1:T(4,128)(2,1)} %param.20) | data formatting | bytes 2138112 | tf_op args[0]
  3.0 24.0 %lower_forward.1 = (bf16[4,528,256]{2,1,0:T(8,128)(2,1)}, bf16[4,16,256]{2,1,0:T(8,128)(2,1)}, bf16[4,528,256]{2,1,0:T(8,128)(2,1)}, bf16[4,528,256]{2,1,0:T(8,1...) custom-call(bf16[4,522,256]{2,1,0:T(8,128)(2,1)} %bitcast.14, ...), custom_call_target="tpu_custom_call" | custom-call | tf_op jit(solution)/shard_map/lower_forward/pallas_call | solution.py:439
  27.0 2.5 %collective-permute-start = (bf16[4,16,256]{2,1,0:T(8,128)(2,1)}, bf16[4,16,256]{2,1,0:T(8,128)(2,1)S(1)}, u32[]{:S(2)}, u32[]{:S(2)}) collective-permute-start(bf16[4,16,256]{2,1,0:T(8,128)(2,1)} %get-tuple-element.57), channel_id=1, source_target_pairs={{0,2},{2,4},{4,6},{6,8},{8,10},{10,12},{12,14},{14,16},{16,18},{18... | collective-permute-start | bytes 98312 | tf_op jit(solution)/shard_map/ppermute | solution.py:622
  31.4 48.5 %upper_both.1 = (bf16[4,522,256]{2,1,0:T(8,128)(2,1)}, f32[4,528,256]{2,1,0:T(8,128)}, bf16[4,16,256]{2,1,0:T(8,128)(2,1)}, bf16[1600,256]{1,0:T(8,128)(2,1)}, bf16[1600,256]{1,0:T(8,128)(2,1)}) custom-call(s32[2]{0:T(128)} %pad_add_fusion.place_ref, s32[4]{0:T(128)} %bitcast.20, bf16[4,528,256]{2,1,0:T(8,128)(2,1)} %get-tuple-element.56.x_ref, ...), custom_call_target="tpu_custom_call" | custom-call | tf_op jit(solution)/shard_map/upper_both/pallas_call | solution.py:517
  79.9 2.7 %collective-permute-start.5 = (bf16[1600,256]{1,0:T(8,128)(2,1)}, bf16[1600,256]{1,0:T(8,128)(2,1)S(1)}, u32[]{:S(2)}, u32[]{:S(2)}) collective-permute-start(bf16[1600,256]{1,0:T(8,128)(2,1)} %get-tuple-element.79), channel_id=1, source_target_pairs={{0,2},{2,0},{4,6},{6,4},{8,10},{10,8},{12,14},{14,12},{16,18},{18,... | collective-permute-start | bytes 2457608 | tf_op jit(solution)/shard_map/ppermute | solution.py:627
  82.6 1.5 collective-permute-start.1
  84.7 1.2 collective-permute-done.1.back_ref
  86.5 31.4 %lower_backward.1 = (bf16[4,522,256]{2,1,0:T(8,128)(2,1)}, bf16[1600,256]{1,0:T(8,128)(2,1)}, bf16[1600,256]{1,0:T(8,128)(2,1)}) custom-call(s32[2]{0:T(128)} %pad_add_fusion.2.place_ref, f32[4,528,256]{2,1,0:T(8,128)} %get-tuple-element.59.grad_ref, bf16[4,16,256]{2,1,0:T(8,128)(2,1)} %copy-done.9, bf16[2,256,256]{2,1,0:T(8,128)(2,1)} %refs_0_.5, ...), custom_call_target="tpu_custom_call" | custom-call | tf_op jit(solution)/shard_map/lower_backward/pallas_call | solution.py:563
  117.9 2.6 %collective-permute-start.2 = (bf16[1600,256]{1,0:T(8,128)(2,1)}, bf16[1600,256]{1,0:T(8,128)(2,1)S(1)}, u32[]{:S(2)}, u32[]{:S(2)}) collective-permute-start(bf16[1600,256]{1,0:T(8,128)(2,1)} %get-tuple-element.77), channel_id=1, source_target_pairs={{0,2},{2,0},{4,6},{6,4},{8,10},{10,8},{12,14},{14,12},{16,18},{18,... | collective-permute-start | bytes 2457608 | tf_op jit(solution)/shard_map/ppermute | solution.py:627
  120.7 3.1 %collective-permute-start.6 = (bf16[800,256]{1,0:T(8,128)(2,1)S(1)}, bf16[800,256]{1,0:T(8,128)(2,1)S(1)}, u32[]{:S(2)}, u32[]{:S(2)}) collective-permute-start(bf16[800,256]{1,0:T(8,128)(2,1)S(1)} %slice.53), channel_id=1, source_target_pairs={{0,4},{2,6},{4,0},{6,2},{8,12},{10,14},{12,8},{14,10},{16,20},{18,... | collective-permute-start | bytes 1228808 | tf_op jit(solution)/shard_map/ppermute | solution.py:627
  124.0 1.6 collective-permute-start.3
  125.6 7.9 %collective-permute-done.6 = bf16[800,256]{1,0:T(8,128)(2,1)S(1)} collective-permute-done((bf16[800,256]{1,0:T(8,128)(2,1)S(1)}, bf16[800,256]{1,0:T(8,128)(2,1)S(1)}, u32[]{:S(2)}, u32[]{:S(2)}) %collective-permute-start.6) | collective-permute-done | bytes 409632 | tf_op jit(solution)/shard_map/ppermute | solution.py:627
  133.6 1.6 collective-permute-start.7
  135.4 3.0 %collective-permute-start.4 = (bf16[400,256]{1,0:T(8,128)(2,1)S(1)}, bf16[400,256]{1,0:T(8,128)(2,1)S(1)}, u32[]{:S(2)}, u32[]{:S(2)}) collective-permute-start(bf16[400,256]{1,0:T(8,128)(2,1)S(1)} %slice.51), channel_id=1, source_target_pairs={{0,4},{2,6},{4,0},{6,2},{8,12},{10,14},{12,8},{14,10},{16,20},{18,... | collective-permute-start | bytes 614408 | tf_op jit(solution)/shard_map/ppermute | solution.py:627
  138.3 1.8 collective-permute-done.7
  140.2 2.5 %collective-permute-done.4 = bf16[400,256]{1,0:T(8,128)(2,1)S(1)} collective-permute-done((bf16[400,256]{1,0:T(8,128)(2,1)S(1)}, bf16[400,256]{1,0:T(8,128)(2,1)S(1)}, u32[]{:S(2)}, u32[]{:S(2)}) %collective-permute-start.4) | collective-permute-done | bytes 204832 | tf_op jit(solution)/shard_map/ppermute | solution.py:627
  142.8 1.8 collective-permute-start.8
  144.7 4.0 %collective-permute-done.8 = bf16[400,256]{1,0:T(8,128)(2,1)S(1)} collective-permute-done((bf16[400,256]{1,0:T(8,128)(2,1)S(1)}, bf16[400,256]{1,0:T(8,128)(2,1)S(1)}, u32[]{:S(2)}, u32[]{:S(2)}) %collective-permute-start.8) | collective-permute-done | bytes 204832 | tf_op jit(solution)/shard_map/ppermute | solution.py:627
  148.8 3.0 %collective-permute-start.9 = (bf16[200,256]{1,0:T(8,128)(2,1)S(1)}, bf16[200,256]{1,0:T(8,128)(2,1)S(1)}, u32[]{:S(2)}, u32[]{:S(2)}) collective-permute-start(bf16[200,256]{1,0:T(8,128)(2,1)S(1)} %broadcast_select_fusion.1), channel_id=1, source_target_pairs={{0,16},{2,18},{4,20},{6,22},{8,24},{10,26},{12,28},{14,30},{16,0},... | collective-permute-start | bytes 307208 | tf_op jit(solution)/shard_map/ppermute | solution.py:627
  151.8 2.9 %collective-permute-done.9 = bf16[200,256]{1,0:T(8,128)(2,1)S(1)} collective-permute-done((bf16[200,256]{1,0:T(8,128)(2,1)S(1)}, bf16[200,256]{1,0:T(8,128)(2,1)S(1)}, u32[]{:S(2)}, u32[]{:S(2)}) %collective-permute-start.9) | collective-permute-done | bytes 102432 | tf_op jit(solution)/shard_map/ppermute | solution.py:627
  154.8 3.5 %collective-permute-start.10 = (bf16[200,256]{1,0:T(8,128)(2,1)S(1)}, bf16[200,256]{1,0:T(8,128)(2,1)S(1)}, u32[]{:S(2)}, u32[]{:S(2)}) collective-permute-start(bf16[200,256]{1,0:T(8,128)(2,1)S(1)} %add_convert_fusion.7), channel_id=1, source_target_pairs={{0,16},{2,18},{4,20},{6,22},{8,24},{10,26},{12,28},{14,30},{16,0},... | collective-permute-start | bytes 307208 | tf_op jit(solution)/shard_map/ppermute | solution.py:627
  158.3 3.3 %collective-permute-done.10 = bf16[200,256]{1,0:T(8,128)(2,1)S(1)} collective-permute-done((bf16[200,256]{1,0:T(8,128)(2,1)S(1)}, bf16[200,256]{1,0:T(8,128)(2,1)S(1)}, u32[]{:S(2)}, u32[]{:S(2)}) %collective-permute-start.10) | collective-permute-done | bytes 102432 | tf_op jit(solution)/shard_map/ppermute | solution.py:627
  161.6 4.2 %collective-permute-start.11 = (bf16[400,256]{1,0:T(8,128)(2,1)S(1)}, bf16[400,256]{1,0:T(8,128)(2,1)S(1)}, u32[]{:S(2)}, u32[]{:S(2)}) collective-permute-start(bf16[400,256]{1,0:T(8,128)(2,1)S(1)} %maximum_select_fusion.1), channel_id=1, source_target_pairs={{0,8},{2,10},{4,12},{6,14},{8,0},{10,2},{12,4},{14,6},{16,24},{18,... | collective-permute-start | bytes 614408 | tf_op jit(solution)/shard_map/ppermute | solution.py:627
  165.8 3.7 %collective-permute-done.11 = bf16[400,256]{1,0:T(8,128)(2,1)S(1)} collective-permute-done((bf16[400,256]{1,0:T(8,128)(2,1)S(1)}, bf16[400,256]{1,0:T(8,128)(2,1)S(1)}, u32[]{:S(2)}, u32[]{:S(2)}) %collective-permute-start.11) | collective-permute-done | bytes 204832 | tf_op jit(solution)/shard_map/ppermute | solution.py:627
  169.8 1.6 collective-permute-start.15
  172.4 5.3 %collective-permute-done.15 = bf16[400,256]{1,0:T(8,128)(2,1)S(1)} collective-permute-done((bf16[400,256]{1,0:T(8,128)(2,1)S(1)}, bf16[400,256]{1,0:T(8,128)(2,1)S(1)}, u32[]{:S(2)}, u32[]{:S(2)}) %collective-permute-start.15) | collective-permute-done | bytes 204832 | tf_op jit(solution)/shard_map/ppermute | solution.py:627
  177.8 1.2 collective-permute-start.16
  179.0 1.6 collective-permute-start.13
  180.6 5.2 %collective-permute-done.16 = bf16[800,256]{1,0:T(8,128)(2,1)S(1)} collective-permute-done((bf16[800,256]{1,0:T(8,128)(2,1)S(1)}, bf16[800,256]{1,0:T(8,128)(2,1)S(1)}, u32[]{:S(2)}, u32[]{:S(2)}) %collective-permute-start.16) | collective-permute-done | bytes 409632 | tf_op jit(solution)/shard_map/ppermute | solution.py:627
  187.9 1.5 copy.39
  189.5 1.5 copy.40
  192.8 5.6 %unpack.1 = (f32[2,256,256]{2,1,0:T(8,128)}, f32[2,256]{1,0:T(2,128)}, f32[2,256,256]{2,1,0:T(8,128)}, f32[2,256,256]{2,1,0:T(8,128)}, f32[2,256]{1,0:T(2,128)},...) custom-call(s32[2]{0:T(128)} %pad_add_fusion.1.place_ref, ...), custom_call_target="tpu_custom_call" | custom-call | tf_op jit(solution)/shard_map/unpack/pallas_call | solution.py:608
  (56 shorter events, 9.4 us)
Async XLA Ops:
  3.0 27.1 %copy-start.10 = (bf16[4,1,1,10,256]{4,0,3,2,1:T(4,128)(2,1)S(1)}, bf16[4,1,1,10,256]{4,0,3,2,1:T(4,128)(2,1)}, u32[]{:S(2)}) copy-start(bf16[4,1,1,10,256]{4,0,3,2,1:T(4,128)(2,1)} %param.21) | copy-start | bytes 61444
  27.0 3.8 %collective-permute-start = (bf16[4,16,256]{2,1,0:T(8,128)(2,1)}, bf16[4,16,256]{2,1,0:T(8,128)(2,1)S(1)}, u32[]{:S(2)}, u32[]{:S(2)}) collective-permute-start(bf16[4,16,256]{2,1,0:T(8,128)(2,1)} %get-tuple-element.57), channel_id=1, source_target_pairs={{0,2},{2,4},{4,6},{6,8},{8,10},{10,12},{12,14},{14,16},{16,18},{18... | collective-permute-start | bytes 98312 | tf_op jit(solution)/shard_map/ppermute | solution.py:622
  30.8 0.6 copy-start.8
  79.9 40.6 %collective-permute-start.5 = (bf16[1600,256]{1,0:T(8,128)(2,1)}, bf16[1600,256]{1,0:T(8,128)(2,1)S(1)}, u32[]{:S(2)}, u32[]{:S(2)}) collective-permute-start(bf16[1600,256]{1,0:T(8,128)(2,1)} %get-tuple-element.79), channel_id=1, source_target_pairs={{0,2},{2,0},{4,6},{6,4},{8,10},{10,8},{12,14},{14,12},{16,18},{18,... | collective-permute-start | bytes 2457608 | tf_op jit(solution)/shard_map/ppermute | solution.py:627
  82.6 3.3 %collective-permute-start.1 = (bf16[4,16,256]{2,1,0:T(8,128)(2,1)}, bf16[4,16,256]{2,1,0:T(8,128)(2,1)S(1)}, u32[]{:S(2)}, u32[]{:S(2)}) collective-permute-start(bf16[4,16,256]{2,1,0:T(8,128)(2,1)} %get-tuple-element.60), channel_id=1, source_target_pairs={{2,0},{4,2},{6,4},{8,6},{10,8},{12,10},{14,12},{16,14},{18,16},{20... | collective-permute-start | bytes 98312 | tf_op jit(solution)/shard_map/ppermute | solution.py:622
  85.9 0.6 copy-start.9
  86.5 34.0 %copy-start.4 = (bf16[1600,256]{1,0:T(8,128)(2,1)S(1)}, bf16[1600,256]{1,0:T(8,128)(2,1)}, u32[]{:S(2)}) copy-start(bf16[1600,256]{1,0:T(8,128)(2,1)} %get-tuple-element.78) | copy-start | bytes 2457604
  117.9 5.9 %collective-permute-start.2 = (bf16[1600,256]{1,0:T(8,128)(2,1)}, bf16[1600,256]{1,0:T(8,128)(2,1)S(1)}, u32[]{:S(2)}, u32[]{:S(2)}) collective-permute-start(bf16[1600,256]{1,0:T(8,128)(2,1)} %get-tuple-element.77), channel_id=1, source_target_pairs={{0,2},{2,0},{4,6},{6,4},{8,10},{10,8},{12,14},{14,12},{16,18},{18,... | collective-permute-start | bytes 2457608 | tf_op jit(solution)/shard_map/ppermute | solution.py:627
  120.5 3.3 %copy-start.6 = (bf16[1600,256]{1,0:T(8,128)(2,1)S(1)}, bf16[1600,256]{1,0:T(8,128)(2,1)}, u32[]{:S(2)}) copy-start(bf16[1600,256]{1,0:T(8,128)(2,1)} %get-tuple-element.76) | copy-start | bytes 2457604
  120.7 12.7 %collective-permute-start.6 = (bf16[800,256]{1,0:T(8,128)(2,1)S(1)}, bf16[800,256]{1,0:T(8,128)(2,1)S(1)}, u32[]{:S(2)}, u32[]{:S(2)}) collective-permute-start(bf16[800,256]{1,0:T(8,128)(2,1)S(1)} %slice.53), channel_id=1, source_target_pairs={{0,4},{2,6},{4,0},{6,2},{8,12},{10,14},{12,8},{14,10},{16,20},{18,... | collective-permute-start | bytes 1228808 | tf_op jit(solution)/shard_map/ppermute | solution.py:627
  124.0 11.2 %collective-permute-start.3 = (bf16[800,256]{1,0:T(8,128)(2,1)S(1)}, bf16[800,256]{1,0:T(8,128)(2,1)S(1)}, u32[]{:S(2)}, u32[]{:S(2)}) collective-permute-start(bf16[800,256]{1,0:T(8,128)(2,1)S(1)} %slice.49), channel_id=1, source_target_pairs={{0,1},{1,0},{2,3},{3,2},{4,5},{5,4},{6,7},{7,6},{8,9},{9,8},{10,11... | collective-permute-start | bytes 1228808 | tf_op jit(solution)/shard_map/ppermute | solution.py:627
  133.6 6.6 %collective-permute-start.7 = (bf16[400,256]{1,0:T(8,128)(2,1)S(1)}, bf16[400,256]{1,0:T(8,128)(2,1)S(1)}, u32[]{:S(2)}, u32[]{:S(2)}) collective-permute-start(bf16[400,256]{1,0:T(8,128)(2,1)S(1)} %slice.55), channel_id=1, source_target_pairs={{0,1},{1,0},{2,3},{3,2},{4,5},{5,4},{6,7},{7,6},{8,9},{9,8},{10,11... | collective-permute-start | bytes 614408 | tf_op jit(solution)/shard_map/ppermute | solution.py:627
  135.4 7.3 %collective-permute-start.4 = (bf16[400,256]{1,0:T(8,128)(2,1)S(1)}, bf16[400,256]{1,0:T(8,128)(2,1)S(1)}, u32[]{:S(2)}, u32[]{:S(2)}) collective-permute-start(bf16[400,256]{1,0:T(8,128)(2,1)S(1)} %slice.51), channel_id=1, source_target_pairs={{0,4},{2,6},{4,0},{6,2},{8,12},{10,14},{12,8},{14,10},{16,20},{18,... | collective-permute-start | bytes 614408 | tf_op jit(solution)/shard_map/ppermute | solution.py:627
  142.8 5.8 %collective-permute-start.8 = (bf16[400,256]{1,0:T(8,128)(2,1)S(1)}, bf16[400,256]{1,0:T(8,128)(2,1)S(1)}, u32[]{:S(2)}, u32[]{:S(2)}) collective-permute-start(bf16[400,256]{1,0:T(8,128)(2,1)S(1)} %broadcast_select_fusion), channel_id=1, source_target_pairs={{0,8},{2,10},{4,12},{6,14},{8,0},{10,2},{12,4},{14,6},{16,24},{18,... | collective-permute-start | bytes 614408 | tf_op jit(solution)/shard_map/ppermute | solution.py:627
  148.8 5.9 %collective-permute-start.9 = (bf16[200,256]{1,0:T(8,128)(2,1)S(1)}, bf16[200,256]{1,0:T(8,128)(2,1)S(1)}, u32[]{:S(2)}, u32[]{:S(2)}) collective-permute-start(bf16[200,256]{1,0:T(8,128)(2,1)S(1)} %broadcast_select_fusion.1), channel_id=1, source_target_pairs={{0,16},{2,18},{4,20},{6,22},{8,24},{10,26},{12,28},{14,30},{16,0},... | collective-permute-start | bytes 307208 | tf_op jit(solution)/shard_map/ppermute | solution.py:627
  154.8 6.8 %collective-permute-start.10 = (bf16[200,256]{1,0:T(8,128)(2,1)S(1)}, bf16[200,256]{1,0:T(8,128)(2,1)S(1)}, u32[]{:S(2)}, u32[]{:S(2)}) collective-permute-start(bf16[200,256]{1,0:T(8,128)(2,1)S(1)} %add_convert_fusion.7), channel_id=1, source_target_pairs={{0,16},{2,18},{4,20},{6,22},{8,24},{10,26},{12,28},{14,30},{16,0},... | collective-permute-start | bytes 307208 | tf_op jit(solution)/shard_map/ppermute | solution.py:627
  161.6 8.0 %collective-permute-start.11 = (bf16[400,256]{1,0:T(8,128)(2,1)S(1)}, bf16[400,256]{1,0:T(8,128)(2,1)S(1)}, u32[]{:S(2)}, u32[]{:S(2)}) collective-permute-start(bf16[400,256]{1,0:T(8,128)(2,1)S(1)} %maximum_select_fusion.1), channel_id=1, source_target_pairs={{0,8},{2,10},{4,12},{6,14},{8,0},{10,2},{12,4},{14,6},{16,24},{18,... | collective-permute-start | bytes 614408 | tf_op jit(solution)/shard_map/ppermute | solution.py:627
  169.8 8.0 %collective-permute-start.15 = (bf16[400,256]{1,0:T(8,128)(2,1)S(1)}, bf16[400,256]{1,0:T(8,128)(2,1)S(1)}, u32[]{:S(2)}, u32[]{:S(2)}) collective-permute-start(bf16[400,256]{1,0:T(8,128)(2,1)S(1)} %get-tuple-element.112), channel_id=1, source_target_pairs={{0,1},{1,0},{2,3},{3,2},{4,5},{5,4},{6,7},{7,6},{8,9},{9,8},{10,11... | collective-permute-start | bytes 614408 | tf_op jit(solution)/shard_map/ppermute | solution.py:627
  171.4 7.6 %collective-permute-start.12 = (bf16[400,256]{1,0:T(8,128)(2,1)S(1)}, bf16[400,256]{1,0:T(8,128)(2,1)S(1)}, u32[]{:S(2)}, u32[]{:S(2)}) collective-permute-start(bf16[400,256]{1,0:T(8,128)(2,1)S(1)} %get-tuple-element.113), channel_id=1, source_target_pairs={{0,4},{2,6},{4,0},{6,2},{8,12},{10,14},{12,8},{14,10},{16,20},{18,... | collective-permute-start | bytes 614408 | tf_op jit(solution)/shard_map/ppermute | solution.py:627
  177.8 8.0 %collective-permute-start.16 = (bf16[800,256]{1,0:T(8,128)(2,1)S(1)}, bf16[800,256]{1,0:T(8,128)(2,1)S(1)}, u32[]{:S(2)}, u32[]{:S(2)}) collective-permute-start(bf16[800,256]{1,0:T(8,128)(2,1)S(1)} %pad_maximum_fusion.3), channel_id=1, source_target_pairs={{0,4},{2,6},{4,0},{6,2},{8,12},{10,14},{12,8},{14,10},{16,20},{18,... | collective-permute-start | bytes 1228808 | tf_op jit(solution)/shard_map/ppermute | solution.py:627
  179.0 8.9 %copy-start.2 = (bf16[4,522,256]{2,1,0:T(8,128)(2,1)S(1)}, bf16[4,522,256]{2,1,0:T(8,128)(2,1)}, u32[]{:S(2)}) copy-start(bf16[4,522,256]{2,1,0:T(8,128)(2,1)} %get-tuple-element.58) | copy-start | bytes 3207172
  179.0 8.0 %collective-permute-start.13 = (bf16[800,256]{1,0:T(8,128)(2,1)S(1)}, bf16[800,256]{1,0:T(8,128)(2,1)S(1)}, u32[]{:S(2)}, u32[]{:S(2)}) collective-permute-start(bf16[800,256]{1,0:T(8,128)(2,1)S(1)} %pad_maximum_fusion.2), channel_id=1, source_target_pairs={{0,1},{1,0},{2,3},{3,2},{4,5},{5,4},{6,7},{7,6},{8,9},{9,8},{10,11... | collective-permute-start | bytes 1228808 | tf_op jit(solution)/shard_map/ppermute | solution.py:627
  185.9 3.6 %copy-start = (bf16[1600,256]{1,0:T(8,128)(2,1)}, bf16[1600,256]{1,0:T(8,128)(2,1)S(1)}, u32[]{:S(2)}) copy-start(bf16[1600,256]{1,0:T(8,128)(2,1)S(1)} %pad_maximum_fusion.1.upper_keep) | copy-start | bytes 2457604
  185.9 3.6 %copy-start.3 = (bf16[4,522,256]{2,1,0:T(8,128)(2,1)S(1)}, bf16[4,522,256]{2,1,0:T(8,128)(2,1)}, u32[]{:S(2)}) copy-start(bf16[4,522,256]{2,1,0:T(8,128)(2,1)} %get-tuple-element.75) | copy-start | bytes 3207172
  185.9 5.1 %collective-permute-start.17 = (bf16[1600,256]{1,0:T(8,128)(2,1)S(1)}, bf16[1600,256]{1,0:T(8,128)(2,1)S(1)}, u32[]{:S(2)}, u32[]{:S(2)}) collective-permute-start(bf16[1600,256]{1,0:T(8,128)(2,1)S(1)} %pad_maximum_fusion.1.upper_keep), channel_id=1, source_target_pairs={{0,2},{2,0},{4,6},{6,4},{8,10},{10,8},{12,14},{14,12},{16,18},{18,... | collective-permute-start | bytes 2457608 | tf_op jit(solution)/shard_map/ppermute | solution.py:627
  187.1 3.9 %copy-start.1 = (bf16[1600,256]{1,0:T(8,128)(2,1)}, bf16[1600,256]{1,0:T(8,128)(2,1)S(1)}, u32[]{:S(2)}) copy-start(bf16[1600,256]{1,0:T(8,128)(2,1)S(1)} %pad_maximum_fusion.lower_keep) | copy-start | bytes 2457604
  187.1 3.9 %collective-permute-start.14 = (bf16[1600,256]{1,0:T(8,128)(2,1)S(1)}, bf16[1600,256]{1,0:T(8,128)(2,1)S(1)}, u32[]{:S(2)}, u32[]{:S(2)}) collective-permute-start(bf16[1600,256]{1,0:T(8,128)(2,1)S(1)} %pad_maximum_fusion.lower_keep), channel_id=1, source_target_pairs={{0,2},{2,0},{4,6},{6,4},{8,10},{10,8},{12,14},{14,12},{16,18},{18,... | collective-permute-start | bytes 2457608 | tf_op jit(solution)/shard_map/ppermute | solution.py:627
  191.0 0.9 copy-start.5
  191.9 0.9 copy-start.7

commit v2 on v1

--- a/solution.py
+++ b/solution.py
@@ -102,8 +102,8 @@
 
 
 def head_block(shape, width):
-    rows = lax.broadcasted_iota(jnp.int32, shape, 0) // TILE
-    lanes = lax.broadcasted_iota(jnp.int32, shape, 1) // width
+    rows = lax.div(lax.broadcasted_iota(jnp.int32, shape, 0), TILE)
+    lanes = lax.div(lax.broadcasted_iota(jnp.int32, shape, 1), width)
     return rows == lanes
 
 
@@ -118,7 +118,7 @@
 
 
 def own_half(pair, h, width):
-    lanes = lax.broadcasted_iota(jnp.int32, pair.shape, 1) // width
+    lanes = lax.div(lax.broadcasted_iota(jnp.int32, pair.shape, 1), width)
     return jnp.where(lanes == h % 2, pair, jnp.zeros_like(pair))
 
 
@@ -131,7 +131,18 @@
     return (top * scale).astype(BF16), (bottom * scale).astype(BF16)
 
 
-def layer_forward(x, layer, w, st, rows):
+def weave(*tasks):
+    tasks = [[task, 0.0, total] for task, total in tasks]
+    while tasks:
+        task = min(tasks, key=lambda t: t[1] / t[2])
+        length = next(task[0], None)
+        if length is None:
+            tasks.remove(task)
+        else:
+            task[1] += length
+
+
+def layer_forward(x, layer, w, st, rows, result):
     full, features = x.shape
     main = full - TILE
     width = features // HEADS
@@ -146,51 +157,73 @@
     st.query[...] = q
     st.key[...] = k
     st.value[...] = v
+    yield 450
     q_t = q[:main].T
     v_t = v[:main].T
     live_rest = lax.broadcasted_iota(jnp.int32, (TILE, 1), 0) < rows - main
     top, bottom = softmax_keys(dot_nt(k, spread_heads(q[main:], width)), live_rest)
     p_rest = jnp.concatenate([top, bottom], axis=0)
     st.prob_rest[...] = p_rest
+    yield 350
     context_rest = fold_heads(dot_tn(p_rest, v), width).astype(BF16)
-    parts, bottoms, totals = [], [], []
     ones = jnp.ones((TILE, main), BF16)
-    for h in range(HEADS):
-        pair = slice(2 * width * (h // 2), 2 * width * (h // 2 + 1))
-        top, bottom = softmax_keys(dot(own_half(k[:, pair], h, width), q_t[pair, :]), live_rest)
-        st.prob[h, :main, :] = top
-        st.prob[h, main:, :] = bottom
-        bottoms.append(bottom)
-        part = dot(jnp.concatenate([v_t[h * width : (h + 1) * width, :], ones], axis=0), top)
-        parts.append(part[:width])
-        totals.append(jnp.broadcast_to(1.0 / (part[width : width + 1] + column_sum(bottom)), (width, main)))
+    scores, weights, parts, bottoms, totals = {}, {}, [], [], []
+    for h in range(-1, HEADS + 1):
+        if h + 1 < HEADS:
+            pair = slice(2 * width * ((h + 1) // 2), 2 * width * ((h + 1) // 2 + 1))
+            scores[h + 1] = dot(own_half(k[:, pair], h + 1, width), q_t[pair, :])
+        if h > 0:
+            top, bottom = weights.pop(h - 1)
+            part = dot(jnp.concatenate([v_t[(h - 1) * width : h * width, :], ones], axis=0), top)
+            parts.append(part[:width])
+            bottoms.append(bottom)
+            totals.append(jnp.broadcast_to(1.0 / (part[width : width + 1] + column_sum(bottom)), (width, main)))
+        if 0 <= h < HEADS:
+            top, bottom = softmax_keys(scores.pop(h), live_rest)
+            st.prob[h, :main, :] = top
+            st.prob[h, main:, :] = bottom
+            weights[h] = top, bottom
+            yield 600
+        else:
+            yield 200
     context_t = jnp.concatenate(parts, axis=0)
     context_t = context_t + dot_tn(spread_heads(v[main:], width), jnp.concatenate(bottoms, axis=0))
     st.context_t[...] = context_t * jnp.concatenate(totals, axis=0)
     context = jnp.concatenate([context_t.astype(BF16).T, context_rest], axis=0)
     st.context[...] = context
+    yield 200
     normed_attn, inverse_attn = normalize(x.astype(F32) + dot(context, w.w_out[0]) + row(w.b_out))
     st.normed_attn[...] = normed_attn
     middle = normed_attn * row(w.gain_attn) + row(w.shift_attn)
     middle_low = middle.astype(BF16)
     st.middle[...] = middle_low
     total = middle + row(w.b_down)
-    for c in range(w.w_up.shape[2] // features):
+    yield 400
+    chunks = w.w_up.shape[2] // features
+
+    def upward(c):
         part = slice(c * features, (c + 1) * features)
-        u = dot(middle_low, w.w_up[0, :, part]) + w.b_up[layer : layer + 1, part]
+        return dot(middle_low, w.w_up[0, :, part]) + w.b_up[layer : layer + 1, part]
+
+    ahead = upward(0)
+    for c in range(chunks):
+        part = slice(c * features, (c + 1) * features)
+        u, ahead = ahead, (upward(c + 1) if c + 1 < chunks else None)
         active, slope = gelu_and_slope(u)
         active = active.astype(BF16)
         st.active[:, part] = active
         st.slope[:, part] = slope.astype(BF16)
         total = total + dot(active, w.w_down[0, part, :])
+        yield 550
     normed_ffn, inverse_ffn = normalize(total)
     st.normed_ffn[...] = normed_ffn
     st.inverse[:, 0:1] = inverse_attn
     st.inverse[:, 1:2] = inverse_ffn
-    return normed_ffn * row(w.gain_ffn) + row(w.shift_ffn)
-
-
-def layer_backward(grad_out, layer, w, st, g, rest, grad_up_ref, grad_s_ref, step, steps):
+    result.append(normed_ffn * row(w.gain_ffn) + row(w.shift_ffn))
+    yield 400
+
+
+def layer_backward(grad_out, layer, w, st, g, rest, grad_up_ref, grad_s_ref, step, result):
     full, features = st.x.shape
     main = full - TILE
     width = features // HEADS
@@ -210,6 +243,7 @@
     rest.branch[place, :] = grad_branch[main:]
     add(g.b_down, column_sum(grad_branch))
     grad_middle = grad_sum
+    yield 500
     for c in range(w.w_up.shape[2] // features):
         part = slice(c * features, (c + 1) * features)
         grad_up = dot_nt(grad_branch, w.w_down[0, part, :]) * st.slope[:, part].astype(F32)
@@ -217,11 +251,14 @@
         grad_up_ref[:, part] = grad_up
         g.b_up[:, part] += column_sum(grad_up)
         grad_middle = grad_middle + dot_nt(grad_up, w.w_up[0, :, part])
+        yield 300
     add(g.w_down, dot_tn(st.active[:main, :], grad_branch[:main]))
+    yield 400
     add(g.w_up, dot_tn(grad_up_ref[:main, :], st.middle[:main, :]))
     rest.middle[place, :] = st.middle[main:, :]
     rest.up[place, :] = grad_up_ref[main:, :]
     rest.active[place, :] = st.active[main:, :]
+    yield 400
     normed_attn = st.normed_attn[...]
     add(g.gain_attn, column_sum(grad_middle * normed_attn))
     add(g.shift_attn, column_sum(grad_middle))
@@ -230,12 +267,14 @@
     rest.attn[place, :] = grad_attn[main:]
     rest.context[place, :] = st.context[main:, :]
     add(g.b_out, column_sum(grad_attn))
+    yield 500
     add(g.w_out, dot_tn(st.context[:main, :], grad_attn[:main]))
     grad_context = dot_nt(grad_attn, w.w_out[0]).astype(BF16)
     grad_context_t = grad_context[:main].T
     product = grad_context_t.astype(F32) * st.context_t[...]
     q, k, v = st.query[...], st.key[...], st.value[...]
     k_t = k[:main].T
+    yield 400
     grad_spread = spread_heads(grad_context[main:], width)
     p_rest = st.prob_rest[...]
     p_rest_wide = p_rest.astype(F32)
@@ -246,6 +285,7 @@
     grad_v = dot(p_rest, grad_spread)
     grad_k = dot(grad_s, spread_heads(q[main:], width))
     grad_q_rest = fold_heads(dot_tn(grad_s, k), width).astype(BF16)
+    yield 400
     left = lax.broadcasted_iota(jnp.int32, (full, 2 * width), 1) < width
     q_parts, k_parts, v_parts, bottoms = [], [], [], []
     for h in range(0, HEADS, 2):
@@ -258,10 +298,13 @@
             grad_s_ref[i] = grad_s
             q_parts.append(dot(k_t[own, :], grad_s[:main]))
             bottoms.append(grad_s[main:])
+            yield 400
         both = dot(st.prob[h : h + 2].reshape(2 * full, main), grad_context[:main, pair])
         v_parts.append(jnp.where(left, both[:full], both[full:]))
+        yield 350
         both = dot(grad_s_ref[h : h + 2].reshape(2 * full, main), q[:main, pair])
         k_parts.append(jnp.where(left, both[:full], both[full:]))
+        yield 350
     grad_v = (grad_v + jnp.concatenate(v_parts, axis=1)).astype(BF16)
     grad_k = (grad_k + jnp.concatenate(k_parts, axis=1)).astype(BF16)
     grad_q_t = jnp.concatenate(q_parts, axis=0)
@@ -273,27 +316,34 @@
     rest.value[place, :] = grad_v[main:]
     add(g.b_query, column_sum(grad_q))
     add(g.b_value, column_sum(grad_v))
+    yield 400
     x_main = st.x[:main, :]
     add(g.w_query, dot_tn(x_main, grad_q[:main]))
     add(g.w_key, dot_tn(x_main, grad_k[:main]))
     add(g.w_value, dot_tn(x_main, grad_v[:main]))
-
-    @pl.when(step == steps - 1)
-    def _():
-        x_rest = rest.x[...]
-        add(g.w_query, dot_tn(x_rest, rest.query[...]))
-        add(g.w_key, dot_tn(x_rest, rest.key[...]))
-        add(g.w_value, dot_tn(x_rest, rest.value[...]))
-        add(g.w_out, dot_tn(rest.context[...], rest.attn[...]))
-        add(g.w_up, dot_tn(rest.up[...], rest.middle[...]))
-        add(g.w_down, dot_tn(rest.active[...], rest.branch[...]))
-
-    return (
+    yield 400
+    result.append(
         grad_resid
         + dot_nt(grad_q, w.w_query[0])
         + dot_nt(grad_k, w.w_key[0])
         + dot_nt(grad_v, w.w_value[0])
     )
+    yield 300
+
+
+def add_rest(g, rest):
+    def add(ref, left, right):
+        ref[...] += dot_tn(left[...], right[...])
+
+    add(g.w_query, rest.x, rest.query)
+    add(g.w_key, rest.x, rest.key)
+    add(g.w_value, rest.x, rest.value)
+    add(g.w_out, rest.context, rest.attn)
+    add(g.w_up, rest.up, rest.middle)
+    add(g.w_down, rest.active, rest.branch)
+
+
+FORWARD, BACKWARD = 6950, 8650
 
 
 def squares(g):
@@ -405,6 +455,16 @@
     return pl.BlockSpec((1,) + tuple(shape[1:]), lambda m: (m,) + (0,) * (rank - 1))
 
 
+def ahead(shape):
+    rank, last = len(shape), shape[0] - 1
+    return pl.BlockSpec((1,) + tuple(shape[1:]), lambda m: (jnp.minimum(m, last),) + (0,) * (rank - 1))
+
+
+def behind(shape):
+    rank = len(shape)
+    return pl.BlockSpec((1,) + tuple(shape[1:]), lambda m: (jnp.maximum(m - 1, 0),) + (0,) * (rank - 1))
+
+
 def fixed(shape):
     rank = len(shape)
     return pl.BlockSpec(tuple(shape), lambda m: (0,) * rank)
@@ -426,7 +486,9 @@
     main = padded.shape[0] - TILE
     padded[main:, :] = jnp.zeros((TILE, padded.shape[1]), BF16)
     padded[:rows, :] = x_ref[0]
-    y = layer_forward(padded[...], 0, w, st, rows).astype(BF16)
+    result = []
+    weave((layer_forward(padded[...], 0, w, st, rows, result), 1))
+    y = result[0].astype(BF16)
     out_ref[0] = y
     sent_ref[0] = y[main:]
 
@@ -454,31 +516,18 @@
         ref[...] = jnp.zeros_like(ref)
 
 
-def upper_kernel(rows, place_ref, count_ref, x_ref, arrived_ref, cot_ref, target_ref, slot_ref, *refs):
-    step, steps = pl.program_id(0), pl.num_programs(0)
-    w, refs = Weights(*refs[: len(Weights._fields)]), refs[len(Weights._fields) :]
-    out_ref, grad_ref, back_ref, keep_ref, send_ref = refs[:5]
-    refs = refs[5:]
-    st, refs = Stash(*refs[: len(Stash._fields)]), refs[len(Stash._fields) :]
-    cot_wide, *refs = refs
-    g, rest, grad_up_ref, grad_s_ref, ordered = take_scratch(refs)
+def upper_forward(rows, lead, arrived_ref, cot_ref, target_ref, slot_ref, count, x_ref, out_ref, grad_out, w, st):
     full, features = x_ref.shape[1:]
     memory = cot_ref.shape[1]
     main = full - TILE
-
-    @pl.when(step == 0)
-    def _():
-        zero_sums(g)
-        cot_wide[...] = jnp.zeros_like(cot_wide)
-
-    lead = place_ref[1] != 0
     x = x_ref[0]
     is_read = lax.broadcasted_iota(jnp.int32, (TILE, features), 0) < memory
     moved = jnp.logical_and(is_read, jnp.logical_not(lead))
     x = jnp.concatenate([jnp.where(moved, arrived_ref[0], x[:TILE]), x[TILE:]], axis=0)
-    y = layer_forward(x, 1, w, st, rows)
+    result = []
+    yield from layer_forward(x, 1, w, st, rows, result)
+    y = result[0]
     out_ref[0] = y[:rows].astype(BF16)
-    count = count_ref[step]
     slots = slot_ref.shape[2]
     slot_row = lax.broadcasted_iota(jnp.int32, (main, slots), 0) - memory
     slot_at = lax.broadcasted_iota(jnp.int32, (main, slots), 1)
@@ -486,16 +535,63 @@
     hit = jnp.where(hit, 1.0, 0.0).astype(BF16)
     used = dot(hit, jnp.ones((slots, features), BF16))
     wanted = dot(hit, target_ref[0])
-    grad_main = (y[:main] * used - wanted) / count.astype(F32)
-    cot_wide[:memory, :] = cot_ref[0].astype(F32)
-    grad_out = jnp.concatenate([grad_main, cot_wide[...]], axis=0)
-    grad_in = layer_backward(grad_out, 1, w, st, g, rest, grad_up_ref, grad_s_ref, step, steps)
+    grad_out[:main, :] = (y[:main] * used - wanted) / count.astype(F32)
+    grad_out[main : main + memory, :] = cot_ref[0].astype(F32)
+    yield 300
+
+
+def upper_backward(lead, memory, grad_out, grad_ref, back_ref, w, st, *refs):
+    result = []
+    yield from layer_backward(grad_out[...], 1, w, st, *refs, result)
+    grad_in = result[0]
+    is_read = lax.broadcasted_iota(jnp.int32, (TILE, grad_in.shape[1]), 0) < memory
+    moved = jnp.logical_and(is_read, jnp.logical_not(lead))
     back_ref[0] = grad_in[:TILE].astype(BF16)
     grad_ref[0, :TILE, :] = jnp.where(moved, 0.0, grad_in[:TILE])
     grad_ref[0, TILE:, :] = grad_in[TILE:]
 
-    @pl.when(step == steps - 1)
+
+def upper_kernel(rows, micro, place_ref, count_ref, x_ref, arrived_ref, cot_ref, target_ref, slot_ref, *refs):
+    step = pl.program_id(0)
+    w, refs = Weights(*refs[: len(Weights._fields)]), refs[len(Weights._fields) :]
+    out_ref, grad_ref, back_ref, keep_ref, send_ref = refs[:5]
+    refs = refs[5:]
+    st, refs = Stash(*refs[: len(Stash._fields)]), refs[len(Stash._fields) :]
+    grad_out, *refs = refs
+    g, rest, grad_up_ref, grad_s_ref, ordered = take_scratch(refs)
+    memory = cot_ref.shape[1]
+    lead = place_ref[1] != 0
+
+    def turn(slot):
+        twice = Stash(*[ref if ref.shape[0] != 2 else ref.at[slot] for ref in st])
+        return twice
+
+    def forward(slot):
+        count = count_ref[jnp.minimum(step, micro - 1)]
+        return upper_forward(
+            rows, lead, arrived_ref, cot_ref, target_ref, slot_ref, count, x_ref, out_ref, grad_out, w, turn(slot)
+        )
+
+    def backward(slot):
+        return upper_backward(
+            lead, memory, grad_out, grad_ref, back_ref, w, turn(slot), g, rest, grad_up_ref, grad_s_ref, step - 1
+        )
+
+    @pl.when(step == 0)
     def _():
+        zero_sums(g)
+        grad_out[grad_out.shape[0] - TILE :, :] = jnp.zeros((TILE, grad_out.shape[1]), F32)
+        weave((forward(0), FORWARD))
+
+    @pl.when(jnp.logical_and(step > 0, step < micro))
+    def _():
+        slot = lax.rem(step, 2)
+        weave((forward(slot), FORWARD), (backward(1 - slot), BACKWARD))
+
+    @pl.when(step == micro)
+    def _():
+        weave((backward((micro - 1) % 2), BACKWARD))
+        add_rest(g, rest)
         emit(g, keep_ref, send_ref, ordered, place_ref[0])
 
 
@@ -514,15 +610,17 @@
         half_packed(features, units),
     ]
     ins = (x, arrived, cotangent, targets, slots)
+    shapes = stash_shapes(full, features, units)
+    once = (shapes.inverse, shapes.normed_attn, shapes.middle, shapes.active, shapes.slope, shapes.normed_ffn)
+    stash = [pltpu.VMEM(s if (s, k) in once and (s, k) != shapes.x else (2,) + s, k) for s, k in shapes] + [pltpu.VMEM((full, features), F32)]
     return pl.pallas_call(
-        functools.partial(upper_kernel, rows),
-        grid=(micro,),
-        in_specs=[smem(), smem()] + [by_micro(a.shape) for a in ins] + weight_specs(weights, 1),
-        out_specs=[by_micro(o.shape) for o in outs[:3]] + [fixed(o.shape) for o in outs[3:]],
+        functools.partial(upper_kernel, rows, micro),
+        grid=(micro + 1,),
+        in_specs=[smem(), smem()] + [ahead(a.shape) for a in ins] + weight_specs(weights, 1),
+        out_specs=[ahead(outs[0].shape), behind(outs[1].shape), behind(outs[2].shape)]
+        + [fixed(o.shape) for o in outs[3:]],
         out_shape=outs,
-        scratch_shapes=[pltpu.VMEM(*shape) for shape in stash_shapes(full, features, units)]
-        + [pltpu.VMEM((TILE, features), F32)]
-        + scratch(micro, full, features, units),
+        scratch_shapes=stash + scratch(micro, full, features, units),
         compiler_params=PARAMS,
         name="upper_both",
     )(place, counts, *ins, *weights)
@@ -544,11 +642,13 @@
     is_write = lax.broadcasted_iota(jnp.int32, (TILE, features), 0) < memory
     returned = jnp.where(is_write, back_ref[0].astype(F32), 0.0)
     grad_out = jnp.concatenate([grad_ref[0, :main, :], grad_ref[0, main:, :] + returned], axis=0)
-    grad_in = layer_backward(grad_out, 0, w, st, g, rest, grad_up_ref, grad_s_ref, step, steps)
-    out_ref[0] = grad_in[: out_ref.shape[1]].astype(BF16)
+    result = []
+    weave((layer_backward(grad_out, 0, w, st, g, rest, grad_up_ref, grad_s_ref, step, result), 1))
+    out_ref[0] = result[0][: out_ref.shape[1]].astype(BF16)
 
     @pl.when(step == steps - 1)
     def _():
+        add_rest(g, rest)
         emit(g, keep_ref, send_ref, ordered, place_ref[0])
 
 

time: 199 us -> 188 us (0.945)
  Pallas kernels: 109 us -> 98.2 us
    pallas_call x1, Pallas kernels: 48.5 us -> 41.5 us  [upper_both(): pl.pallas_call(functools.partial(upper_kernel, rows, micro), grid=(micro...]
    pallas_call x1, Pallas kernels: 24 us -> 21.5 us  [lower_forward(): pl.pallas_call(lower_forward_kernel, grid=(micro,), in_specs=[by_micro(hi...]
where the time goes in v2:
time: 188 us; the launch traced here: 187 us
  Pallas kernels  98.2 us (52%)
  waiting for transfers between devices  40.3 us (21%)
  starting transfers between devices  35.2 us (19%)
  local copies, waits for them, and re-layouts  9.19 us (5%)
  other arithmetic  3.26 us (2%)
    pallas_call x1, Pallas kernels, upper_both(): pl.pallas_call(functools.partial(upper_kernel, rows, micro), grid=(micro...  41.5 us
    ppermute x16, waiting for transfers between devices, swap(): lax.ppermute(value, axis, [(i, i ^ step) for i in range(lax.axis_size(axi...  38.9 us
    ppermute x16, starting transfers between devices, swap(): lax.ppermute(value, axis, [(i, i ^ step) for i in range(lax.axis_size(axi...  31.6 us
    pallas_call x1, Pallas kernels, lower_backward(): pl.pallas_call(functools.partial(lower_backward_kernel, memory), grid=(mi...  29.5 us
    pallas_call x1, Pallas kernels, lower_forward(): pl.pallas_call(lower_forward_kernel, grid=(micro,), in_specs=[by_micro(hi...  21.5 us
    unnamed x26, local copies, waits for them, and re-layouts  9.07 us
    pallas_call x1, Pallas kernels, unpack(): pl.pallas_call(unpack_kernel, in_specs=[smem()] + [pl.BlockSpec(memory_sp...  5.62 us
  transfers between devices with their start and end apart: 18, of which 12 were waited for; matrix products, arithmetic and copies ran while one was open for 3% of the time, Pallas kernels for 16%

profile of v2, /device:TPU:0, one launch (start us, length us, event | category | flops | bytes accessed | tf_op | source)
XLA Modules:
  0.0 187.3 jit_solution(14428415657650978126)
XLA Ops:
  0.7 2.4 %copy.43 = bf16[4,1,1,522,256]{4,3,0,2,1:T(8,128)(2,1)} copy(bf16[4,1,1,522,256]{4,0,3,2,1:T(4,128)(2,1)} %param.20) | data formatting | bytes 2138112 | tf_op args[0]
  3.0 21.5 %lower_forward.1 = (bf16[4,528,256]{2,1,0:T(8,128)(2,1)}, bf16[4,16,256]{2,1,0:T(8,128)(2,1)}, bf16[4,528,256]{2,1,0:T(8,128)(2,1)}, bf16[4,528,256]{2,1,0:T(8,1...) custom-call(bf16[4,522,256]{2,1,0:T(8,128)(2,1)} %bitcast.14, ...), custom_call_target="tpu_custom_call" | custom-call | tf_op jit(solution)/shard_map/lower_forward/pallas_call | solution.py:501
  24.6 2.4 %collective-permute-start = (bf16[4,16,256]{2,1,0:T(8,128)(2,1)}, bf16[4,16,256]{2,1,0:T(8,128)(2,1)S(1)}, u32[]{:S(2)}, u32[]{:S(2)}) collective-permute-start(bf16[4,16,256]{2,1,0:T(8,128)(2,1)} %get-tuple-element.57), channel_id=1, source_target_pairs={{0,2},{2,4},{4,6},{6,8},{8,10},{10,12},{12,14},{14,16},{16,18},{18... | collective-permute-start | bytes 98312 | tf_op jit(solution)/shard_map/ppermute | solution.py:722
  28.8 41.5 %upper_both.1 = (bf16[4,522,256]{2,1,0:T(8,128)(2,1)}, f32[4,528,256]{2,1,0:T(8,128)}, bf16[4,16,256]{2,1,0:T(8,128)(2,1)}, bf16[1600,256]{1,0:T(8,128)(2,1)}, bf16[1600,256]{1,0:T(8,128)(2,1)}) custom-call(s32[2]{0:T(128)} %pad_add_fusion.place_ref, s32[4]{0:T(128)} %bitcast.20, bf16[4,528,256]{2,1,0:T(8,128)(2,1)} %get-tuple-element.56.x_ref, ...), custom_call_target="tpu_custom_call" | custom-call | tf_op jit(solution)/shard_map/upper_both/pallas_call | solution.py:616
  70.3 2.7 %collective-permute-start.5 = (bf16[1600,256]{1,0:T(8,128)(2,1)}, bf16[1600,256]{1,0:T(8,128)(2,1)S(1)}, u32[]{:S(2)}, u32[]{:S(2)}) collective-permute-start(bf16[1600,256]{1,0:T(8,128)(2,1)} %get-tuple-element.79), channel_id=1, source_target_pairs={{0,2},{2,0},{4,6},{6,4},{8,10},{10,8},{12,14},{14,12},{16,18},{18,... | collective-permute-start | bytes 2457608 | tf_op jit(solution)/shard_map/ppermute | solution.py:727
  73.0 1.3 collective-permute-start.1
  74.9 1.4 collective-permute-done.1.back_ref
  76.9 29.5 %lower_backward.1 = (bf16[4,522,256]{2,1,0:T(8,128)(2,1)}, bf16[1600,256]{1,0:T(8,128)(2,1)}, bf16[1600,256]{1,0:T(8,128)(2,1)}) custom-call(s32[2]{0:T(128)} %pad_add_fusion.2.place_ref, f32[4,528,256]{2,1,0:T(8,128)} %get-tuple-element.59.grad_ref, bf16[4,16,256]{2,1,0:T(8,128)(2,1)} %copy-done.9, bf16[2,256,256]{2,1,0:T(8,128)(2,1)} %refs_0_.5, ...), custom_call_target="tpu_custom_call" | custom-call | tf_op jit(solution)/shard_map/lower_backward/pallas_call | solution.py:663
  106.5 2.7 %collective-permute-start.2 = (bf16[1600,256]{1,0:T(8,128)(2,1)}, bf16[1600,256]{1,0:T(8,128)(2,1)S(1)}, u32[]{:S(2)}, u32[]{:S(2)}) collective-permute-start(bf16[1600,256]{1,0:T(8,128)(2,1)} %get-tuple-element.77), channel_id=1, source_target_pairs={{0,2},{2,0},{4,6},{6,4},{8,10},{10,8},{12,14},{14,12},{16,18},{18,... | collective-permute-start | bytes 2457608 | tf_op jit(solution)/shard_map/ppermute | solution.py:727
  109.5 3.1 %collective-permute-start.6 = (bf16[800,256]{1,0:T(8,128)(2,1)S(1)}, bf16[800,256]{1,0:T(8,128)(2,1)S(1)}, u32[]{:S(2)}, u32[]{:S(2)}) collective-permute-start(bf16[800,256]{1,0:T(8,128)(2,1)S(1)} %slice.53), channel_id=1, source_target_pairs={{0,4},{2,6},{4,0},{6,2},{8,12},{10,14},{12,8},{14,10},{16,20},{18,... | collective-permute-start | bytes 1228808 | tf_op jit(solution)/shard_map/ppermute | solution.py:727
  112.8 1.5 collective-permute-start.3
  114.3 7.9 %collective-permute-done.6 = bf16[800,256]{1,0:T(8,128)(2,1)S(1)} collective-permute-done((bf16[800,256]{1,0:T(8,128)(2,1)S(1)}, bf16[800,256]{1,0:T(8,128)(2,1)S(1)}, u32[]{:S(2)}, u32[]{:S(2)}) %collective-permute-start.6) | collective-permute-done | bytes 409632 | tf_op jit(solution)/shard_map/ppermute | solution.py:727
  122.3 1.5 collective-permute-start.7
  124.1 3.0 %collective-permute-start.4 = (bf16[400,256]{1,0:T(8,128)(2,1)S(1)}, bf16[400,256]{1,0:T(8,128)(2,1)S(1)}, u32[]{:S(2)}, u32[]{:S(2)}) collective-permute-start(bf16[400,256]{1,0:T(8,128)(2,1)S(1)} %slice.51), channel_id=1, source_target_pairs={{0,4},{2,6},{4,0},{6,2},{8,12},{10,14},{12,8},{14,10},{16,20},{18,... | collective-permute-start | bytes 614408 | tf_op jit(solution)/shard_map/ppermute | solution.py:727
  127.1 1.8 collective-permute-done.7
  128.9 2.5 %collective-permute-done.4 = bf16[400,256]{1,0:T(8,128)(2,1)S(1)} collective-permute-done((bf16[400,256]{1,0:T(8,128)(2,1)S(1)}, bf16[400,256]{1,0:T(8,128)(2,1)S(1)}, u32[]{:S(2)}, u32[]{:S(2)}) %collective-permute-start.4) | collective-permute-done | bytes 204832 | tf_op jit(solution)/shard_map/ppermute | solution.py:727
  131.5 1.9 collective-permute-start.8
  133.4 4.0 %collective-permute-done.8 = bf16[400,256]{1,0:T(8,128)(2,1)S(1)} collective-permute-done((bf16[400,256]{1,0:T(8,128)(2,1)S(1)}, bf16[400,256]{1,0:T(8,128)(2,1)S(1)}, u32[]{:S(2)}, u32[]{:S(2)}) %collective-permute-start.8) | collective-permute-done | bytes 204832 | tf_op jit(solution)/shard_map/ppermute | solution.py:727
  137.5 3.0 %collective-permute-start.9 = (bf16[200,256]{1,0:T(8,128)(2,1)S(1)}, bf16[200,256]{1,0:T(8,128)(2,1)S(1)}, u32[]{:S(2)}, u32[]{:S(2)}) collective-permute-start(bf16[200,256]{1,0:T(8,128)(2,1)S(1)} %broadcast_select_fusion.1), channel_id=1, source_target_pairs={{0,16},{2,18},{4,20},{6,22},{8,24},{10,26},{12,28},{14,30},{16,0},... | collective-permute-start | bytes 307208 | tf_op jit(solution)/shard_map/ppermute | solution.py:727
  140.6 4.0 %collective-permute-done.9 = bf16[200,256]{1,0:T(8,128)(2,1)S(1)} collective-permute-done((bf16[200,256]{1,0:T(8,128)(2,1)S(1)}, bf16[200,256]{1,0:T(8,128)(2,1)S(1)}, u32[]{:S(2)}, u32[]{:S(2)}) %collective-permute-start.9) | collective-permute-done | bytes 102432 | tf_op jit(solution)/shard_map/ppermute | solution.py:727
  144.6 2.4 %collective-permute-start.10 = (bf16[200,256]{1,0:T(8,128)(2,1)S(1)}, bf16[200,256]{1,0:T(8,128)(2,1)S(1)}, u32[]{:S(2)}, u32[]{:S(2)}) collective-permute-start(bf16[200,256]{1,0:T(8,128)(2,1)S(1)} %add_convert_fusion.7), channel_id=1, source_target_pairs={{0,16},{2,18},{4,20},{6,22},{8,24},{10,26},{12,28},{14,30},{16,0},... | collective-permute-start | bytes 307208 | tf_op jit(solution)/shard_map/ppermute | solution.py:727
  147.0 3.3 %collective-permute-done.10 = bf16[200,256]{1,0:T(8,128)(2,1)S(1)} collective-permute-done((bf16[200,256]{1,0:T(8,128)(2,1)S(1)}, bf16[200,256]{1,0:T(8,128)(2,1)S(1)}, u32[]{:S(2)}, u32[]{:S(2)}) %collective-permute-start.10) | collective-permute-done | bytes 102432 | tf_op jit(solution)/shard_map/ppermute | solution.py:727
  150.4 4.2 %collective-permute-start.11 = (bf16[400,256]{1,0:T(8,128)(2,1)S(1)}, bf16[400,256]{1,0:T(8,128)(2,1)S(1)}, u32[]{:S(2)}, u32[]{:S(2)}) collective-permute-start(bf16[400,256]{1,0:T(8,128)(2,1)S(1)} %maximum_select_fusion.1), channel_id=1, source_target_pairs={{0,8},{2,10},{4,12},{6,14},{8,0},{10,2},{12,4},{14,6},{16,24},{18,... | collective-permute-start | bytes 614408 | tf_op jit(solution)/shard_map/ppermute | solution.py:727
  154.6 3.7 %collective-permute-done.11 = bf16[400,256]{1,0:T(8,128)(2,1)S(1)} collective-permute-done((bf16[400,256]{1,0:T(8,128)(2,1)S(1)}, bf16[400,256]{1,0:T(8,128)(2,1)S(1)}, u32[]{:S(2)}, u32[]{:S(2)}) %collective-permute-start.11) | collective-permute-done | bytes 204832 | tf_op jit(solution)/shard_map/ppermute | solution.py:727
  158.5 1.6 collective-permute-start.15
  161.1 5.4 %collective-permute-done.15 = bf16[400,256]{1,0:T(8,128)(2,1)S(1)} collective-permute-done((bf16[400,256]{1,0:T(8,128)(2,1)S(1)}, bf16[400,256]{1,0:T(8,128)(2,1)S(1)}, u32[]{:S(2)}, u32[]{:S(2)}) %collective-permute-start.15) | collective-permute-done | bytes 204832 | tf_op jit(solution)/shard_map/ppermute | solution.py:727
  166.5 1.1 collective-permute-start.16
  167.7 1.6 collective-permute-start.13
  169.3 5.2 %collective-permute-done.16 = bf16[800,256]{1,0:T(8,128)(2,1)S(1)} collective-permute-done((bf16[800,256]{1,0:T(8,128)(2,1)S(1)}, bf16[800,256]{1,0:T(8,128)(2,1)S(1)}, u32[]{:S(2)}, u32[]{:S(2)}) %collective-permute-start.16) | collective-permute-done | bytes 409632 | tf_op jit(solution)/shard_map/ppermute | solution.py:727
  176.6 1.5 copy.39
  178.2 1.5 copy.40
  181.5 5.6 %unpack.1 = (f32[2,256,256]{2,1,0:T(8,128)}, f32[2,256]{1,0:T(2,128)}, f32[2,256,256]{2,1,0:T(8,128)}, f32[2,256,256]{2,1,0:T(8,128)}, f32[2,256]{1,0:T(2,128)},...) custom-call(s32[2]{0:T(128)} %pad_add_fusion.1.place_ref, ...), custom_call_target="tpu_custom_call" | custom-call | tf_op jit(solution)/shard_map/unpack/pallas_call | solution.py:708
  (56 shorter events, 9.4 us)
Async XLA Ops:
  3.0 24.6 %copy-start.10 = (bf16[4,1,1,10,256]{4,0,3,2,1:T(4,128)(2,1)S(1)}, bf16[4,1,1,10,256]{4,0,3,2,1:T(4,128)(2,1)}, u32[]{:S(2)}) copy-start(bf16[4,1,1,10,256]{4,0,3,2,1:T(4,128)(2,1)} %param.21) | copy-start | bytes 61444
  24.6 3.6 %collective-permute-start = (bf16[4,16,256]{2,1,0:T(8,128)(2,1)}, bf16[4,16,256]{2,1,0:T(8,128)(2,1)S(1)}, u32[]{:S(2)}, u32[]{:S(2)}) collective-permute-start(bf16[4,16,256]{2,1,0:T(8,128)(2,1)} %get-tuple-element.57), channel_id=1, source_target_pairs={{0,2},{2,4},{4,6},{6,8},{8,10},{10,12},{12,14},{14,16},{16,18},{18... | collective-permute-start | bytes 98312 | tf_op jit(solution)/shard_map/ppermute | solution.py:722
  28.2 0.6 copy-start.8
  70.3 38.9 %collective-permute-start.5 = (bf16[1600,256]{1,0:T(8,128)(2,1)}, bf16[1600,256]{1,0:T(8,128)(2,1)S(1)}, u32[]{:S(2)}, u32[]{:S(2)}) collective-permute-start(bf16[1600,256]{1,0:T(8,128)(2,1)} %get-tuple-element.79), channel_id=1, source_target_pairs={{0,2},{2,0},{4,6},{6,4},{8,10},{10,8},{12,14},{14,12},{16,18},{18,... | collective-permute-start | bytes 2457608 | tf_op jit(solution)/shard_map/ppermute | solution.py:727
  73.0 3.3 %collective-permute-start.1 = (bf16[4,16,256]{2,1,0:T(8,128)(2,1)}, bf16[4,16,256]{2,1,0:T(8,128)(2,1)S(1)}, u32[]{:S(2)}, u32[]{:S(2)}) collective-permute-start(bf16[4,16,256]{2,1,0:T(8,128)(2,1)} %get-tuple-element.60), channel_id=1, source_target_pairs={{2,0},{4,2},{6,4},{8,6},{10,8},{12,10},{14,12},{16,14},{18,16},{20... | collective-permute-start | bytes 98312 | tf_op jit(solution)/shard_map/ppermute | solution.py:722
  76.3 0.6 copy-start.9
  76.9 32.3 %copy-start.4 = (bf16[1600,256]{1,0:T(8,128)(2,1)S(1)}, bf16[1600,256]{1,0:T(8,128)(2,1)}, u32[]{:S(2)}) copy-start(bf16[1600,256]{1,0:T(8,128)(2,1)} %get-tuple-element.78) | copy-start | bytes 2457604
  106.5 6.0 %collective-permute-start.2 = (bf16[1600,256]{1,0:T(8,128)(2,1)}, bf16[1600,256]{1,0:T(8,128)(2,1)S(1)}, u32[]{:S(2)}, u32[]{:S(2)}) collective-permute-start(bf16[1600,256]{1,0:T(8,128)(2,1)} %get-tuple-element.77), channel_id=1, source_target_pairs={{0,2},{2,0},{4,6},{6,4},{8,10},{10,8},{12,14},{14,12},{16,18},{18,... | collective-permute-start | bytes 2457608 | tf_op jit(solution)/shard_map/ppermute | solution.py:727
  109.2 3.3 %copy-start.6 = (bf16[1600,256]{1,0:T(8,128)(2,1)S(1)}, bf16[1600,256]{1,0:T(8,128)(2,1)}, u32[]{:S(2)}) copy-start(bf16[1600,256]{1,0:T(8,128)(2,1)} %get-tuple-element.76) | copy-start | bytes 2457604
  109.5 12.7 %collective-permute-start.6 = (bf16[800,256]{1,0:T(8,128)(2,1)S(1)}, bf16[800,256]{1,0:T(8,128)(2,1)S(1)}, u32[]{:S(2)}, u32[]{:S(2)}) collective-permute-start(bf16[800,256]{1,0:T(8,128)(2,1)S(1)} %slice.53), channel_id=1, source_target_pairs={{0,4},{2,6},{4,0},{6,2},{8,12},{10,14},{12,8},{14,10},{16,20},{18,... | collective-permute-start | bytes 1228808 | tf_op jit(solution)/shard_map/ppermute | solution.py:727
  112.8 11.2 %collective-permute-start.3 = (bf16[800,256]{1,0:T(8,128)(2,1)S(1)}, bf16[800,256]{1,0:T(8,128)(2,1)S(1)}, u32[]{:S(2)}, u32[]{:S(2)}) collective-permute-start(bf16[800,256]{1,0:T(8,128)(2,1)S(1)} %slice.49), channel_id=1, source_target_pairs={{0,1},{1,0},{2,3},{3,2},{4,5},{5,4},{6,7},{7,6},{8,9},{9,8},{10,11... | collective-permute-start | bytes 1228808 | tf_op jit(solution)/shard_map/ppermute | solution.py:727
  122.3 6.6 %collective-permute-start.7 = (bf16[400,256]{1,0:T(8,128)(2,1)S(1)}, bf16[400,256]{1,0:T(8,128)(2,1)S(1)}, u32[]{:S(2)}, u32[]{:S(2)}) collective-permute-start(bf16[400,256]{1,0:T(8,128)(2,1)S(1)} %slice.55), channel_id=1, source_target_pairs={{0,1},{1,0},{2,3},{3,2},{4,5},{5,4},{6,7},{7,6},{8,9},{9,8},{10,11... | collective-permute-start | bytes 614408 | tf_op jit(solution)/shard_map/ppermute | solution.py:727
  124.1 7.3 %collective-permute-start.4 = (bf16[400,256]{1,0:T(8,128)(2,1)S(1)}, bf16[400,256]{1,0:T(8,128)(2,1)S(1)}, u32[]{:S(2)}, u32[]{:S(2)}) collective-permute-start(bf16[400,256]{1,0:T(8,128)(2,1)S(1)} %slice.51), channel_id=1, source_target_pairs={{0,4},{2,6},{4,0},{6,2},{8,12},{10,14},{12,8},{14,10},{16,20},{18,... | collective-permute-start | bytes 614408 | tf_op jit(solution)/shard_map/ppermute | solution.py:727
  131.5 5.8 %collective-permute-start.8 = (bf16[400,256]{1,0:T(8,128)(2,1)S(1)}, bf16[400,256]{1,0:T(8,128)(2,1)S(1)}, u32[]{:S(2)}, u32[]{:S(2)}) collective-permute-start(bf16[400,256]{1,0:T(8,128)(2,1)S(1)} %broadcast_select_fusion), channel_id=1, source_target_pairs={{0,8},{2,10},{4,12},{6,14},{8,0},{10,2},{12,4},{14,6},{16,24},{18,... | collective-permute-start | bytes 614408 | tf_op jit(solution)/shard_map/ppermute | solution.py:727
  137.5 7.0 %collective-permute-start.9 = (bf16[200,256]{1,0:T(8,128)(2,1)S(1)}, bf16[200,256]{1,0:T(8,128)(2,1)S(1)}, u32[]{:S(2)}, u32[]{:S(2)}) collective-permute-start(bf16[200,256]{1,0:T(8,128)(2,1)S(1)} %broadcast_select_fusion.1), channel_id=1, source_target_pairs={{0,16},{2,18},{4,20},{6,22},{8,24},{10,26},{12,28},{14,30},{16,0},... | collective-permute-start | bytes 307208 | tf_op jit(solution)/shard_map/ppermute | solution.py:727
  144.6 5.7 %collective-permute-start.10 = (bf16[200,256]{1,0:T(8,128)(2,1)S(1)}, bf16[200,256]{1,0:T(8,128)(2,1)S(1)}, u32[]{:S(2)}, u32[]{:S(2)}) collective-permute-start(bf16[200,256]{1,0:T(8,128)(2,1)S(1)} %add_convert_fusion.7), channel_id=1, source_target_pairs={{0,16},{2,18},{4,20},{6,22},{8,24},{10,26},{12,28},{14,30},{16,0},... | collective-permute-start | bytes 307208 | tf_op jit(solution)/shard_map/ppermute | solution.py:727
  150.4 7.9 %collective-permute-start.11 = (bf16[400,256]{1,0:T(8,128)(2,1)S(1)}, bf16[400,256]{1,0:T(8,128)(2,1)S(1)}, u32[]{:S(2)}, u32[]{:S(2)}) collective-permute-start(bf16[400,256]{1,0:T(8,128)(2,1)S(1)} %maximum_select_fusion.1), channel_id=1, source_target_pairs={{0,8},{2,10},{4,12},{6,14},{8,0},{10,2},{12,4},{14,6},{16,24},{18,... | collective-permute-start | bytes 614408 | tf_op jit(solution)/shard_map/ppermute | solution.py:727
  158.5 8.0 %collective-permute-start.15 = (bf16[400,256]{1,0:T(8,128)(2,1)S(1)}, bf16[400,256]{1,0:T(8,128)(2,1)S(1)}, u32[]{:S(2)}, u32[]{:S(2)}) collective-permute-start(bf16[400,256]{1,0:T(8,128)(2,1)S(1)} %get-tuple-element.112), channel_id=1, source_target_pairs={{0,1},{1,0},{2,3},{3,2},{4,5},{5,4},{6,7},{7,6},{8,9},{9,8},{10,11... | collective-permute-start | bytes 614408 | tf_op jit(solution)/shard_map/ppermute | solution.py:727
  160.1 7.6 %collective-permute-start.12 = (bf16[400,256]{1,0:T(8,128)(2,1)S(1)}, bf16[400,256]{1,0:T(8,128)(2,1)S(1)}, u32[]{:S(2)}, u32[]{:S(2)}) collective-permute-start(bf16[400,256]{1,0:T(8,128)(2,1)S(1)} %get-tuple-element.113), channel_id=1, source_target_pairs={{0,4},{2,6},{4,0},{6,2},{8,12},{10,14},{12,8},{14,10},{16,20},{18,... | collective-permute-start | bytes 614408 | tf_op jit(solution)/shard_map/ppermute | solution.py:727
  166.5 8.0 %collective-permute-start.16 = (bf16[800,256]{1,0:T(8,128)(2,1)S(1)}, bf16[800,256]{1,0:T(8,128)(2,1)S(1)}, u32[]{:S(2)}, u32[]{:S(2)}) collective-permute-start(bf16[800,256]{1,0:T(8,128)(2,1)S(1)} %pad_maximum_fusion.3), channel_id=1, source_target_pairs={{0,4},{2,6},{4,0},{6,2},{8,12},{10,14},{12,8},{14,10},{16,20},{18,... | collective-permute-start | bytes 1228808 | tf_op jit(solution)/shard_map/ppermute | solution.py:727
  167.7 8.9 %copy-start.2 = (bf16[4,522,256]{2,1,0:T(8,128)(2,1)S(1)}, bf16[4,522,256]{2,1,0:T(8,128)(2,1)}, u32[]{:S(2)}) copy-start(bf16[4,522,256]{2,1,0:T(8,128)(2,1)} %get-tuple-element.58) | copy-start | bytes 3207172
  167.7 8.0 %collective-permute-start.13 = (bf16[800,256]{1,0:T(8,128)(2,1)S(1)}, bf16[800,256]{1,0:T(8,128)(2,1)S(1)}, u32[]{:S(2)}, u32[]{:S(2)}) collective-permute-start(bf16[800,256]{1,0:T(8,128)(2,1)S(1)} %pad_maximum_fusion.2), channel_id=1, source_target_pairs={{0,1},{1,0},{2,3},{3,2},{4,5},{5,4},{6,7},{7,6},{8,9},{9,8},{10,11... | collective-permute-start | bytes 1228808 | tf_op jit(solution)/shard_map/ppermute | solution.py:727
  174.6 3.6 %copy-start = (bf16[1600,256]{1,0:T(8,128)(2,1)}, bf16[1600,256]{1,0:T(8,128)(2,1)S(1)}, u32[]{:S(2)}) copy-start(bf16[1600,256]{1,0:T(8,128)(2,1)S(1)} %pad_maximum_fusion.1.upper_keep) | copy-start | bytes 2457604
  174.6 3.6 %copy-start.3 = (bf16[4,522,256]{2,1,0:T(8,128)(2,1)S(1)}, bf16[4,522,256]{2,1,0:T(8,128)(2,1)}, u32[]{:S(2)}) copy-start(bf16[4,522,256]{2,1,0:T(8,128)(2,1)} %get-tuple-element.75) | copy-start | bytes 3207172
  174.6 5.1 %collective-permute-start.17 = (bf16[1600,256]{1,0:T(8,128)(2,1)S(1)}, bf16[1600,256]{1,0:T(8,128)(2,1)S(1)}, u32[]{:S(2)}, u32[]{:S(2)}) collective-permute-start(bf16[1600,256]{1,0:T(8,128)(2,1)S(1)} %pad_maximum_fusion.1.upper_keep), channel_id=1, source_target_pairs={{0,2},{2,0},{4,6},{6,4},{8,10},{10,8},{12,14},{14,12},{16,18},{18,... | collective-permute-start | bytes 2457608 | tf_op jit(solution)/shard_map/ppermute | solution.py:727
  175.8 3.9 %copy-start.1 = (bf16[1600,256]{1,0:T(8,128)(2,1)}, bf16[1600,256]{1,0:T(8,128)(2,1)S(1)}, u32[]{:S(2)}) copy-start(bf16[1600,256]{1,0:T(8,128)(2,1)S(1)} %pad_maximum_fusion.lower_keep) | copy-start | bytes 2457604
  175.8 3.9 %collective-permute-start.14 = (bf16[1600,256]{1,0:T(8,128)(2,1)S(1)}, bf16[1600,256]{1,0:T(8,128)(2,1)S(1)}, u32[]{:S(2)}, u32[]{:S(2)}) collective-permute-start(bf16[1600,256]{1,0:T(8,128)(2,1)S(1)} %pad_maximum_fusion.lower_keep), channel_id=1, source_target_pairs={{0,2},{2,0},{4,6},{6,4},{8,10},{10,8},{12,14},{14,12},{16,18},{18,... | collective-permute-start | bytes 2457608 | tf_op jit(solution)/shard_map/ppermute | solution.py:727
  179.7 0.9 copy-start.5
  180.6 0.9 copy-start.7

commit v3 on v2

--- a/solution.py
+++ b/solution.py
@@ -5,17 +5,21 @@
 import jax.numpy as jnp
 from jax import lax
 from jax.experimental import pallas as pl
+from jax.experimental.layout import Layout, with_layout_constraint
 from jax.experimental.pallas import tpu as pltpu
 from jax.sharding import PartitionSpec as P
 
 EPSILON = 1e-12
 DENSITY = 0.3989422804014327
 ROOT_HALF = 0.7071067811865476
+BELL = -0.7213475204444817
 HEADS = 4
 TILE = 16
+STRIP = 64
 PIECES = 8
 LOW = -1e30
 F32, BF16 = jnp.float32, jnp.bfloat16
+LINE, PAIR = "seg", "item"
 
 
 class Weights(NamedTuple):
@@ -43,6 +47,7 @@
     value: Any
     prob: Any
     prob_rest: Any
+    scale: Any
     context_t: Any
     context: Any
     inverse: Any
@@ -96,11 +101,6 @@
     return inverse * (grad - mean(grad) - normed * mean(grad * normed))
 
 
-def gelu_and_slope(u):
-    phi = 0.5 + 0.5 * lax.erf(u * ROOT_HALF)
-    return u * phi, phi + u * (jnp.exp(u * u * -0.5) * DENSITY)
-
-
 def head_block(shape, width):
     rows = lax.div(lax.broadcasted_iota(jnp.int32, shape, 0), TILE)
     lanes = lax.div(lax.broadcasted_iota(jnp.int32, shape, 1), width)
@@ -122,13 +122,14 @@
     return jnp.where(lanes == h % 2, pair, jnp.zeros_like(pair))
 
 
-def softmax_keys(s, live_rest):
+def weigh_keys(s, live_rest):
     main = s.shape[0] - TILE
     top, bottom = s[:main], jnp.where(live_rest, s[main:], LOW)
     peak = jnp.maximum(jnp.max(top, axis=0, keepdims=True), jnp.max(bottom, axis=0, keepdims=True))
-    top, bottom = jnp.exp(top - peak), jnp.exp(bottom - peak)
-    scale = 1.0 / (jnp.sum(top, axis=0, keepdims=True) + jnp.sum(bottom, axis=0, keepdims=True))
-    return (top * scale).astype(BF16), (bottom * scale).astype(BF16)
+    yield 120
+    top = jnp.exp(top - peak).astype(BF16)
+    yield 220
+    return top, jnp.exp(bottom - peak).astype(BF16)
 
 
 def weave(*tasks):
@@ -152,43 +153,49 @@
 
     st.x[...] = x
     q = ((dot(x, w.w_query[0]) + row(w.b_query)) * 0.125).astype(BF16)
+    yield 150
     k = dot(x, w.w_key[0]).astype(BF16)
+    yield 150
     v = (dot(x, w.w_value[0]) + row(w.b_value)).astype(BF16)
     st.query[...] = q
     st.key[...] = k
     st.value[...] = v
-    yield 450
+    yield 150
     q_t = q[:main].T
     v_t = v[:main].T
     live_rest = lax.broadcasted_iota(jnp.int32, (TILE, 1), 0) < rows - main
-    top, bottom = softmax_keys(dot_nt(k, spread_heads(q[main:], width)), live_rest)
+    top, bottom = yield from weigh_keys(dot_nt(k, spread_heads(q[main:], width)), live_rest)
     p_rest = jnp.concatenate([top, bottom], axis=0)
+    p_rest = (p_rest.astype(F32) * (1.0 / column_sum(p_rest))).astype(BF16)
     st.prob_rest[...] = p_rest
-    yield 350
+    yield 50
     context_rest = fold_heads(dot_tn(p_rest, v), width).astype(BF16)
     ones = jnp.ones((TILE, main), BF16)
-    scores, weights, parts, bottoms, totals = {}, {}, [], [], []
+    scores, weights, parts, bottoms, scales = {}, {}, [], [], []
     for h in range(-1, HEADS + 1):
         if h + 1 < HEADS:
             pair = slice(2 * width * ((h + 1) // 2), 2 * width * ((h + 1) // 2 + 1))
             scores[h + 1] = dot(own_half(k[:, pair], h + 1, width), q_t[pair, :])
+            yield 80
         if h > 0:
             top, bottom = weights.pop(h - 1)
             part = dot(jnp.concatenate([v_t[(h - 1) * width : h * width, :], ones], axis=0), top)
             parts.append(part[:width])
             bottoms.append(bottom)
-            totals.append(jnp.broadcast_to(1.0 / (part[width : width + 1] + column_sum(bottom)), (width, main)))
+            scale = 1.0 / (part[width : width + 1] + column_sum(bottom))
+            st.scale[h - 1 : h, :] = scale
+            scales.append(jnp.broadcast_to(scale, (width, main)))
+            yield 80
         if 0 <= h < HEADS:
-            top, bottom = softmax_keys(scores.pop(h), live_rest)
+            top, bottom = yield from weigh_keys(scores.pop(h), live_rest)
             st.prob[h, :main, :] = top
             st.prob[h, main:, :] = bottom
             weights[h] = top, bottom
-            yield 600
-        else:
-            yield 200
+            yield 60
     context_t = jnp.concatenate(parts, axis=0)
     context_t = context_t + dot_tn(spread_heads(v[main:], width), jnp.concatenate(bottoms, axis=0))
-    st.context_t[...] = context_t * jnp.concatenate(totals, axis=0)
+    context_t = context_t * jnp.concatenate(scales, axis=0)
+    st.context_t[...] = context_t
     context = jnp.concatenate([context_t.astype(BF16).T, context_rest], axis=0)
     st.context[...] = context
     yield 200
@@ -209,12 +216,16 @@
     for c in range(chunks):
         part = slice(c * features, (c + 1) * features)
         u, ahead = ahead, (upward(c + 1) if c + 1 < chunks else None)
-        active, slope = gelu_and_slope(u)
-        active = active.astype(BF16)
+        yield 50
+        phi = 0.5 + 0.5 * lax.erf(u * ROOT_HALF)
+        active = (u * phi).astype(BF16)
         st.active[:, part] = active
+        yield 200
+        slope = phi + u * (jnp.exp2(u * u * BELL) * DENSITY)
         st.slope[:, part] = slope.astype(BF16)
+        yield 220
         total = total + dot(active, w.w_down[0, part, :])
-        yield 550
+        yield 80
     normed_ffn, inverse_ffn = normalize(total)
     st.normed_ffn[...] = normed_ffn
     st.inverse[:, 0:1] = inverse_attn
@@ -248,10 +259,11 @@
         part = slice(c * features, (c + 1) * features)
         grad_up = dot_nt(grad_branch, w.w_down[0, part, :]) * st.slope[:, part].astype(F32)
         grad_up = grad_up.astype(BF16)
+        yield 150
         grad_up_ref[:, part] = grad_up
         g.b_up[:, part] += column_sum(grad_up)
         grad_middle = grad_middle + dot_nt(grad_up, w.w_up[0, :, part])
-        yield 300
+        yield 150
     add(g.w_down, dot_tn(st.active[:main, :], grad_branch[:main]))
     yield 400
     add(g.w_up, dot_tn(grad_up_ref[:main, :], st.middle[:main, :]))
@@ -269,13 +281,14 @@
     add(g.b_out, column_sum(grad_attn))
     yield 500
     add(g.w_out, dot_tn(st.context[:main, :], grad_attn[:main]))
-    grad_context = dot_nt(grad_attn, w.w_out[0]).astype(BF16)
-    grad_context_t = grad_context[:main].T
+    scale = jnp.concatenate([jnp.broadcast_to(st.scale[h : h + 1, :], (width, main)) for h in range(HEADS)], axis=0)
+    grad_context_t = (dot_nt(w.w_out[0], grad_attn[:main]) * scale).astype(BF16)
+    grad_context = grad_context_t.T
     product = grad_context_t.astype(F32) * st.context_t[...]
     q, k, v = st.query[...], st.key[...], st.value[...]
     k_t = k[:main].T
     yield 400
-    grad_spread = spread_heads(grad_context[main:], width)
+    grad_spread = spread_heads(dot_nt(grad_attn[main:], w.w_out[0]).astype(BF16), width)
     p_rest = st.prob_rest[...]
     p_rest_wide = p_rest.astype(F32)
     grad_p = dot_nt(v, grad_spread)
@@ -293,13 +306,15 @@
         for i in (h, h + 1):
             own = slice(i * width, (i + 1) * width)
             grad_p = dot(own_half(v[:, pair], i, width), grad_context_t[pair, :])
+            yield 130
             grad_s = st.prob[i].astype(F32) * (grad_p - jnp.sum(product[own, :], axis=0, keepdims=True))
             grad_s = grad_s.astype(BF16)
             grad_s_ref[i] = grad_s
+            yield 140
             q_parts.append(dot(k_t[own, :], grad_s[:main]))
             bottoms.append(grad_s[main:])
-            yield 400
-        both = dot(st.prob[h : h + 2].reshape(2 * full, main), grad_context[:main, pair])
+            yield 130
+        both = dot(st.prob[h : h + 2].reshape(2 * full, main), grad_context[:, pair])
         v_parts.append(jnp.where(left, both[:full], both[full:]))
         yield 350
         both = dot(grad_s_ref[h : h + 2].reshape(2 * full, main), q[:main, pair])
@@ -339,11 +354,16 @@
     add(g.w_key, rest.x, rest.key)
     add(g.w_value, rest.x, rest.value)
     add(g.w_out, rest.context, rest.attn)
-    add(g.w_up, rest.up, rest.middle)
-    add(g.w_down, rest.active, rest.branch)
-
-
-FORWARD, BACKWARD = 6950, 8650
+    units, features = g.w_down.shape
+
+    @pl.loop(0, units // features)
+    def _(c):
+        part = pl.ds(pl.multiple_of(c * features, features), features)
+        g.w_up[part, :] += dot_tn(rest.up[:, part], rest.middle[...])
+        g.w_down[part, :] += dot_tn(rest.active[:, part], rest.branch[...])
+
+
+FORWARD, BACKWARD = 6000, 8650
 
 
 def squares(g):
@@ -407,6 +427,7 @@
         value=square,
         prob=((HEADS, full, main), BF16),
         prob_rest=((full, HEADS * TILE), BF16),
+        scale=((HEADS, main), F32),
         context_t=((features, main), F32),
         context=square,
         inverse=((full, 2), F32),
@@ -513,7 +534,14 @@
 
 def zero_sums(g):
     for ref in g:
-        ref[...] = jnp.zeros_like(ref)
+        rows, features = ref.shape
+        if rows == 1:
+            ref[...] = jnp.zeros_like(ref)
+        else:
+
+            @pl.loop(0, rows // STRIP)
+            def _(i, ref=ref, features=features):
+                ref[pl.ds(pl.multiple_of(i * STRIP, STRIP), STRIP), :] = jnp.zeros((STRIP, features), F32)
 
 
 def upper_forward(rows, lead, arrived_ref, cot_ref, target_ref, slot_ref, count, x_ref, out_ref, grad_out, w, st):
@@ -551,7 +579,7 @@
     grad_ref[0, TILE:, :] = grad_in[TILE:]
 
 
-def upper_kernel(rows, micro, place_ref, count_ref, x_ref, arrived_ref, cot_ref, target_ref, slot_ref, *refs):
+def upper_kernel(rows, micro, bits, count_ref, x_ref, arrived_ref, cot_ref, target_ref, slot_ref, *refs):
     step = pl.program_id(0)
     w, refs = Weights(*refs[: len(Weights._fields)]), refs[len(Weights._fields) :]
     out_ref, grad_ref, back_ref, keep_ref, send_ref = refs[:5]
@@ -560,7 +588,7 @@
     grad_out, *refs = refs
     g, rest, grad_up_ref, grad_s_ref, ordered = take_scratch(refs)
     memory = cot_ref.shape[1]
-    lead = place_ref[1] != 0
+    lead = lax.axis_index(LINE) == 0
 
     def turn(slot):
         twice = Stash(*[ref if ref.shape[0] != 2 else ref.at[slot] for ref in st])
@@ -592,14 +620,14 @@
     def _():
         weave((backward((micro - 1) % 2), BACKWARD))
         add_rest(g, rest)
-        emit(g, keep_ref, send_ref, ordered, place_ref[0])
+        emit(g, keep_ref, send_ref, ordered, place_of(bits))
 
 
 def half_packed(features, units):
     return jax.ShapeDtypeStruct((packed_rows(features, units) // 2, features), BF16)
 
 
-def upper_both(place, counts, x, arrived, cotangent, targets, slots, weights, rows):
+def upper_both(bits, counts, x, arrived, cotangent, targets, slots, weights, rows):
     micro, full, features = x.shape
     units = weights.w_up.shape[2]
     outs = [
@@ -614,19 +642,19 @@
     once = (shapes.inverse, shapes.normed_attn, shapes.middle, shapes.active, shapes.slope, shapes.normed_ffn)
     stash = [pltpu.VMEM(s if (s, k) in once and (s, k) != shapes.x else (2,) + s, k) for s, k in shapes] + [pltpu.VMEM((full, features), F32)]
     return pl.pallas_call(
-        functools.partial(upper_kernel, rows, micro),
+        functools.partial(upper_kernel, rows, micro, bits),
         grid=(micro + 1,),
-        in_specs=[smem(), smem()] + [ahead(a.shape) for a in ins] + weight_specs(weights, 1),
+        in_specs=[smem()] + [ahead(a.shape) for a in ins] + weight_specs(weights, 1),
         out_specs=[ahead(outs[0].shape), behind(outs[1].shape), behind(outs[2].shape)]
         + [fixed(o.shape) for o in outs[3:]],
         out_shape=outs,
         scratch_shapes=stash + scratch(micro, full, features, units),
         compiler_params=PARAMS,
         name="upper_both",
-    )(place, counts, *ins, *weights)
-
-
-def lower_backward_kernel(memory, place_ref, grad_ref, back_ref, *refs):
+    )(counts, *ins, *weights)
+
+
+def lower_backward_kernel(memory, bits, grad_ref, back_ref, *refs):
     step, steps = pl.program_id(0), pl.num_programs(0)
     w, refs = Weights(*refs[: len(Weights._fields)]), refs[len(Weights._fields) :]
     st, refs = Stash(*[ref.at[0] for ref in refs[: len(Stash._fields)]]), refs[len(Stash._fields) :]
@@ -649,10 +677,10 @@
     @pl.when(step == steps - 1)
     def _():
         add_rest(g, rest)
-        emit(g, keep_ref, send_ref, ordered, place_ref[0])
-
-
-def lower_backward(place, grad, back, weights, stash, rows, memory):
+        emit(g, keep_ref, send_ref, ordered, place_of(bits))
+
+
+def lower_backward(bits, grad, back, weights, stash, rows, memory):
     micro, full, features = grad.shape
     units = weights.w_up.shape[2]
     outs = [
@@ -661,9 +689,9 @@
         half_packed(features, units),
     ]
     return pl.pallas_call(
-        functools.partial(lower_backward_kernel, memory),
+        functools.partial(lower_backward_kernel, memory, bits),
         grid=(micro,),
-        in_specs=[smem(), by_micro(grad.shape), by_micro(back.shape)]
+        in_specs=[by_micro(grad.shape), by_micro(back.shape)]
         + weight_specs(weights, 0)
         + [by_micro(a.shape) for a in stash],
         out_specs=[by_micro(outs[0].shape)] + [fixed(o.shape) for o in outs[1:]],
@@ -671,49 +699,74 @@
         scratch_shapes=scratch(micro, full, features, units),
         compiler_params=PARAMS,
         name="lower_backward",
-    )(place, grad, back, *weights, *stash)
-
-
-def unpack_kernel(place_ref, lower_keep, lower_got, upper_keep, upper_got, *refs):
-    out, ordered = Weights(*refs[: len(Weights._fields)]), refs[-1]
+    )(grad, back, *weights, *stash)
+
+
+def unpack_kernel(place_of_layer, *refs):
+    sources, refs = refs[:4], refs[4:]
+    out, refs = Weights(*refs[: len(Weights._fields)]), refs[len(Weights._fields) :]
+    ordered, *staged, in_sems, out_sems = refs
     features, units = out.w_up.shape[1:]
     chunks = units // features
-    half = lower_keep.shape[0]
+    half = sources[0].shape[0]
     rows, piece = 2 * half, 2 * half // PIECES
-    for layer, (keep, got) in enumerate(((lower_keep, lower_got), (upper_keep, upper_got))):
-        me = place_ref[layer]
-        ordered[:half, :] = keep[...]
-        ordered[half:, :] = got[...]
-        sizes = [features] * 4 + [units, units]
-        sizes.append(rows - sum(sizes))
-        arrays = squares(out) + (out.w_up, out.w_down)
+    arrays = squares(out) + (out.w_up, out.w_down)
+    loads = [
+        pltpu.make_async_copy(source, ordered.at[i // 2, (i % 2) * half : (i % 2 + 1) * half], in_sems.at[i])
+        for i, source in enumerate(sources)
+    ]
+    for load in loads:
+        load.start()
+    for load in loads:
+        load.wait()
+    sizes = [features] * 4 + [units, units]
+    sizes.append(rows - sum(sizes))
+    me = [place_of_layer(layer) for layer in range(2)]
+
+    def store(index, layer):
+        return pltpu.make_async_copy(staged[index].at[layer], arrays[index].at[layer], out_sems.at[layer, index])
+
+    @pl.loop(0, 2)
+    def _(layer):
+        mine = jnp.where(layer == 0, me[0], me[1])
         for index, start, which, offset, take in spans(sizes, rows):
-            at = pl.multiple_of((which ^ me) * piece, TILE) + offset
-            value = ordered[pl.ds(pl.multiple_of(at, TILE), take), :].astype(F32)
+            at = pl.multiple_of((which ^ mine) * piece, TILE) + offset
+            value = ordered[layer, pl.ds(pl.multiple_of(at, TILE), take), :]
             if index == 4:
-                out.w_up[layer, :, start : start + take] = value.T
+                staged[index][layer, :, start : start + take] = value.T.astype(F32)
             elif index < 6:
-                arrays[index][layer, start : start + take, :] = value
+                staged[index][layer, start : start + take, :] = value.astype(F32)
             else:
+                value = value.astype(F32)
                 names = lines(out)
                 for i, ref in enumerate(names):
-                    ref[layer : layer + 1, :] = value[i : i + 1]
+                    ref[pl.ds(layer, 1), :] = value[i : i + 1]
                 for c in range(chunks):
                     i = len(names) + c
-                    out.b_up[layer : layer + 1, c * features : (c + 1) * features] = value[i : i + 1]
-
-
-def unpack(places, parts, weights):
+                    out.b_up[pl.ds(layer, 1), c * features : (c + 1) * features] = value[i : i + 1]
+            if index < 6 and start + take == sizes[index]:
+                store(index, layer).start()
+
+    for layer in range(2):
+        for index in range(6):
+            store(index, layer).wait()
+
+
+def unpack(bits, parts, weights):
     outs = [jax.ShapeDtypeStruct(weight.shape, F32) for weight in weights]
+    shapes = Weights(*outs)
+    large = squares(shapes) + (shapes.w_up, shapes.w_down)
     return pl.pallas_call(
-        unpack_kernel,
-        in_specs=[smem()] + [pl.BlockSpec(memory_space=pltpu.VMEM)] * 4,
-        out_specs=[pl.BlockSpec(memory_space=pltpu.VMEM)] * len(outs),
+        functools.partial(unpack_kernel, lambda layer: place_of(bits[layer])),
+        in_specs=[pl.BlockSpec(memory_space=pl.ANY)] * 4,
+        out_specs=[pl.BlockSpec(memory_space=pl.ANY if len(o.shape) == 3 else pltpu.VMEM) for o in outs],
         out_shape=outs,
-        scratch_shapes=[pltpu.VMEM((2 * parts[0].shape[0], parts[0].shape[1]), BF16)],
-        compiler_params=PARAMS,
+        scratch_shapes=[pltpu.VMEM((2, 2 * parts[0].shape[0], parts[0].shape[1]), BF16)]
+        + [pltpu.VMEM(o.shape, F32) for o in large]
+        + [pltpu.SemaphoreType.DMA((4,)), pltpu.SemaphoreType.DMA((2, 6))],
+        compiler_params=pltpu.CompilerParams(vmem_limit_bytes=20 * 2**20),
         name="unpack",
-    )(places, *parts)
+    )(*parts)
 
 
 def from_behind(value, axis, steps):
@@ -734,36 +787,45 @@
 def place_of(bits):
     me = jnp.int32(0)
     for axis, step in bits:
-        me = me * 2 + (lax.axis_index(axis) // step) % 2
+        me = me * 2 + lax.rem(lax.div(lax.axis_index(axis), step), 2)
     return me
 
 
 def sum_rest(value, bits):
-    kept, halved = value, []
-    for axis, step in bits:
-        half = kept.shape[0] // 2
-        if half % (TILE // 2):
-            kept = plus(kept, swap(kept, (axis, step)))
-            continue
-        halved.append((axis, step))
-        upper = (lax.axis_index(axis) // step) % 2
-        low, high = kept[:half], kept[half:]
-        got = swap(jnp.where(upper == 0, high, low), (axis, step))
-        kept = plus(jnp.where(upper == 0, low, high), got)
-    for axis, step in reversed(halved):
-        upper = (lax.axis_index(axis) // step) % 2
-        got = swap(kept, (axis, step))
-        kept = jnp.where(upper == 0, jnp.concatenate([kept, got]), jnp.concatenate([got, kept]))
-    return kept
-
-
-def sum_all(lower, upper, lower_bits, upper_bits, rest_bits):
+    axis, step = bits[0]
+    me = (lax.axis_index(axis) // step) % 4
+
+    def across(part, k):
+        return lax.ppermute(part, axis, [(i, i ^ (k * step)) for i in range(lax.axis_size(axis))])
+
+    rows = value.shape[0] // 4
+    quarter = [lax.dynamic_slice_in_dim(value, (me ^ k) * rows, rows) for k in range(4)]
+    got = [across(quarter[k], k) for k in (1, 2, 3)]
+    kept = quarter[0].astype(F32)
+    for part in got:
+        kept = kept + part.astype(F32)
+    kept = kept.astype(BF16)
+    for bit in bits[2:]:
+        kept = plus(kept, swap(kept, bit))
+    a, b, c, d = [kept] + [across(kept, k) for k in (1, 2, 3)]
+    odd, high = me % 2 == 1, me >= 2
+    first, second = jnp.where(odd, b, a), jnp.where(odd, a, b)
+    third, fourth = jnp.where(odd, d, c), jnp.where(odd, c, d)
+    lower, upper = jnp.concatenate([first, second], axis=0), jnp.concatenate([third, fourth], axis=0)
+    return jnp.where(high, jnp.concatenate([upper, lower], axis=0), jnp.concatenate([lower, upper], axis=0))
+
+
+def sum_all(lower, upper, lower_bits, upper_bits, rest_bits, others):
     chains = []
     for (keep, send), bits in ((lower, lower_bits), (upper, upper_bits)):
         chains.append((plus(keep, swap(send, bits[0])), bits))
     for level in (1, 2):
         sent = [swap(kept[kept.shape[0] // 2 :], bits[level]) for kept, bits in chains]
         chains = [(plus(kept[: kept.shape[0] // 2], got), bits) for got, (kept, bits) in zip(sent, chains)]
+        if level == 1:
+            others = [with_layout_constraint(jnp.transpose(v, (1, 0, 2)), Layout((0, 1, 2))) for v in others]
+            others, tied = lax.optimization_barrier((others, [kept for kept, _ in chains]))
+            chains = [(kept, bits) for kept, (_, bits) in zip(tied, chains)]
     size = chains[0][0].shape[0]
     both = sum_rest(jnp.concatenate([kept for kept, _ in chains], axis=0), rest_bits)
     chains = [(both[:size], lower_bits), (both[size:], upper_bits)]
@@ -773,7 +835,7 @@
     out = []
     for kept, bits in chains:
         out += [kept, swap(kept, bits[0])]
-    return out
+    return out, others
 
 
 def local(hidden, write_cotangent, targets, positions, counts, *weights):
@@ -781,19 +843,16 @@
     micro, _, _, rows, features = hidden.shape
     memory = write_cotangent.shape[3]
     full = -(-rows // TILE) * TILE
-    bits = [(axis, 1 << i) for axis in ("seg", "item") for i in range(lax.axis_size(axis).bit_length() - 1)]
-    core, along, across = ("seg", 1), ("seg", 2), ("item", 1)
+    bits = [(axis, 1 << i) for axis in (LINE, PAIR) for i in range(lax.axis_size(axis).bit_length() - 1)]
+    core, along, across = (LINE, 1), (LINE, 2), (PAIR, 1)
     lower_bits, upper_bits = (core, across, along), (core, along, across)
     rest_bits = [bit for bit in bits if bit not in lower_bits]
-    lead = (lax.axis_index("seg") == 0).astype(jnp.int32)
-    places = [place_of(lower_bits), place_of(upper_bits)]
-    lower_place, upper_place = (jnp.stack([place, lead]) for place in places)
 
     hidden_rows = hidden.reshape(micro, rows, features)
     lower_out, sent, stash = lower_forward(hidden_rows, weights, full)
-    arrived = from_behind(sent, "seg", 1)
+    arrived = from_behind(sent, LINE, 1)
     out, grad, back, *upper = upper_both(
-        upper_place,
+        upper_bits,
         counts.reshape(micro),
         lower_out,
         arrived,
@@ -803,16 +862,17 @@
         weights,
         rows,
     )
-    returned = from_behind(back, "seg", -1)
-    grad_in, *lower = lower_backward(lower_place, grad, returned, weights, stash, rows, memory)
-    parts = sum_all(lower, upper, lower_bits, upper_bits, rest_bits)
-    grads = unpack(jnp.stack(places), parts, weights)
-    return (out.reshape(hidden.shape), grad_in.reshape(hidden.shape)) + tuple(grads)
+    returned = from_behind(back, LINE, -1)
+    grad_in, *lower = lower_backward(lower_bits, grad, returned, weights, stash, rows, memory)
+    parts, (out, grad_in) = sum_all(lower, upper, lower_bits, upper_bits, rest_bits, (out, grad_in))
+    grads = unpack((lower_bits, upper_bits), parts, weights)
+    out, grad_in = (jnp.transpose(v, (1, 0, 2)).reshape(hidden.shape) for v in (out, grad_in))
+    return (out, grad_in) + tuple(grads)
 
 
 def solution(mesh):
-    split = P(None, "item", "seg", None, None)
-    placed = (split, split, split, P(None, "item", "seg", None), P(None, "item", "seg"))
+    split = P(None, PAIR, LINE, None, None)
+    placed = (split, split, split, P(None, PAIR, LINE, None), P(None, PAIR, LINE))
     count = len(Weights._fields)
     return jax.shard_map(
         local,

time: 188 us -> 179 us (0.952)
  starting transfers between devices: 35.2 us -> 31.9 us
  Pallas kernels: 98.2 us -> 95.6 us
    ppermute x16 -> x12, waiting for transfers between devices: 38.9 us -> 24 us  [swap(): lax.ppermute(value, axis, [(i, i ^ step) for i in range(lax.axis_size(axi...]
    ppermute x0 -> x6, waiting for transfers between devices: none -> 14.3 us  [across(): lax.ppermute(part, axis, [(i, i ^ k * step) for i in range(lax.axis_size(...]
    ppermute x16 -> x12, starting transfers between devices: 31.6 us -> 20.3 us  [swap(): lax.ppermute(value, axis, [(i, i ^ step) for i in range(lax.axis_size(axi...]
    ppermute x0 -> x6, starting transfers between devices: none -> 7.98 us  [across(): lax.ppermute(part, axis, [(i, i ^ k * step) for i in range(lax.axis_size(...]
    unnamed x26 -> x16, local copies, waits for them, and re-layouts: 9.07 us -> 4.22 us
    pallas_call x0 -> x2, local copies, waits for them, and re-layouts: none -> 3.05 us  [the longest x1 1.53 us: upper_both(): pl.pallas_call(functools.partial(upper_kernel, rows, micro, bits), grid=(...]
    pallas_call x3, Pallas kernels: 76.6 us -> 74.7 us  [the longest x1 40.6 us: upper_both(): pl.pallas_call(functools.partial(upper_kernel, rows, micro, bits), grid=(...]
    another operation x3 -> x0, other arithmetic: 1.93 us -> none  [the longest x2 1.18 us: local(): lower_place, upper_place = (jnp.stack([place, lead]) for place in places)]
  transfers between devices with their start and end apart: 18 -> 20, of which waited for: 12 -> 16; matrix products, arithmetic and copies ran while one was open for 3% -> 3% of each run, Pallas kernels for 16% -> 17%
where the time goes in v3:
time: 179 us
  Pallas kernels  95.6 us (53%)
  waiting for transfers between devices  40.8 us (23%)
  starting transfers between devices  31.9 us (18%)
  local copies, waits for them, and re-layouts  7.39 us (4%)
  other arithmetic  2.1 us (1%)
    pallas_call x1, Pallas kernels, upper_both(): pl.pallas_call(functools.partial(upper_kernel, rows, micro, bits), grid=(...  40.6 us
    pallas_call x1, Pallas kernels, lower_backward(): pl.pallas_call(functools.partial(lower_backward_kernel, memory, bits), gr...  29.8 us
    ppermute x12, waiting for transfers between devices, swap(): lax.ppermute(value, axis, [(i, i ^ step) for i in range(lax.axis_size(axi...  24 us
    pallas_call x1, Pallas kernels, lower_forward(): pl.pallas_call(lower_forward_kernel, grid=(micro,), in_specs=[by_micro(hi...  20.9 us
    ppermute x12, starting transfers between devices, swap(): lax.ppermute(value, axis, [(i, i ^ step) for i in range(lax.axis_size(axi...  20.3 us
    ppermute x6, waiting for transfers between devices, across(): lax.ppermute(part, axis, [(i, i ^ k * step) for i in range(lax.axis_size(...  14.3 us
    ppermute x6, starting transfers between devices, across(): lax.ppermute(part, axis, [(i, i ^ k * step) for i in range(lax.axis_size(...  7.98 us
    unnamed x16, local copies, waits for them, and re-layouts  4.22 us
  transfers between devices with their start and end apart: 20, of which 16 were waited for; matrix products, arithmetic and copies ran while one was open for 3% of the time, Pallas kernels for 17%

profile of v3, /device:TPU:0, one launch (start us, length us, event | category | flops | bytes accessed | tf_op | source)
XLA Modules:
  0.0 178.8 jit_solution(14279182482924961900)
XLA Ops:
  0.7 2.4 %copy.45 = bf16[4,1,1,522,256]{4,3,0,2,1:T(8,128)(2,1)} copy(bf16[4,1,1,522,256]{4,0,3,2,1:T(4,128)(2,1)} %param.20) | data formatting | bytes 2138112 | tf_op args[0]
  3.0 20.9 %lower_forward.1 = (bf16[4,528,256]{2,1,0:T(8,128)(2,1)}, bf16[4,16,256]{2,1,0:T(8,128)(2,1)}, bf16[4,528,256]{2,1,0:T(8,128)(2,1)}, bf16[4,528,256]{2,1,0:T(8,1...) custom-call(bf16[4,522,256]{2,1,0:T(8,128)(2,1)} %bitcast.21, ...), custom_call_target="tpu_custom_call" | custom-call | tf_op jit(solution)/shard_map/lower_forward/pallas_call | solution.py:522
  23.9 2.4 %collective-permute-start = (bf16[4,16,256]{2,1,0:T(8,128)(2,1)}, bf16[4,16,256]{2,1,0:T(8,128)(2,1)S(1)}, u32[]{:S(2)}, u32[]{:S(2)}) collective-permute-start(bf16[4,16,256]{2,1,0:T(8,128)(2,1)} %get-tuple-element.62), channel_id=1, source_target_pairs={{0,2},{2,4},{4,6},{6,8},{8,10},{10,12},{12,14},{14,16},{16,18},{18... | collective-permute-start | bytes 98312 | tf_op jit(solution)/shard_map/ppermute | solution.py:775
  27.9 40.6 %upper_both.1 = (bf16[4,522,256]{2,1,0:T(8,128)(2,1)}, f32[4,528,256]{2,1,0:T(8,128)}, bf16[4,16,256]{2,1,0:T(8,128)(2,1)}, bf16[1600,256]{1,0:T(8,128)(2,1)}, bf16[1600,256]{1,0:T(8,128)(2,1)}) custom-call(s32[4]{0:T(128)} %bitcast.27, bf16[4,528,256]{2,1,0:T(8,128)(2,1)} %get-tuple-element.61.x_ref, bf16[4,16,256]{2,1,0:T(8,128)(2,1)} %copy-done.5, ...), custom_call_target="tpu_custom_call" | custom-call | tf_op jit(solution)/shard_map/upper_both/pallas_call | solution.py:644
  68.6 3.0 %collective-permute-start.4 = (bf16[1600,256]{1,0:T(8,128)(2,1)}, bf16[1600,256]{1,0:T(8,128)(2,1)S(1)}, u32[]{:S(2)}, u32[]{:S(2)}) collective-permute-start(bf16[1600,256]{1,0:T(8,128)(2,1)} %get-tuple-element.85), channel_id=1, source_target_pairs={{0,2},{2,0},{4,6},{6,4},{8,10},{10,8},{12,14},{14,12},{16,18},{18,... | collective-permute-start | bytes 2457608 | tf_op jit(solution)/shard_map/ppermute | solution.py:780
  72.8 2.0 %collective-permute-done.1.back_ref = bf16[4,16,256]{2,1,0:T(8,128)(2,1)S(1)} collective-permute-done((bf16[4,16,256]{2,1,0:T(8,128)(2,1)}, bf16[4,16,256]{2,1,0:T(8,128)(2,1)S(1)}, u32[]{:S(2)}, u32[]{:S(2)}) %collective-permute-start.1) | collective-permute-done | bytes 32800 | tf_op jit(solution)/shard_map/ppermute | solution.py:775
  75.4 29.8 %lower_backward.1 = (bf16[4,522,256]{2,1,0:T(8,128)(2,1)}, bf16[1600,256]{1,0:T(8,128)(2,1)}, bf16[1600,256]{1,0:T(8,128)(2,1)}) custom-call(f32[4,528,256]{2,1,0:T(8,128)} %get-tuple-element.64.grad_ref, bf16[4,16,256]{2,1,0:T(8,128)(2,1)} %copy-done.4, bf16[2,256,256]{2,1,0:T(8,128)(2,1)} %refs_0_.5, f32[2,256]{1,0:T(2,128)} %refs_1_.5, ...), custom_call_target="tpu_custom_call" | custom-call | tf_op jit(solution)/shard_map/lower_backward/pallas_call | solution.py:691
  105.3 2.7 %collective-permute-start.2 = (bf16[1600,256]{1,0:T(8,128)(2,1)}, bf16[1600,256]{1,0:T(8,128)(2,1)S(1)}, u32[]{:S(2)}, u32[]{:S(2)}) collective-permute-start(bf16[1600,256]{1,0:T(8,128)(2,1)} %get-tuple-element.83), channel_id=1, source_target_pairs={{0,2},{2,0},{4,6},{6,4},{8,10},{10,8},{12,14},{14,12},{16,18},{18,... | collective-permute-start | bytes 2457608 | tf_op jit(solution)/shard_map/ppermute | solution.py:780
  108.3 3.0 %collective-permute-start.5 = (bf16[800,256]{1,0:T(8,128)(2,1)S(1)}, bf16[800,256]{1,0:T(8,128)(2,1)S(1)}, u32[]{:S(2)}, u32[]{:S(2)}) collective-permute-start(bf16[800,256]{1,0:T(8,128)(2,1)S(1)} %slice.43), channel_id=1, source_target_pairs={{0,4},{2,6},{4,0},{6,2},{8,12},{10,14},{12,8},{14,10},{16,20},{18,... | collective-permute-start | bytes 1228808 | tf_op jit(solution)/shard_map/ppermute | solution.py:780
  111.6 1.6 collective-permute-start.3
  113.2 1.5 copy.47
  114.7 1.5 copy.46
  116.2 4.8 %collective-permute-done.5 = bf16[800,256]{1,0:T(8,128)(2,1)S(1)} collective-permute-done((bf16[800,256]{1,0:T(8,128)(2,1)S(1)}, bf16[800,256]{1,0:T(8,128)(2,1)S(1)}, u32[]{:S(2)}, u32[]{:S(2)}) %collective-permute-start.5) | collective-permute-done | bytes 409632 | tf_op jit(solution)/shard_map/ppermute | solution.py:780
  121.1 1.7 collective-permute-done.3
  122.9 2.5 %collective-permute-start.6 = (bf16[400,256]{1,0:T(8,128)(2,1)S(1)}, bf16[400,256]{1,0:T(8,128)(2,1)S(1)}, u32[]{:S(2)}, u32[]{:S(2)}) collective-permute-start(bf16[400,256]{1,0:T(8,128)(2,1)S(1)} %slice.35), channel_id=1, source_target_pairs={{0,4},{2,6},{4,0},{6,2},{8,12},{10,14},{12,8},{14,10},{16,20},{18,... | collective-permute-start | bytes 614408 | tf_op jit(solution)/shard_map/ppermute | solution.py:780
  125.5 1.6 collective-permute-start.7
  127.0 3.2 %collective-permute-done.6 = bf16[400,256]{1,0:T(8,128)(2,1)S(1)} collective-permute-done((bf16[400,256]{1,0:T(8,128)(2,1)S(1)}, bf16[400,256]{1,0:T(8,128)(2,1)S(1)}, u32[]{:S(2)}, u32[]{:S(2)}) %collective-permute-start.6) | collective-permute-done | bytes 204832 | tf_op jit(solution)/shard_map/ppermute | solution.py:780
  130.3 1.5 collective-permute-done.7
  132.6 2.5 %collective-permute-start.10 = (bf16[200,256]{1,0:T(8,128)(2,1)S(1)}, bf16[200,256]{1,0:T(8,128)(2,1)S(1)}, u32[]{:S(2)}, u32[]{:S(2)}) collective-permute-start(bf16[200,256]{1,0:T(8,128)(2,1)S(1)} %get-tuple-element.109), channel_id=1, source_target_pairs={{0,24},{2,26},{4,28},{6,30},{8,16},{10,18},{12,20},{14,22},{16,8},... | collective-permute-start | bytes 307208 | tf_op jit(solution)/shard_map/ppermute | solution.py:799
  135.8 1.3 collective-permute-start.8
  137.1 3.2 %collective-permute-done.10 = bf16[200,256]{1,0:T(8,128)(2,1)S(1)} collective-permute-done((bf16[200,256]{1,0:T(8,128)(2,1)S(1)}, bf16[200,256]{1,0:T(8,128)(2,1)S(1)}, u32[]{:S(2)}, u32[]{:S(2)}) %collective-permute-start.10) | collective-permute-done | bytes 102432 | tf_op jit(solution)/shard_map/ppermute | solution.py:799
  140.3 3.2 %collective-permute-done.9 = bf16[200,256]{1,0:T(8,128)(2,1)S(1)} collective-permute-done((bf16[200,256]{1,0:T(8,128)(2,1)S(1)}, bf16[200,256]{1,0:T(8,128)(2,1)S(1)}, u32[]{:S(2)}, u32[]{:S(2)}) %collective-permute-start.9) | collective-permute-done | bytes 102432 | tf_op jit(solution)/shard_map/ppermute | solution.py:799
  143.8 2.5 %collective-permute-start.11 = (bf16[200,256]{1,0:T(8,128)(2,1)S(1)}, bf16[200,256]{1,0:T(8,128)(2,1)S(1)}, u32[]{:S(2)}, u32[]{:S(2)}) collective-permute-start(bf16[200,256]{1,0:T(8,128)(2,1)S(1)} %add_convert_fusion.6), channel_id=1, source_target_pairs={{0,24},{2,26},{4,28},{6,30},{8,16},{10,18},{12,20},{14,22},{16,8},... | collective-permute-start | bytes 307208 | tf_op jit(solution)/shard_map/ppermute | solution.py:799
  147.2 2.6 %collective-permute-done.13 = bf16[200,256]{1,0:T(8,128)(2,1)S(1)} collective-permute-done((bf16[200,256]{1,0:T(8,128)(2,1)S(1)}, bf16[200,256]{1,0:T(8,128)(2,1)S(1)}, u32[]{:S(2)}, u32[]{:S(2)}) %collective-permute-start.13) | collective-permute-done | bytes 102432 | tf_op jit(solution)/shard_map/ppermute | solution.py:799
  149.9 1.7 collective-permute-done.11
  151.6 3.7 %collective-permute-done.12 = bf16[200,256]{1,0:T(8,128)(2,1)S(1)} collective-permute-done((bf16[200,256]{1,0:T(8,128)(2,1)S(1)}, bf16[200,256]{1,0:T(8,128)(2,1)S(1)}, u32[]{:S(2)}, u32[]{:S(2)}) %collective-permute-start.12) | collective-permute-done | bytes 102432 | tf_op jit(solution)/shard_map/ppermute | solution.py:799
  156.2 1.5 collective-permute-start.17
  157.7 3.6 %collective-permute-done.14 = bf16[400,256]{1,0:T(8,128)(2,1)S(1)} collective-permute-done((bf16[400,256]{1,0:T(8,128)(2,1)S(1)}, bf16[400,256]{1,0:T(8,128)(2,1)S(1)}, u32[]{:S(2)}, u32[]{:S(2)}) %collective-permute-start.14) | collective-permute-done | bytes 204832 | tf_op jit(solution)/shard_map/ppermute | solution.py:780
  162.7 2.0 %collective-permute-start.18 = (bf16[800,256]{1,0:T(8,128)(2,1)S(1)}, bf16[800,256]{1,0:T(8,128)(2,1)S(1)}, u32[]{:S(2)}, u32[]{:S(2)}) collective-permute-start(bf16[800,256]{1,0:T(8,128)(2,1)S(1)} %pad_maximum_fusion.3), channel_id=1, source_target_pairs={{0,4},{2,6},{4,0},{6,2},{8,12},{10,14},{12,8},{14,10},{16,20},{18,... | collective-permute-start | bytes 1228808 | tf_op jit(solution)/shard_map/ppermute | solution.py:780
  164.7 6.1 %collective-permute-done.15 = bf16[800,256]{1,0:T(8,128)(2,1)S(1)} collective-permute-done((bf16[800,256]{1,0:T(8,128)(2,1)S(1)}, bf16[800,256]{1,0:T(8,128)(2,1)S(1)}, u32[]{:S(2)}, u32[]{:S(2)}) %collective-permute-start.15) | collective-permute-done | bytes 409632 | tf_op jit(solution)/shard_map/ppermute | solution.py:780
  171.5 1.7 collective-permute-done.16.refs_1_
  174.4 4.2 %unpack.1 = (f32[2,256,256]{2,1,0:T(8,128)}, f32[2,256]{1,0:T(2,128)}, f32[2,256,256]{2,1,0:T(8,128)}, f32[2,256,256]{2,1,0:T(8,128)}, f32[2,256]{1,0:T(2,128)},...) custom-call(bf16[1600,256]{1,0:T(8,128)(2,1)S(1)} %pad_maximum_fusio, ...), custom_call_target="tpu_custom_call" | custom-call | tf_op jit(solution)/shard_map/unpack/pallas_call | solution.py:759
  (50 shorter events, 11.3 us)
Async XLA Ops:
  3.0 23.3 %copy-start.6 = (bf16[4,1,1,10,256]{4,0,3,2,1:T(4,128)(2,1)S(1)}, bf16[4,1,1,10,256]{4,0,3,2,1:T(4,128)(2,1)}, u32[]{:S(2)}) copy-start(bf16[4,1,1,10,256]{4,0,3,2,1:T(4,128)(2,1)} %param.21) | copy-start | bytes 61444
  23.9 3.4 %collective-permute-start = (bf16[4,16,256]{2,1,0:T(8,128)(2,1)}, bf16[4,16,256]{2,1,0:T(8,128)(2,1)S(1)}, u32[]{:S(2)}, u32[]{:S(2)}) collective-permute-start(bf16[4,16,256]{2,1,0:T(8,128)(2,1)} %get-tuple-element.62), channel_id=1, source_target_pairs={{0,2},{2,4},{4,6},{6,8},{8,10},{10,12},{12,14},{14,16},{16,18},{18... | collective-permute-start | bytes 98312 | tf_op jit(solution)/shard_map/ppermute | solution.py:775
  27.3 0.6 copy-start.5
  68.6 39.5 %collective-permute-start.4 = (bf16[1600,256]{1,0:T(8,128)(2,1)}, bf16[1600,256]{1,0:T(8,128)(2,1)S(1)}, u32[]{:S(2)}, u32[]{:S(2)}) collective-permute-start(bf16[1600,256]{1,0:T(8,128)(2,1)} %get-tuple-element.85), channel_id=1, source_target_pairs={{0,2},{2,0},{4,6},{6,4},{8,10},{10,8},{12,14},{14,12},{16,18},{18,... | collective-permute-start | bytes 2457608 | tf_op jit(solution)/shard_map/ppermute | solution.py:780
  71.5 3.3 %collective-permute-start.1 = (bf16[4,16,256]{2,1,0:T(8,128)(2,1)}, bf16[4,16,256]{2,1,0:T(8,128)(2,1)S(1)}, u32[]{:S(2)}, u32[]{:S(2)}) collective-permute-start(bf16[4,16,256]{2,1,0:T(8,128)(2,1)} %get-tuple-element.65), channel_id=1, source_target_pairs={{2,0},{4,2},{6,4},{8,6},{10,8},{12,10},{14,12},{16,14},{18,16},{20... | collective-permute-start | bytes 98312 | tf_op jit(solution)/shard_map/ppermute | solution.py:775
  74.8 0.6 copy-start.4
  75.4 32.6 %copy-start.2 = (bf16[1600,256]{1,0:T(8,128)(2,1)S(1)}, bf16[1600,256]{1,0:T(8,128)(2,1)}, u32[]{:S(2)}) copy-start(bf16[1600,256]{1,0:T(8,128)(2,1)} %get-tuple-element.84) | copy-start | bytes 2457604
  105.3 6.1 %collective-permute-start.2 = (bf16[1600,256]{1,0:T(8,128)(2,1)}, bf16[1600,256]{1,0:T(8,128)(2,1)S(1)}, u32[]{:S(2)}, u32[]{:S(2)}) collective-permute-start(bf16[1600,256]{1,0:T(8,128)(2,1)} %get-tuple-element.83), channel_id=1, source_target_pairs={{0,2},{2,0},{4,6},{6,4},{8,10},{10,8},{12,14},{14,12},{16,18},{18,... | collective-permute-start | bytes 2457608 | tf_op jit(solution)/shard_map/ppermute | solution.py:780
  108.0 3.3 %copy-start.3 = (bf16[1600,256]{1,0:T(8,128)(2,1)S(1)}, bf16[1600,256]{1,0:T(8,128)(2,1)}, u32[]{:S(2)}) copy-start(bf16[1600,256]{1,0:T(8,128)(2,1)} %get-tuple-element.82) | copy-start | bytes 2457604
  108.3 12.7 %collective-permute-start.5 = (bf16[800,256]{1,0:T(8,128)(2,1)S(1)}, bf16[800,256]{1,0:T(8,128)(2,1)S(1)}, u32[]{:S(2)}, u32[]{:S(2)}) collective-permute-start(bf16[800,256]{1,0:T(8,128)(2,1)S(1)} %slice.43), channel_id=1, source_target_pairs={{0,4},{2,6},{4,0},{6,2},{8,12},{10,14},{12,8},{14,10},{16,20},{18,... | collective-permute-start | bytes 1228808 | tf_op jit(solution)/shard_map/ppermute | solution.py:780
  111.3 1.8 %copy-start = (bf16[4,522,256]{2,1,0:T(8,128)(2,1)S(1)}, bf16[4,522,256]{2,1,0:T(8,128)(2,1)}, u32[]{:S(2)}) copy-start(bf16[4,522,256]{2,1,0:T(8,128)(2,1)} %get-tuple-element.63) | copy-start | bytes 3207172
  111.6 3.1 %copy-start.1 = (bf16[4,522,256]{2,1,0:T(8,128)(2,1)S(1)}, bf16[4,522,256]{2,1,0:T(8,128)(2,1)}, u32[]{:S(2)}) copy-start(bf16[4,522,256]{2,1,0:T(8,128)(2,1)} %get-tuple-element.81) | copy-start | bytes 3207172
  111.6 11.2 %collective-permute-start.3 = (bf16[800,256]{1,0:T(8,128)(2,1)S(1)}, bf16[800,256]{1,0:T(8,128)(2,1)S(1)}, u32[]{:S(2)}, u32[]{:S(2)}) collective-permute-start(bf16[800,256]{1,0:T(8,128)(2,1)S(1)} %slice.41), channel_id=1, source_target_pairs={{0,1},{1,0},{2,3},{3,2},{4,5},{5,4},{6,7},{7,6},{8,9},{9,8},{10,11... | collective-permute-start | bytes 1228808 | tf_op jit(solution)/shard_map/ppermute | solution.py:780
  122.9 7.3 %collective-permute-start.6 = (bf16[400,256]{1,0:T(8,128)(2,1)S(1)}, bf16[400,256]{1,0:T(8,128)(2,1)S(1)}, u32[]{:S(2)}, u32[]{:S(2)}) collective-permute-start(bf16[400,256]{1,0:T(8,128)(2,1)S(1)} %slice.35), channel_id=1, source_target_pairs={{0,4},{2,6},{4,0},{6,2},{8,12},{10,14},{12,8},{14,10},{16,20},{18,... | collective-permute-start | bytes 614408 | tf_op jit(solution)/shard_map/ppermute | solution.py:780
  125.5 6.3 %collective-permute-start.7 = (bf16[400,256]{1,0:T(8,128)(2,1)S(1)}, bf16[400,256]{1,0:T(8,128)(2,1)S(1)}, u32[]{:S(2)}, u32[]{:S(2)}) collective-permute-start(bf16[400,256]{1,0:T(8,128)(2,1)S(1)} %slice.37), channel_id=1, source_target_pairs={{0,1},{1,0},{2,3},{3,2},{4,5},{5,4},{6,7},{7,6},{8,9},{9,8},{10,11... | collective-permute-start | bytes 614408 | tf_op jit(solution)/shard_map/ppermute | solution.py:780
  132.6 7.6 %collective-permute-start.10 = (bf16[200,256]{1,0:T(8,128)(2,1)S(1)}, bf16[200,256]{1,0:T(8,128)(2,1)S(1)}, u32[]{:S(2)}, u32[]{:S(2)}) collective-permute-start(bf16[200,256]{1,0:T(8,128)(2,1)S(1)} %get-tuple-element.109), channel_id=1, source_target_pairs={{0,24},{2,26},{4,28},{6,30},{8,16},{10,18},{12,20},{14,22},{16,8},... | collective-permute-start | bytes 307208 | tf_op jit(solution)/shard_map/ppermute | solution.py:799
  135.1 8.3 %collective-permute-start.9 = (bf16[200,256]{1,0:T(8,128)(2,1)S(1)}, bf16[200,256]{1,0:T(8,128)(2,1)S(1)}, u32[]{:S(2)}, u32[]{:S(2)}) collective-permute-start(bf16[200,256]{1,0:T(8,128)(2,1)S(1)} %get-tuple-element.108), channel_id=1, source_target_pairs={{0,16},{2,18},{4,20},{6,22},{8,24},{10,26},{12,28},{14,30},{16,0},... | collective-permute-start | bytes 307208 | tf_op jit(solution)/shard_map/ppermute | solution.py:799
  135.8 7.7 %collective-permute-start.8 = (bf16[200,256]{1,0:T(8,128)(2,1)S(1)}, bf16[200,256]{1,0:T(8,128)(2,1)S(1)}, u32[]{:S(2)}, u32[]{:S(2)}) collective-permute-start(bf16[200,256]{1,0:T(8,128)(2,1)S(1)} %get-tuple-element.107), channel_id=1, source_target_pairs={{0,8},{2,10},{4,12},{6,14},{8,0},{10,2},{12,4},{14,6},{16,24},{18,... | collective-permute-start | bytes 307208 | tf_op jit(solution)/shard_map/ppermute | solution.py:799
  143.7 6.2 %collective-permute-start.13 = (bf16[200,256]{1,0:T(8,128)(2,1)S(1)}, bf16[200,256]{1,0:T(8,128)(2,1)S(1)}, u32[]{:S(2)}, u32[]{:S(2)}) collective-permute-start(bf16[200,256]{1,0:T(8,128)(2,1)S(1)} %add_convert_fusion.6), channel_id=1, source_target_pairs={{0,8},{2,10},{4,12},{6,14},{8,0},{10,2},{12,4},{14,6},{16,24},{18,... | collective-permute-start | bytes 307208 | tf_op jit(solution)/shard_map/ppermute | solution.py:799
  143.8 7.8 %collective-permute-start.11 = (bf16[200,256]{1,0:T(8,128)(2,1)S(1)}, bf16[200,256]{1,0:T(8,128)(2,1)S(1)}, u32[]{:S(2)}, u32[]{:S(2)}) collective-permute-start(bf16[200,256]{1,0:T(8,128)(2,1)S(1)} %add_convert_fusion.6), channel_id=1, source_target_pairs={{0,24},{2,26},{4,28},{6,30},{8,16},{10,18},{12,20},{14,22},{16,8},... | collective-permute-start | bytes 307208 | tf_op jit(solution)/shard_map/ppermute | solution.py:799
  146.3 8.9 %collective-permute-start.12 = (bf16[200,256]{1,0:T(8,128)(2,1)S(1)}, bf16[200,256]{1,0:T(8,128)(2,1)S(1)}, u32[]{:S(2)}, u32[]{:S(2)}) collective-permute-start(bf16[200,256]{1,0:T(8,128)(2,1)S(1)} %add_convert_fusion.6), channel_id=1, source_target_pairs={{0,16},{2,18},{4,20},{6,22},{8,24},{10,26},{12,28},{14,30},{16,0},... | collective-permute-start | bytes 307208 | tf_op jit(solution)/shard_map/ppermute | solution.py:799
  155.5 5.8 %collective-permute-start.14 = (bf16[400,256]{1,0:T(8,128)(2,1)S(1)}, bf16[400,256]{1,0:T(8,128)(2,1)S(1)}, u32[]{:S(2)}, u32[]{:S(2)}) collective-permute-start(bf16[400,256]{1,0:T(8,128)(2,1)S(1)} %get-tuple-element.106), channel_id=1, source_target_pairs={{0,4},{2,6},{4,0},{6,2},{8,12},{10,14},{12,8},{14,10},{16,20},{18,... | collective-permute-start | bytes 614408 | tf_op jit(solution)/shard_map/ppermute | solution.py:780
  156.2 6.4 %collective-permute-start.17 = (bf16[400,256]{1,0:T(8,128)(2,1)S(1)}, bf16[400,256]{1,0:T(8,128)(2,1)S(1)}, u32[]{:S(2)}, u32[]{:S(2)}) collective-permute-start(bf16[400,256]{1,0:T(8,128)(2,1)S(1)} %get-tuple-element.105), channel_id=1, source_target_pairs={{0,1},{1,0},{2,3},{3,2},{4,5},{5,4},{6,7},{7,6},{8,9},{9,8},{10,11... | collective-permute-start | bytes 614408 | tf_op jit(solution)/shard_map/ppermute | solution.py:780
  161.3 9.4 %collective-permute-start.15 = (bf16[800,256]{1,0:T(8,128)(2,1)S(1)}, bf16[800,256]{1,0:T(8,128)(2,1)S(1)}, u32[]{:S(2)}, u32[]{:S(2)}) collective-permute-start(bf16[800,256]{1,0:T(8,128)(2,1)S(1)} %pad_maximum_fusion.2), channel_id=1, source_target_pairs={{0,1},{1,0},{2,3},{3,2},{4,5},{5,4},{6,7},{7,6},{8,9},{9,8},{10,11... | collective-permute-start | bytes 1228808 | tf_op jit(solution)/shard_map/ppermute | solution.py:780
  162.7 8.5 %collective-permute-start.18 = (bf16[800,256]{1,0:T(8,128)(2,1)S(1)}, bf16[800,256]{1,0:T(8,128)(2,1)S(1)}, u32[]{:S(2)}, u32[]{:S(2)}) collective-permute-start(bf16[800,256]{1,0:T(8,128)(2,1)S(1)} %pad_maximum_fusion.3), channel_id=1, source_target_pairs={{0,4},{2,6},{4,0},{6,2},{8,12},{10,14},{12,8},{14,10},{16,20},{18,... | collective-permute-start | bytes 1228808 | tf_op jit(solution)/shard_map/ppermute | solution.py:780
  170.8 2.4 %collective-permute-start.16 = (bf16[1600,256]{1,0:T(8,128)(2,1)S(1)}, bf16[1600,256]{1,0:T(8,128)(2,1)S(1)}, u32[]{:S(2)}, u32[]{:S(2)}) collective-permute-start(bf16[1600,256]{1,0:T(8,128)(2,1)S(1)} %pad_maximum_fusion.refs_0_), channel_id=1, source_target_pairs={{0,2},{2,0},{4,6},{6,4},{8,10},{10,8},{12,14},{14,12},{16,18},{18,... | collective-permute-start | bytes 2457608 | tf_op jit(solution)/shard_map/ppermute | solution.py:780
  171.3 3.1 %collective-permute-start.19 = (bf16[1600,256]{1,0:T(8,128)(2,1)S(1)}, bf16[1600,256]{1,0:T(8,128)(2,1)S(1)}, u32[]{:S(2)}, u32[]{:S(2)}) collective-permute-start(bf16[1600,256]{1,0:T(8,128)(2,1)S(1)} %pad_maximum_fusion.1.refs_2_), channel_id=1, source_target_pairs={{0,2},{2,0},{4,6},{6,4},{8,10},{10,8},{12,14},{14,12},{16,18},{18,... | collective-permute-start | bytes 2457608 | tf_op jit(solution)/shard_map/ppermute | solution.py:780

commit v4 on v3

--- a/solution.py
+++ b/solution.py
@@ -132,7 +132,7 @@
     return top, jnp.exp(bottom - peak).astype(BF16)
 
 
-def weave(*tasks):
+def woven(*tasks):
     tasks = [[task, 0.0, total] for task, total in tasks]
     while tasks:
         task = min(tasks, key=lambda t: t[1] / t[2])
@@ -141,6 +141,16 @@
             tasks.remove(task)
         else:
             task[1] += length
+            yield length
+
+
+def weave(*tasks):
+    for _ in woven(*tasks):
+        pass
+
+
+def at(w, layer):
+    return layer if w.w_query.shape[0] > 1 else 0
 
 
 def layer_forward(x, layer, w, st, rows, result):
@@ -152,11 +162,11 @@
         return ref[layer : layer + 1, :]
 
     st.x[...] = x
-    q = ((dot(x, w.w_query[0]) + row(w.b_query)) * 0.125).astype(BF16)
+    q = ((dot(x, w.w_query[at(w, layer)]) + row(w.b_query)) * 0.125).astype(BF16)
     yield 150
-    k = dot(x, w.w_key[0]).astype(BF16)
+    k = dot(x, w.w_key[at(w, layer)]).astype(BF16)
     yield 150
-    v = (dot(x, w.w_value[0]) + row(w.b_value)).astype(BF16)
+    v = (dot(x, w.w_value[at(w, layer)]) + row(w.b_value)).astype(BF16)
     st.query[...] = q
     st.key[...] = k
     st.value[...] = v
@@ -164,34 +174,43 @@
     q_t = q[:main].T
     v_t = v[:main].T
     live_rest = lax.broadcasted_iota(jnp.int32, (TILE, 1), 0) < rows - main
-    top, bottom = yield from weigh_keys(dot_nt(k, spread_heads(q[main:], width)), live_rest)
-    p_rest = jnp.concatenate([top, bottom], axis=0)
-    p_rest = (p_rest.astype(F32) * (1.0 / column_sum(p_rest))).astype(BF16)
-    st.prob_rest[...] = p_rest
-    yield 50
-    context_rest = fold_heads(dot_tn(p_rest, v), width).astype(BF16)
+    def last_rows(out):
+        top, bottom = yield from weigh_keys(dot_nt(k, spread_heads(q[main:], width)), live_rest)
+        p_rest = jnp.concatenate([top, bottom], axis=0)
+        p_rest = (p_rest.astype(F32) * (1.0 / column_sum(p_rest))).astype(BF16)
+        st.prob_rest[...] = p_rest
+        yield 50
+        out.append(fold_heads(dot_tn(p_rest, v), width).astype(BF16))
+        yield 50
+
     ones = jnp.ones((TILE, main), BF16)
     scores, weights, parts, bottoms, scales = {}, {}, [], [], []
-    for h in range(-1, HEADS + 1):
-        if h + 1 < HEADS:
-            pair = slice(2 * width * ((h + 1) // 2), 2 * width * ((h + 1) // 2 + 1))
-            scores[h + 1] = dot(own_half(k[:, pair], h + 1, width), q_t[pair, :])
-            yield 80
-        if h > 0:
-            top, bottom = weights.pop(h - 1)
-            part = dot(jnp.concatenate([v_t[(h - 1) * width : h * width, :], ones], axis=0), top)
-            parts.append(part[:width])
-            bottoms.append(bottom)
-            scale = 1.0 / (part[width : width + 1] + column_sum(bottom))
-            st.scale[h - 1 : h, :] = scale
-            scales.append(jnp.broadcast_to(scale, (width, main)))
-            yield 80
-        if 0 <= h < HEADS:
-            top, bottom = yield from weigh_keys(scores.pop(h), live_rest)
-            st.prob[h, :main, :] = top
-            st.prob[h, main:, :] = bottom
-            weights[h] = top, bottom
-            yield 60
+
+    def first_rows():
+        for h in range(-1, HEADS + 1):
+            if h + 1 < HEADS:
+                pair = slice(2 * width * ((h + 1) // 2), 2 * width * ((h + 1) // 2 + 1))
+                scores[h + 1] = dot(own_half(k[:, pair], h + 1, width), q_t[pair, :])
+                yield 80
+            if h > 0:
+                top, bottom = weights.pop(h - 1)
+                part = dot(jnp.concatenate([v_t[(h - 1) * width : h * width, :], ones], axis=0), top)
+                parts.append(part[:width])
+                bottoms.append(bottom)
+                scale = 1.0 / (part[width : width + 1] + column_sum(bottom))
+                st.scale[h - 1 : h, :] = scale
+                scales.append(jnp.broadcast_to(scale, (width, main)))
+                yield 80
+            if 0 <= h < HEADS:
+                top, bottom = yield from weigh_keys(scores.pop(h), live_rest)
+                st.prob[h, :main, :] = top
+                st.prob[h, main:, :] = bottom
+                weights[h] = top, bottom
+                yield 60
+
+    at_last = []
+    yield from woven((last_rows(at_last), 450), (first_rows(), 2600))
+    (context_rest,) = at_last
     context_t = jnp.concatenate(parts, axis=0)
     context_t = context_t + dot_tn(spread_heads(v[main:], width), jnp.concatenate(bottoms, axis=0))
     context_t = context_t * jnp.concatenate(scales, axis=0)
@@ -199,7 +218,7 @@
     context = jnp.concatenate([context_t.astype(BF16).T, context_rest], axis=0)
     st.context[...] = context
     yield 200
-    normed_attn, inverse_attn = normalize(x.astype(F32) + dot(context, w.w_out[0]) + row(w.b_out))
+    normed_attn, inverse_attn = normalize(x.astype(F32) + dot(context, w.w_out[at(w, layer)]) + row(w.b_out))
     st.normed_attn[...] = normed_attn
     middle = normed_attn * row(w.gain_attn) + row(w.shift_attn)
     middle_low = middle.astype(BF16)
@@ -210,7 +229,7 @@
 
     def upward(c):
         part = slice(c * features, (c + 1) * features)
-        return dot(middle_low, w.w_up[0, :, part]) + w.b_up[layer : layer + 1, part]
+        return dot(middle_low, w.w_up[at(w, layer), :, part]) + w.b_up[layer : layer + 1, part]
 
     ahead = upward(0)
     for c in range(chunks):
@@ -224,7 +243,7 @@
         slope = phi + u * (jnp.exp2(u * u * BELL) * DENSITY)
         st.slope[:, part] = slope.astype(BF16)
         yield 220
-        total = total + dot(active, w.w_down[0, part, :])
+        total = total + dot(active, w.w_down[at(w, layer), part, :])
         yield 80
     normed_ffn, inverse_ffn = normalize(total)
     st.normed_ffn[...] = normed_ffn
@@ -234,7 +253,7 @@
     yield 400
 
 
-def layer_backward(grad_out, layer, w, st, g, rest, grad_up_ref, grad_s_ref, step, result):
+def layer_backward(grad_out, layer, w, st, g, rest, grad_up_ref, grad_s_ref, step, result, fill=False):
     full, features = st.x.shape
     main = full - TILE
     width = features // HEADS
@@ -257,69 +276,102 @@
     yield 500
     for c in range(w.w_up.shape[2] // features):
         part = slice(c * features, (c + 1) * features)
-        grad_up = dot_nt(grad_branch, w.w_down[0, part, :]) * st.slope[:, part].astype(F32)
+        grad_up = dot_nt(grad_branch, w.w_down[at(w, layer), part, :]) * st.slope[:, part].astype(F32)
         grad_up = grad_up.astype(BF16)
         yield 150
         grad_up_ref[:, part] = grad_up
         g.b_up[:, part] += column_sum(grad_up)
-        grad_middle = grad_middle + dot_nt(grad_up, w.w_up[0, :, part])
+        grad_middle = grad_middle + dot_nt(grad_up, w.w_up[at(w, layer), :, part])
         yield 150
-    add(g.w_down, dot_tn(st.active[:main, :], grad_branch[:main]))
-    yield 400
-    add(g.w_up, dot_tn(grad_up_ref[:main, :], st.middle[:main, :]))
     rest.middle[place, :] = st.middle[main:, :]
     rest.up[place, :] = grad_up_ref[main:, :]
     rest.active[place, :] = st.active[main:, :]
-    yield 400
+    rest.context[place, :] = st.context[main:, :]
+
+    def grad_ffn(cuts):
+        for cut in range(cuts):
+            part = slice(cut * units // cuts, (cut + 1) * units // cuts)
+            g.w_down[part, :] += dot_tn(st.active[:main, part], grad_branch[:main])
+            yield 360 // cuts
+            g.w_up[part, :] += dot_tn(grad_up_ref[:main, part], st.middle[:main, :])
+            yield 360 // cuts
+
+    units = w.w_up.shape[2]
+    filler = grad_ffn(2 if fill else 1)
+    if not fill:
+        yield from filler
     normed_attn = st.normed_attn[...]
+    yield next(filler, 0)
     add(g.gain_attn, column_sum(grad_middle * normed_attn))
     add(g.shift_attn, column_sum(grad_middle))
-    grad_resid = norm_back(grad_middle * row(w.gain_attn), normed_attn, st.inverse[:, 0:1])
+    if fill:
+        yield 100
+        yield next(filler, 0)
+    grad_normed = grad_middle * row(w.gain_attn)
+    mean_grad, mean_both = mean(grad_normed), mean(grad_normed * normed_attn)
+    if fill:
+        yield 150
+        yield next(filler, 0)
+    grad_resid = st.inverse[:, 0:1] * (grad_normed - mean_grad - normed_attn * mean_both)
     grad_attn = grad_resid.astype(BF16)
+    if fill:
+        yield 150
+    yield from filler
     rest.attn[place, :] = grad_attn[main:]
-    rest.context[place, :] = st.context[main:, :]
     add(g.b_out, column_sum(grad_attn))
-    yield 500
+    yield 50
     add(g.w_out, dot_tn(st.context[:main, :], grad_attn[:main]))
     scale = jnp.concatenate([jnp.broadcast_to(st.scale[h : h + 1, :], (width, main)) for h in range(HEADS)], axis=0)
-    grad_context_t = (dot_nt(w.w_out[0], grad_attn[:main]) * scale).astype(BF16)
+    grad_context_t = (dot_nt(w.w_out[at(w, layer)], grad_attn[:main]) * scale).astype(BF16)
     grad_context = grad_context_t.T
     product = grad_context_t.astype(F32) * st.context_t[...]
     q, k, v = st.query[...], st.key[...], st.value[...]
     k_t = k[:main].T
     yield 400
-    grad_spread = spread_heads(dot_nt(grad_attn[main:], w.w_out[0]).astype(BF16), width)
-    p_rest = st.prob_rest[...]
-    p_rest_wide = p_rest.astype(F32)
-    grad_p = dot_nt(v, grad_spread)
-    centre = jnp.sum(p_rest_wide * grad_p, axis=0, keepdims=True) / jnp.sum(p_rest_wide, axis=0, keepdims=True)
-    grad_s = p_rest_wide * (grad_p - centre)
-    grad_s = grad_s.astype(BF16)
-    grad_v = dot(p_rest, grad_spread)
-    grad_k = dot(grad_s, spread_heads(q[main:], width))
-    grad_q_rest = fold_heads(dot_tn(grad_s, k), width).astype(BF16)
-    yield 400
+    def last_rows(out):
+        grad_spread = spread_heads(dot_nt(grad_attn[main:], w.w_out[at(w, layer)]).astype(BF16), width)
+        p_rest = st.prob_rest[...]
+        p_rest_wide = p_rest.astype(F32)
+        yield 60
+        grad_p = dot_nt(v, grad_spread)
+        out.append(dot(p_rest, grad_spread))
+        yield 100
+        centre = jnp.sum(p_rest_wide * grad_p, axis=0, keepdims=True) / jnp.sum(p_rest_wide, axis=0, keepdims=True)
+        yield 100
+        grad_s = (p_rest_wide * (grad_p - centre)).astype(BF16)
+        yield 60
+        out.append(dot(grad_s, spread_heads(q[main:], width)))
+        yield 60
+        out.append(fold_heads(dot_tn(grad_s, k), width).astype(BF16))
+        yield 60
+
     left = lax.broadcasted_iota(jnp.int32, (full, 2 * width), 1) < width
     q_parts, k_parts, v_parts, bottoms = [], [], [], []
-    for h in range(0, HEADS, 2):
-        pair = slice(width * h, width * (h + 2))
-        for i in (h, h + 1):
-            own = slice(i * width, (i + 1) * width)
-            grad_p = dot(own_half(v[:, pair], i, width), grad_context_t[pair, :])
-            yield 130
-            grad_s = st.prob[i].astype(F32) * (grad_p - jnp.sum(product[own, :], axis=0, keepdims=True))
-            grad_s = grad_s.astype(BF16)
-            grad_s_ref[i] = grad_s
-            yield 140
-            q_parts.append(dot(k_t[own, :], grad_s[:main]))
-            bottoms.append(grad_s[main:])
-            yield 130
-        both = dot(st.prob[h : h + 2].reshape(2 * full, main), grad_context[:, pair])
-        v_parts.append(jnp.where(left, both[:full], both[full:]))
-        yield 350
-        both = dot(grad_s_ref[h : h + 2].reshape(2 * full, main), q[:main, pair])
-        k_parts.append(jnp.where(left, both[:full], both[full:]))
-        yield 350
+
+    def first_rows():
+        for h in range(0, HEADS, 2):
+            pair = slice(width * h, width * (h + 2))
+            for i in (h, h + 1):
+                own = slice(i * width, (i + 1) * width)
+                grad_p = dot(own_half(v[:, pair], i, width), grad_context_t[pair, :])
+                yield 130
+                grad_s = st.prob[i].astype(F32) * (grad_p - jnp.sum(product[own, :], axis=0, keepdims=True))
+                grad_s = grad_s.astype(BF16)
+                grad_s_ref[i] = grad_s
+                yield 140
+                q_parts.append(dot(k_t[own, :], grad_s[:main]))
+                bottoms.append(grad_s[main:])
+                yield 130
+            both = dot(st.prob[h : h + 2].reshape(2 * full, main), grad_context[:, pair])
+            v_parts.append(jnp.where(left, both[:full], both[full:]))
+            yield 350
+            both = dot(grad_s_ref[h : h + 2].reshape(2 * full, main), q[:main, pair])
+            k_parts.append(jnp.where(left, both[:full], both[full:]))
+            yield 350
+
+    at_last = []
+    yield from woven((last_rows(at_last), 500), (first_rows(), 3000))
+    grad_v, grad_k, grad_q_rest = at_last
     grad_v = (grad_v + jnp.concatenate(v_parts, axis=1)).astype(BF16)
     grad_k = (grad_k + jnp.concatenate(k_parts, axis=1)).astype(BF16)
     grad_q_t = jnp.concatenate(q_parts, axis=0)
@@ -339,9 +391,9 @@
     yield 400
     result.append(
         grad_resid
-        + dot_nt(grad_q, w.w_query[0])
-        + dot_nt(grad_k, w.w_key[0])
-        + dot_nt(grad_v, w.w_value[0])
+        + dot_nt(grad_q, w.w_query[at(w, layer)])
+        + dot_nt(grad_k, w.w_key[at(w, layer)])
+        + dot_nt(grad_v, w.w_value[at(w, layer)])
     )
     yield 300
 
@@ -363,7 +415,7 @@
         g.w_down[part, :] += dot_tn(rest.active[:, part], rest.branch[...])
 
 
-FORWARD, BACKWARD = 6000, 8650
+FORWARD, BACKWARD = 7600, 8650
 
 
 def squares(g):
@@ -461,10 +513,12 @@
     return g, Rest(*refs[:count]), *refs[count:]
 
 
-def weight_specs(weights, layer):
+def weight_specs(weights, layer=None):
     specs = []
     for weight in weights:
-        if weight.ndim == 3:
+        if layer is None:
+            specs.append(whole())
+        elif weight.ndim == 3:
             specs.append(pl.BlockSpec((1,) + weight.shape[1:], lambda m: (layer, 0, 0)))
         else:
             specs.append(pl.BlockSpec(weight.shape, lambda m: (0, 0)))
@@ -491,11 +545,12 @@
     return pl.BlockSpec(tuple(shape), lambda m: (0,) * rank)
 
 
+def whole():
+    return pl.BlockSpec(memory_space=pltpu.VMEM)
+
+
 def smem():
     return pl.BlockSpec(memory_space=pltpu.SMEM)
-
-
-PARAMS = pltpu.CompilerParams(vmem_limit_bytes=60 * 2**20)
 
 
 def lower_forward_kernel(x_ref, *refs):
@@ -526,7 +581,7 @@
         out_specs=[by_micro(o.shape) for o in outs],
         out_shape=outs,
         scratch_shapes=[pltpu.VMEM((full, features), BF16)],
-        compiler_params=PARAMS,
+        compiler_params=pltpu.CompilerParams(vmem_limit_bytes=60 * 2**20),
         name="lower_forward",
     )(hidden, *weights)
     return out, sent, Stash(*stash)
@@ -544,14 +599,14 @@
                 ref[pl.ds(pl.multiple_of(i * STRIP, STRIP), STRIP), :] = jnp.zeros((STRIP, features), F32)
 
 
-def upper_forward(rows, lead, arrived_ref, cot_ref, target_ref, slot_ref, count, x_ref, out_ref, grad_out, w, st):
+def upper_forward(rows, lead, arrived, cot_ref, target_ref, slot_ref, count, x_ref, out_ref, grad_out, w, st):
     full, features = x_ref.shape[1:]
     memory = cot_ref.shape[1]
     main = full - TILE
     x = x_ref[0]
     is_read = lax.broadcasted_iota(jnp.int32, (TILE, features), 0) < memory
     moved = jnp.logical_and(is_read, jnp.logical_not(lead))
-    x = jnp.concatenate([jnp.where(moved, arrived_ref[0], x[:TILE]), x[TILE:]], axis=0)
+    x = jnp.concatenate([jnp.where(moved, arrived, x[:TILE]), x[TILE:]], axis=0)
     result = []
     yield from layer_forward(x, 1, w, st, rows, result)
     y = result[0]
@@ -568,9 +623,9 @@
     yield 300
 
 
-def upper_backward(lead, memory, grad_out, grad_ref, back_ref, w, st, *refs):
+def upper_backward(lead, memory, grad_out, grad_ref, back_ref, w, st, *refs, fill):
     result = []
-    yield from layer_backward(grad_out[...], 1, w, st, *refs, result)
+    yield from layer_backward(grad_out[...], 1, w, st, *refs, result, fill)
     grad_in = result[0]
     is_read = lax.broadcasted_iota(jnp.int32, (TILE, grad_in.shape[1]), 0) < memory
     moved = jnp.logical_and(is_read, jnp.logical_not(lead))
@@ -595,15 +650,15 @@
         return twice
 
     def forward(slot):
-        count = count_ref[jnp.minimum(step, micro - 1)]
+        now = jnp.minimum(step, micro - 1)
+        count, arrived = count_ref[now], arrived_ref[now]
         return upper_forward(
-            rows, lead, arrived_ref, cot_ref, target_ref, slot_ref, count, x_ref, out_ref, grad_out, w, turn(slot)
+            rows, lead, arrived, cot_ref, target_ref, slot_ref, count, x_ref, out_ref, grad_out, w, turn(slot)
         )
 
-    def backward(slot):
-        return upper_backward(
-            lead, memory, grad_out, grad_ref, back_ref, w, turn(slot), g, rest, grad_up_ref, grad_s_ref, step - 1
-        )
+    def backward(slot, fill):
+        refs = (g, rest, grad_up_ref, grad_s_ref, step - 1)
+        return upper_backward(lead, memory, grad_out, grad_ref, back_ref, w, turn(slot), *refs, fill=fill)
 
     @pl.when(step == 0)
     def _():
@@ -614,11 +669,11 @@
     @pl.when(jnp.logical_and(step > 0, step < micro))
     def _():
         slot = lax.rem(step, 2)
-        weave((forward(slot), FORWARD), (backward(1 - slot), BACKWARD))
+        weave((forward(slot), FORWARD), (backward(1 - slot, True), BACKWARD))
 
     @pl.when(step == micro)
     def _():
-        weave((backward((micro - 1) % 2), BACKWARD))
+        weave((backward((micro - 1) % 2, False), BACKWARD))
         add_rest(g, rest)
         emit(g, keep_ref, send_ref, ordered, place_of(bits))
 
@@ -644,12 +699,12 @@
     return pl.pallas_call(
         functools.partial(upper_kernel, rows, micro, bits),
         grid=(micro + 1,),
-        in_specs=[smem()] + [ahead(a.shape) for a in ins] + weight_specs(weights, 1),
+        in_specs=[smem()] + [whole() if a is arrived else ahead(a.shape) for a in ins] + weight_specs(weights),
         out_specs=[ahead(outs[0].shape), behind(outs[1].shape), behind(outs[2].shape)]
         + [fixed(o.shape) for o in outs[3:]],
         out_shape=outs,
         scratch_shapes=stash + scratch(micro, full, features, units),
-        compiler_params=PARAMS,
+        compiler_params=pltpu.CompilerParams(vmem_limit_bytes=48 * 2**20),
         name="upper_both",
     )(counts, *ins, *weights)
 
@@ -668,7 +723,7 @@
         zero_sums(g)
 
     is_write = lax.broadcasted_iota(jnp.int32, (TILE, features), 0) < memory
-    returned = jnp.where(is_write, back_ref[0].astype(F32), 0.0)
+    returned = jnp.where(is_write, back_ref[step].astype(F32), 0.0)
     grad_out = jnp.concatenate([grad_ref[0, :main, :], grad_ref[0, main:, :] + returned], axis=0)
     result = []
     weave((layer_backward(grad_out, 0, w, st, g, rest, grad_up_ref, grad_s_ref, step, result), 1))
@@ -691,13 +746,13 @@
     return pl.pallas_call(
         functools.partial(lower_backward_kernel, memory, bits),
         grid=(micro,),
-        in_specs=[by_micro(grad.shape), by_micro(back.shape)]
-        + weight_specs(weights, 0)
+        in_specs=[by_micro(grad.shape), whole()]
+        + weight_specs(weights)
         + [by_micro(a.shape) for a in stash],
         out_specs=[by_micro(outs[0].shape)] + [fixed(o.shape) for o in outs[1:]],
         out_shape=outs,
         scratch_shapes=scratch(micro, full, features, units),
-        compiler_params=PARAMS,
+        compiler_params=pltpu.CompilerParams(vmem_limit_bytes=48 * 2**20),
         name="lower_backward",
     )(grad, back, *weights, *stash)
 
@@ -717,8 +772,6 @@
     ]
     for load in loads:
         load.start()
-    for load in loads:
-        load.wait()
     sizes = [features] * 4 + [units, units]
     sizes.append(rows - sum(sizes))
     me = [place_of_layer(layer) for layer in range(2)]
@@ -728,6 +781,13 @@
 
     @pl.loop(0, 2)
     def _(layer):
+        for i in range(2):
+
+            @pl.when(layer == i)
+            def _(i=i):
+                loads[2 * i].wait()
+                loads[2 * i + 1].wait()
+
         mine = jnp.where(layer == 0, me[0], me[1])
         for index, start, which, offset, take in spans(sizes, rows):
             at = pl.multiple_of((which ^ mine) * piece, TILE) + offset

time: 179 us -> 172 us (0.961)
  Pallas kernels: 95.6 us -> 90.1 us
    pallas_call x1, Pallas kernels: 40.6 us -> 38.1 us  [upper_both(): pl.pallas_call(functools.partial(upper_kernel, rows, micro, bits), grid=(...]
    pallas_call x1, Pallas kernels: 29.8 us -> 27.5 us  [lower_backward(): pl.pallas_call(functools.partial(lower_backward_kernel, memory, bits), gr...]
    unnamed x16 -> x46, local copies, waits for them, and re-layouts: 4.22 us -> 2.49 us
  transfers between devices with their start and end apart: 20 -> 20, of which waited for: 16 -> 17; matrix products, arithmetic and copies ran while one was open for 3% -> 2% of each run, Pallas kernels for 17% -> 16%
where the time goes in v4:
time: 172 us
  Pallas kernels  90.1 us (52%)
  waiting for transfers between devices  41.3 us (24%)
  starting transfers between devices  31.4 us (18%)
  local copies, waits for them, and re-layouts  5.66 us (3%)
  other arithmetic  2.17 us (1%)
    pallas_call x1, Pallas kernels, upper_both(): pl.pallas_call(functools.partial(upper_kernel, rows, micro, bits), grid=(...  38.1 us
    pallas_call x1, Pallas kernels, lower_backward(): pl.pallas_call(functools.partial(lower_backward_kernel, memory, bits), gr...  27.5 us
    ppermute x12, waiting for transfers between devices, swap(): lax.ppermute(value, axis, [(i, i ^ step) for i in range(lax.axis_size(axi...  24.4 us
    pallas_call x1, Pallas kernels, lower_forward(): pl.pallas_call(lower_forward_kernel, grid=(micro,), in_specs=[by_micro(hi...  20.2 us
    ppermute x12, starting transfers between devices, swap(): lax.ppermute(value, axis, [(i, i ^ step) for i in range(lax.axis_size(axi...  19.8 us
    ppermute x6, waiting for transfers between devices, across(): lax.ppermute(part, axis, [(i, i ^ k * step) for i in range(lax.axis_size(...  14.1 us
    ppermute x6, starting transfers between devices, across(): lax.ppermute(part, axis, [(i, i ^ k * step) for i in range(lax.axis_size(...  7.98 us
    pallas_call x1, Pallas kernels, unpack(): pl.pallas_call(functools.partial(unpack_kernel, lambda layer: place_of(bi...  4.23 us
  transfers between devices with their start and end apart: 20, of which 17 were waited for; matrix products, arithmetic and copies ran while one was open for 2% of the time, Pallas kernels for 16%

profile of v4, /device:TPU:0, one launch (start us, length us, event | category | flops | bytes accessed | tf_op | source)
XLA Modules:
  0.0 172.0 jit_solution(11866998842118586404)
XLA Ops:
  0.7 2.4 %copy.45 = bf16[4,1,1,522,256]{4,3,0,2,1:T(8,128)(2,1)} copy(bf16[4,1,1,522,256]{4,0,3,2,1:T(4,128)(2,1)} %param.20) | data formatting | bytes 2138112 | tf_op args[0]
  3.2 20.2 %lower_forward.1 = (bf16[4,528,256]{2,1,0:T(8,128)(2,1)}, bf16[4,16,256]{2,1,0:T(8,128)(2,1)}, bf16[4,528,256]{2,1,0:T(8,128)(2,1)}, bf16[4,528,256]{2,1,0:T(8,1...) custom-call(bf16[4,522,256]{2,1,0:T(8,128)(2,1)} %bitcast.25, ...), custom_call_target="tpu_custom_call" | custom-call | tf_op jit(solution)/shard_map/lower_forward/pallas_call | solution.py:577
  23.4 2.4 %collective-permute-start = (bf16[4,16,256]{2,1,0:T(8,128)(2,1)}, bf16[4,16,256]{2,1,0:T(8,128)(2,1)S(1)}, u32[]{:S(2)}, u32[]{:S(2)}) collective-permute-start(bf16[4,16,256]{2,1,0:T(8,128)(2,1)} %get-tuple-element.62), channel_id=1, source_target_pairs={{0,2},{2,4},{4,6},{6,8},{8,10},{10,12},{12,14},{14,16},{16,18},{18... | collective-permute-start | bytes 98312 | tf_op jit(solution)/shard_map/ppermute | solution.py:835
  27.0 38.1 %upper_both.1 = (bf16[4,522,256]{2,1,0:T(8,128)(2,1)S(1)}, f32[4,528,256]{2,1,0:T(8,128)}, bf16[4,16,256]{2,1,0:T(8,128)(2,1)S(1)}, bf16[1600,256]{1,0:T(8,128)(2,1)S(1)}, bf16[1600,256]{1,0:T(8,128)(2,1)S(1)}) custom-call(s32[4]{0:T(128)S(1)} %bitcast.24, bf16[4,528,256]{2,1,0:T(8,128)(2,1)} %get-tuple-element.61.x_ref, ...), custom_call_target="tpu_custom_call" | custom-call | tf_op jit(solution)/shard_map/upper_both/pallas_call | solution.py:699
  65.2 2.9 %collective-permute-start.4 = (bf16[1600,256]{1,0:T(8,128)(2,1)S(1)}, bf16[1600,256]{1,0:T(8,128)(2,1)S(1)}, u32[]{:S(2)}, u32[]{:S(2)}) collective-permute-start(bf16[1600,256]{1,0:T(8,128)(2,1)S(1)} %get-tuple-element.85), channel_id=1, source_target_pairs={{0,2},{2,0},{4,6},{6,4},{8,10},{10,8},{12,14},{14,12},{16,18},{18,... | collective-permute-start | bytes 2457608 | tf_op jit(solution)/shard_map/ppermute | solution.py:840
  69.4 1.8 %collective-permute-done.1.back_ref = bf16[4,16,256]{2,1,0:T(8,128)(2,1)S(1)} collective-permute-done((bf16[4,16,256]{2,1,0:T(8,128)(2,1)S(1)}, bf16[4,16,256]{2,1,0:T(8,128)(2,1)S(1)}, u32[]{:S(2)}, u32[]{:S(2)}) %collective-permute-start.1) | collective-permute-done | bytes 32800 | tf_op jit(solution)/shard_map/ppermute | solution.py:835
  71.2 27.5 %lower_backward.1 = (bf16[4,522,256]{2,1,0:T(8,128)(2,1)}, bf16[1600,256]{1,0:T(8,128)(2,1)S(1)}, bf16[1600,256]{1,0:T(8,128)(2,1)S(1)}) custom-call(f32[4,528,256]{2,1,0:T(8,128)} %get-tuple-element.64.grad_ref, bf16[4,16,256]{2,1,0:T(8,128)(2,1)S(1)} %collective-permute-done.1.back_ref, bf16[2,256,256]{2,1,0:T(8,128)(2,1)S(1)} %copy-done.2, ...), custom_call_target="tpu_custom_call" | custom-call | tf_op jit(solution)/shard_map/lower_backward/pallas_call | solution.py:746
  98.7 2.7 %collective-permute-start.2 = (bf16[1600,256]{1,0:T(8,128)(2,1)S(1)}, bf16[1600,256]{1,0:T(8,128)(2,1)S(1)}, u32[]{:S(2)}, u32[]{:S(2)}) collective-permute-start(bf16[1600,256]{1,0:T(8,128)(2,1)S(1)} %get-tuple-element.83), channel_id=1, source_target_pairs={{0,2},{2,0},{4,6},{6,4},{8,10},{10,8},{12,14},{14,12},{16,18},{18,... | collective-permute-start | bytes 2457608 | tf_op jit(solution)/shard_map/ppermute | solution.py:840
  101.6 3.1 %collective-permute-start.5 = (bf16[800,256]{1,0:T(8,128)(2,1)S(1)}, bf16[800,256]{1,0:T(8,128)(2,1)S(1)}, u32[]{:S(2)}, u32[]{:S(2)}) collective-permute-start(bf16[800,256]{1,0:T(8,128)(2,1)S(1)} %slice.43), channel_id=1, source_target_pairs={{0,4},{2,6},{4,0},{6,2},{8,12},{10,14},{12,8},{14,10},{16,20},{18,... | collective-permute-start | bytes 1228808 | tf_op jit(solution)/shard_map/ppermute | solution.py:840
  105.0 1.6 collective-permute-start.3
  106.6 1.5 copy.47
  108.1 1.5 copy.46
  109.6 4.8 %collective-permute-done.5 = bf16[800,256]{1,0:T(8,128)(2,1)S(1)} collective-permute-done((bf16[800,256]{1,0:T(8,128)(2,1)S(1)}, bf16[800,256]{1,0:T(8,128)(2,1)S(1)}, u32[]{:S(2)}, u32[]{:S(2)}) %collective-permute-start.5) | collective-permute-done | bytes 409632 | tf_op jit(solution)/shard_map/ppermute | solution.py:840
  114.5 1.7 collective-permute-done.3
  116.3 2.3 %collective-permute-start.6 = (bf16[400,256]{1,0:T(8,128)(2,1)S(1)}, bf16[400,256]{1,0:T(8,128)(2,1)S(1)}, u32[]{:S(2)}, u32[]{:S(2)}) collective-permute-start(bf16[400,256]{1,0:T(8,128)(2,1)S(1)} %slice.35), channel_id=1, source_target_pairs={{0,4},{2,6},{4,0},{6,2},{8,12},{10,14},{12,8},{14,10},{16,20},{18,... | collective-permute-start | bytes 614408 | tf_op jit(solution)/shard_map/ppermute | solution.py:840
  118.6 1.6 collective-permute-start.7
  120.2 3.2 %collective-permute-done.6 = bf16[400,256]{1,0:T(8,128)(2,1)S(1)} collective-permute-done((bf16[400,256]{1,0:T(8,128)(2,1)S(1)}, bf16[400,256]{1,0:T(8,128)(2,1)S(1)}, u32[]{:S(2)}, u32[]{:S(2)}) %collective-permute-start.6) | collective-permute-done | bytes 204832 | tf_op jit(solution)/shard_map/ppermute | solution.py:840
  123.5 1.5 collective-permute-done.7
  125.8 2.5 %collective-permute-start.10 = (bf16[200,256]{1,0:T(8,128)(2,1)S(1)}, bf16[200,256]{1,0:T(8,128)(2,1)S(1)}, u32[]{:S(2)}, u32[]{:S(2)}) collective-permute-start(bf16[200,256]{1,0:T(8,128)(2,1)S(1)} %get-tuple-element.109), channel_id=1, source_target_pairs={{0,24},{2,26},{4,28},{6,30},{8,16},{10,18},{12,20},{14,22},{16,8},... | collective-permute-start | bytes 307208 | tf_op jit(solution)/shard_map/ppermute | solution.py:859
  130.3 3.1 %collective-permute-done.10 = bf16[200,256]{1,0:T(8,128)(2,1)S(1)} collective-permute-done((bf16[200,256]{1,0:T(8,128)(2,1)S(1)}, bf16[200,256]{1,0:T(8,128)(2,1)S(1)}, u32[]{:S(2)}, u32[]{:S(2)}) %collective-permute-start.10) | collective-permute-done | bytes 102432 | tf_op jit(solution)/shard_map/ppermute | solution.py:859
  133.3 3.3 %collective-permute-done.9 = bf16[200,256]{1,0:T(8,128)(2,1)S(1)} collective-permute-done((bf16[200,256]{1,0:T(8,128)(2,1)S(1)}, bf16[200,256]{1,0:T(8,128)(2,1)S(1)}, u32[]{:S(2)}, u32[]{:S(2)}) %collective-permute-start.9) | collective-permute-done | bytes 102432 | tf_op jit(solution)/shard_map/ppermute | solution.py:859
  136.9 2.5 %collective-permute-start.11 = (bf16[200,256]{1,0:T(8,128)(2,1)S(1)}, bf16[200,256]{1,0:T(8,128)(2,1)S(1)}, u32[]{:S(2)}, u32[]{:S(2)}) collective-permute-start(bf16[200,256]{1,0:T(8,128)(2,1)S(1)} %add_convert_fusion.6), channel_id=1, source_target_pairs={{0,24},{2,26},{4,28},{6,30},{8,16},{10,18},{12,20},{14,22},{16,8},... | collective-permute-start | bytes 307208 | tf_op jit(solution)/shard_map/ppermute | solution.py:859
  140.4 2.4 %collective-permute-done.13 = bf16[200,256]{1,0:T(8,128)(2,1)S(1)} collective-permute-done((bf16[200,256]{1,0:T(8,128)(2,1)S(1)}, bf16[200,256]{1,0:T(8,128)(2,1)S(1)}, u32[]{:S(2)}, u32[]{:S(2)}) %collective-permute-start.13) | collective-permute-done | bytes 102432 | tf_op jit(solution)/shard_map/ppermute | solution.py:859
  142.8 1.7 collective-permute-done.11
  144.5 3.7 %collective-permute-done.12 = bf16[200,256]{1,0:T(8,128)(2,1)S(1)} collective-permute-done((bf16[200,256]{1,0:T(8,128)(2,1)S(1)}, bf16[200,256]{1,0:T(8,128)(2,1)S(1)}, u32[]{:S(2)}, u32[]{:S(2)}) %collective-permute-start.12) | collective-permute-done | bytes 102432 | tf_op jit(solution)/shard_map/ppermute | solution.py:859
  149.4 1.5 collective-permute-start.17
  150.9 3.4 %collective-permute-done.14 = bf16[400,256]{1,0:T(8,128)(2,1)S(1)} collective-permute-done((bf16[400,256]{1,0:T(8,128)(2,1)S(1)}, bf16[400,256]{1,0:T(8,128)(2,1)S(1)}, u32[]{:S(2)}, u32[]{:S(2)}) %collective-permute-start.14) | collective-permute-done | bytes 204832 | tf_op jit(solution)/shard_map/ppermute | solution.py:840
  154.3 1.6 collective-permute-start.15
  156.0 1.4 collective-permute-start.18
  157.4 6.5 %collective-permute-done.15 = bf16[800,256]{1,0:T(8,128)(2,1)S(1)} collective-permute-done((bf16[800,256]{1,0:T(8,128)(2,1)S(1)}, bf16[800,256]{1,0:T(8,128)(2,1)S(1)}, u32[]{:S(2)}, u32[]{:S(2)}) %collective-permute-start.15) | collective-permute-done | bytes 409632 | tf_op jit(solution)/shard_map/ppermute | solution.py:840
  164.7 1.7 collective-permute-done.16.refs_1_
  167.5 4.2 %unpack.1 = (f32[2,256,256]{2,1,0:T(8,128)}, f32[2,256]{1,0:T(2,128)}, f32[2,256,256]{2,1,0:T(8,128)}, f32[2,256,256]{2,1,0:T(8,128)}, f32[2,256]{1,0:T(2,128)},...) custom-call(bf16[1600,256]{1,0:T(8,128)(2,1)S(1)} %pad_maximum_fusio, ...), custom_call_target="tpu_custom_call" | custom-call | tf_op jit(solution)/shard_map/unpack/pallas_call | solution.py:819
  (80 shorter events, 10.5 us)
Async XLA Ops:
  3.0 23.8 %copy-start = (bf16[2,256,1024]{2,1,0:T(8,128)(2,1)S(1)}, bf16[2,256,1024]{2,1,0:T(8,128)(2,1)}, u32[]{:S(2)}) copy-start(bf16[2,256,1024]{2,1,0:T(8,128)(2,1)} %refs_9_.5) | copy-start | bytes 3145732
  3.0 23.8 %copy-start.1 = (bf16[2,1024,256]{2,1,0:T(8,128)(2,1)S(1)}, bf16[2,1024,256]{2,1,0:T(8,128)(2,1)}, u32[]{:S(2)}) copy-start(bf16[2,1024,256]{2,1,0:T(8,128)(2,1)} %refs_11_.5) | copy-start | bytes 3145732
  3.0 23.8 %copy-start.2 = (bf16[2,256,256]{2,1,0:T(8,128)(2,1)S(1)}, bf16[2,256,256]{2,1,0:T(8,128)(2,1)}, u32[]{:S(2)}) copy-start(bf16[2,256,256]{2,1,0:T(8,128)(2,1)} %refs_0_.5) | copy-start | bytes 786436
  3.0 23.8 %copy-start.3 = (bf16[2,256,256]{2,1,0:T(8,128)(2,1)S(1)}, bf16[2,256,256]{2,1,0:T(8,128)(2,1)}, u32[]{:S(2)}) copy-start(bf16[2,256,256]{2,1,0:T(8,128)(2,1)} %refs_2_.5) | copy-start | bytes 786436
  3.0 23.8 %copy-start.4 = (bf16[2,256,256]{2,1,0:T(8,128)(2,1)S(1)}, bf16[2,256,256]{2,1,0:T(8,128)(2,1)}, u32[]{:S(2)}) copy-start(bf16[2,256,256]{2,1,0:T(8,128)(2,1)} %refs_3_.5) | copy-start | bytes 786436
  3.0 23.8 %copy-start.5 = (bf16[2,256,256]{2,1,0:T(8,128)(2,1)S(1)}, bf16[2,256,256]{2,1,0:T(8,128)(2,1)}, u32[]{:S(2)}) copy-start(bf16[2,256,256]{2,1,0:T(8,128)(2,1)} %refs_5_.5) | copy-start | bytes 786436
  3.1 23.8 %copy-start.7 = (bf16[4,1,1,80,256]{4,3,2,1,0:T(8,128)(2,1)S(1)}, bf16[4,1,1,80,256]{4,3,2,1,0:T(8,128)(2,1)}, u32[]{:S(2)}) copy-start(bf16[4,1,1,80,256]{4,3,2,1,0:T(8,128)(2,1)} %param.22) | copy-start | bytes 491524
  3.1 23.8 %copy-start.8 = (f32[2,1024]{1,0:T(2,128)S(1)}, f32[2,1024]{1,0:T(2,128)}, u32[]{:S(2)}) copy-start(f32[2,1024]{1,0:T(2,128)} %refs_10_.5) | copy-start | bytes 24580
  3.1 23.8 %copy-start.10 = (f32[2,256]{1,0:T(2,128)S(1)}, f32[2,256]{1,0:T(2,128)}, u32[]{:S(2)}) copy-start(f32[2,256]{1,0:T(2,128)} %refs_1_.5) | copy-start | bytes 6148
  3.1 23.8 %copy-start.11 = (f32[2,256]{1,0:T(2,128)S(1)}, f32[2,256]{1,0:T(2,128)}, u32[]{:S(2)}) copy-start(f32[2,256]{1,0:T(2,128)} %refs_4_.5) | copy-start | bytes 6148
  23.4 3.4 %collective-permute-start = (bf16[4,16,256]{2,1,0:T(8,128)(2,1)}, bf16[4,16,256]{2,1,0:T(8,128)(2,1)S(1)}, u32[]{:S(2)}, u32[]{:S(2)}) collective-permute-start(bf16[4,16,256]{2,1,0:T(8,128)(2,1)} %get-tuple-element.62), channel_id=1, source_target_pairs={{0,2},{2,4},{4,6},{6,8},{8,10},{10,12},{12,14},{14,16},{16,18},{18... | collective-permute-start | bytes 98312 | tf_op jit(solution)/shard_map/ppermute | solution.py:835
  27.0 44.2 %copy-start.6 = (bf16[4,528,64]{2,1,0:T(8,128)(2,1)S(1)}, bf16[4,528,64]{2,1,0:T(8,128)(2,1)}, u32[]{:S(2)}) copy-start(bf16[4,528,64]{2,1,0:T(8,128)(2,1)} %get-tuple-element.71.refs_20_) | copy-start | bytes 811012
  27.0 44.1 %copy-start.9 = (f32[4,4,512]{2,1,0:T(4,128)S(1)}, f32[4,4,512]{2,1,0:T(4,128)}, u32[]{:S(2)}) copy-start(f32[4,4,512]{2,1,0:T(4,128)} %get-tuple-element.72.refs_21_) | copy-start | bytes 98308
  65.2 36.2 %collective-permute-start.4 = (bf16[1600,256]{1,0:T(8,128)(2,1)S(1)}, bf16[1600,256]{1,0:T(8,128)(2,1)S(1)}, u32[]{:S(2)}, u32[]{:S(2)}) collective-permute-start(bf16[1600,256]{1,0:T(8,128)(2,1)S(1)} %get-tuple-element.85), channel_id=1, source_target_pairs={{0,2},{2,0},{4,6},{6,4},{8,10},{10,8},{12,14},{14,12},{16,18},{18,... | collective-permute-start | bytes 2457608 | tf_op jit(solution)/shard_map/ppermute | solution.py:840
  68.1 3.1 %collective-permute-start.1 = (bf16[4,16,256]{2,1,0:T(8,128)(2,1)S(1)}, bf16[4,16,256]{2,1,0:T(8,128)(2,1)S(1)}, u32[]{:S(2)}, u32[]{:S(2)}) collective-permute-start(bf16[4,16,256]{2,1,0:T(8,128)(2,1)S(1)} %get-tuple-element.65), channel_id=1, source_target_pairs={{2,0},{4,2},{6,4},{8,6},{10,8},{12,10},{14,12},{16,14},{18,16},{20... | collective-permute-start | bytes 98312 | tf_op jit(solution)/shard_map/ppermute | solution.py:835
  98.7 6.1 %collective-permute-start.2 = (bf16[1600,256]{1,0:T(8,128)(2,1)S(1)}, bf16[1600,256]{1,0:T(8,128)(2,1)S(1)}, u32[]{:S(2)}, u32[]{:S(2)}) collective-permute-start(bf16[1600,256]{1,0:T(8,128)(2,1)S(1)} %get-tuple-element.83), channel_id=1, source_target_pairs={{0,2},{2,0},{4,6},{6,4},{8,10},{10,8},{12,14},{14,12},{16,18},{18,... | collective-permute-start | bytes 2457608 | tf_op jit(solution)/shard_map/ppermute | solution.py:840
  101.6 12.7 %collective-permute-start.5 = (bf16[800,256]{1,0:T(8,128)(2,1)S(1)}, bf16[800,256]{1,0:T(8,128)(2,1)S(1)}, u32[]{:S(2)}, u32[]{:S(2)}) collective-permute-start(bf16[800,256]{1,0:T(8,128)(2,1)S(1)} %slice.43), channel_id=1, source_target_pairs={{0,4},{2,6},{4,0},{6,2},{8,12},{10,14},{12,8},{14,10},{16,20},{18,... | collective-permute-start | bytes 1228808 | tf_op jit(solution)/shard_map/ppermute | solution.py:840
  105.0 11.2 %collective-permute-start.3 = (bf16[800,256]{1,0:T(8,128)(2,1)S(1)}, bf16[800,256]{1,0:T(8,128)(2,1)S(1)}, u32[]{:S(2)}, u32[]{:S(2)}) collective-permute-start(bf16[800,256]{1,0:T(8,128)(2,1)S(1)} %slice.41), channel_id=1, source_target_pairs={{0,1},{1,0},{2,3},{3,2},{4,5},{5,4},{6,7},{7,6},{8,9},{9,8},{10,11... | collective-permute-start | bytes 1228808 | tf_op jit(solution)/shard_map/ppermute | solution.py:840
  116.3 7.1 %collective-permute-start.6 = (bf16[400,256]{1,0:T(8,128)(2,1)S(1)}, bf16[400,256]{1,0:T(8,128)(2,1)S(1)}, u32[]{:S(2)}, u32[]{:S(2)}) collective-permute-start(bf16[400,256]{1,0:T(8,128)(2,1)S(1)} %slice.35), channel_id=1, source_target_pairs={{0,4},{2,6},{4,0},{6,2},{8,12},{10,14},{12,8},{14,10},{16,20},{18,... | collective-permute-start | bytes 614408 | tf_op jit(solution)/shard_map/ppermute | solution.py:840
  118.6 6.3 %collective-permute-start.7 = (bf16[400,256]{1,0:T(8,128)(2,1)S(1)}, bf16[400,256]{1,0:T(8,128)(2,1)S(1)}, u32[]{:S(2)}, u32[]{:S(2)}) collective-permute-start(bf16[400,256]{1,0:T(8,128)(2,1)S(1)} %slice.37), channel_id=1, source_target_pairs={{0,1},{1,0},{2,3},{3,2},{4,5},{5,4},{6,7},{7,6},{8,9},{9,8},{10,11... | collective-permute-start | bytes 614408 | tf_op jit(solution)/shard_map/ppermute | solution.py:840
  125.8 7.5 %collective-permute-start.10 = (bf16[200,256]{1,0:T(8,128)(2,1)S(1)}, bf16[200,256]{1,0:T(8,128)(2,1)S(1)}, u32[]{:S(2)}, u32[]{:S(2)}) collective-permute-start(bf16[200,256]{1,0:T(8,128)(2,1)S(1)} %get-tuple-element.109), channel_id=1, source_target_pairs={{0,24},{2,26},{4,28},{6,30},{8,16},{10,18},{12,20},{14,22},{16,8},... | collective-permute-start | bytes 307208 | tf_op jit(solution)/shard_map/ppermute | solution.py:859
  128.3 8.3 %collective-permute-start.9 = (bf16[200,256]{1,0:T(8,128)(2,1)S(1)}, bf16[200,256]{1,0:T(8,128)(2,1)S(1)}, u32[]{:S(2)}, u32[]{:S(2)}) collective-permute-start(bf16[200,256]{1,0:T(8,128)(2,1)S(1)} %get-tuple-element.108), channel_id=1, source_target_pairs={{0,16},{2,18},{4,20},{6,22},{8,24},{10,26},{12,28},{14,30},{16,0},... | collective-permute-start | bytes 307208 | tf_op jit(solution)/shard_map/ppermute | solution.py:859
  128.9 7.7 %collective-permute-start.8 = (bf16[200,256]{1,0:T(8,128)(2,1)S(1)}, bf16[200,256]{1,0:T(8,128)(2,1)S(1)}, u32[]{:S(2)}, u32[]{:S(2)}) collective-permute-start(bf16[200,256]{1,0:T(8,128)(2,1)S(1)} %get-tuple-element.107), channel_id=1, source_target_pairs={{0,8},{2,10},{4,12},{6,14},{8,0},{10,2},{12,4},{14,6},{16,24},{18,... | collective-permute-start | bytes 307208 | tf_op jit(solution)/shard_map/ppermute | solution.py:859
  136.8 6.0 %collective-permute-start.13 = (bf16[200,256]{1,0:T(8,128)(2,1)S(1)}, bf16[200,256]{1,0:T(8,128)(2,1)S(1)}, u32[]{:S(2)}, u32[]{:S(2)}) collective-permute-start(bf16[200,256]{1,0:T(8,128)(2,1)S(1)} %add_convert_fusion.6), channel_id=1, source_target_pairs={{0,8},{2,10},{4,12},{6,14},{8,0},{10,2},{12,4},{14,6},{16,24},{18,... | collective-permute-start | bytes 307208 | tf_op jit(solution)/shard_map/ppermute | solution.py:859
  136.9 7.6 %collective-permute-start.11 = (bf16[200,256]{1,0:T(8,128)(2,1)S(1)}, bf16[200,256]{1,0:T(8,128)(2,1)S(1)}, u32[]{:S(2)}, u32[]{:S(2)}) collective-permute-start(bf16[200,256]{1,0:T(8,128)(2,1)S(1)} %add_convert_fusion.6), channel_id=1, source_target_pairs={{0,24},{2,26},{4,28},{6,30},{8,16},{10,18},{12,20},{14,22},{16,8},... | collective-permute-start | bytes 307208 | tf_op jit(solution)/shard_map/ppermute | solution.py:859
  139.5 8.7 %collective-permute-start.12 = (bf16[200,256]{1,0:T(8,128)(2,1)S(1)}, bf16[200,256]{1,0:T(8,128)(2,1)S(1)}, u32[]{:S(2)}, u32[]{:S(2)}) collective-permute-start(bf16[200,256]{1,0:T(8,128)(2,1)S(1)} %add_convert_fusion.6), channel_id=1, source_target_pairs={{0,16},{2,18},{4,20},{6,22},{8,24},{10,26},{12,28},{14,30},{16,0},... | collective-permute-start | bytes 307208 | tf_op jit(solution)/shard_map/ppermute | solution.py:859
  148.4 5.8 %collective-permute-start.14 = (bf16[400,256]{1,0:T(8,128)(2,1)S(1)}, bf16[400,256]{1,0:T(8,128)(2,1)S(1)}, u32[]{:S(2)}, u32[]{:S(2)}) collective-permute-start(bf16[400,256]{1,0:T(8,128)(2,1)S(1)} %get-tuple-element.106), channel_id=1, source_target_pairs={{0,4},{2,6},{4,0},{6,2},{8,12},{10,14},{12,8},{14,10},{16,20},{18,... | collective-permute-start | bytes 614408 | tf_op jit(solution)/shard_map/ppermute | solution.py:840
  149.4 6.5 %collective-permute-start.17 = (bf16[400,256]{1,0:T(8,128)(2,1)S(1)}, bf16[400,256]{1,0:T(8,128)(2,1)S(1)}, u32[]{:S(2)}, u32[]{:S(2)}) collective-permute-start(bf16[400,256]{1,0:T(8,128)(2,1)S(1)} %get-tuple-element.105), channel_id=1, source_target_pairs={{0,1},{1,0},{2,3},{3,2},{4,5},{5,4},{6,7},{7,6},{8,9},{9,8},{10,11... | collective-permute-start | bytes 614408 | tf_op jit(solution)/shard_map/ppermute | solution.py:840
  154.3 9.6 %collective-permute-start.15 = (bf16[800,256]{1,0:T(8,128)(2,1)S(1)}, bf16[800,256]{1,0:T(8,128)(2,1)S(1)}, u32[]{:S(2)}, u32[]{:S(2)}) collective-permute-start(bf16[800,256]{1,0:T(8,128)(2,1)S(1)} %pad_maximum_fusion.2), channel_id=1, source_target_pairs={{0,1},{1,0},{2,3},{3,2},{4,5},{5,4},{6,7},{7,6},{8,9},{9,8},{10,11... | collective-permute-start | bytes 1228808 | tf_op jit(solution)/shard_map/ppermute | solution.py:840
  156.0 8.4 %collective-permute-start.18 = (bf16[800,256]{1,0:T(8,128)(2,1)S(1)}, bf16[800,256]{1,0:T(8,128)(2,1)S(1)}, u32[]{:S(2)}, u32[]{:S(2)}) collective-permute-start(bf16[800,256]{1,0:T(8,128)(2,1)S(1)} %pad_maximum_fusion.3), channel_id=1, source_target_pairs={{0,4},{2,6},{4,0},{6,2},{8,12},{10,14},{12,8},{14,10},{16,20},{18,... | collective-permute-start | bytes 1228808 | tf_op jit(solution)/shard_map/ppermute | solution.py:840
  164.0 2.4 %collective-permute-start.16 = (bf16[1600,256]{1,0:T(8,128)(2,1)S(1)}, bf16[1600,256]{1,0:T(8,128)(2,1)S(1)}, u32[]{:S(2)}, u32[]{:S(2)}) collective-permute-start(bf16[1600,256]{1,0:T(8,128)(2,1)S(1)} %pad_maximum_fusion.refs_0_), channel_id=1, source_target_pairs={{0,2},{2,0},{4,6},{6,4},{8,10},{10,8},{12,14},{14,12},{16,18},{18,... | collective-permute-start | bytes 2457608 | tf_op jit(solution)/shard_map/ppermute | solution.py:840
  164.5 3.1 %collective-permute-start.19 = (bf16[1600,256]{1,0:T(8,128)(2,1)S(1)}, bf16[1600,256]{1,0:T(8,128)(2,1)S(1)}, u32[]{:S(2)}, u32[]{:S(2)}) collective-permute-start(bf16[1600,256]{1,0:T(8,128)(2,1)S(1)} %pad_maximum_fusion.1.refs_2_), channel_id=1, source_target_pairs={{0,2},{2,0},{4,6},{6,4},{8,10},{10,8},{12,14},{14,12},{16,18},{18,... | collective-permute-start | bytes 2457608 | tf_op jit(solution)/shard_map/ppermute | solution.py:840
  (10 other events, 216.4 us)

commit v5 on v4

--- a/solution.py
+++ b/solution.py
@@ -704,7 +704,7 @@
         + [fixed(o.shape) for o in outs[3:]],
         out_shape=outs,
         scratch_shapes=stash + scratch(micro, full, features, units),
-        compiler_params=pltpu.CompilerParams(vmem_limit_bytes=48 * 2**20),
+        compiler_params=pltpu.CompilerParams(vmem_limit_bytes=52 * 2**20),
         name="upper_both",
     )(counts, *ins, *weights)
 
@@ -752,12 +752,12 @@
         out_specs=[by_micro(outs[0].shape)] + [fixed(o.shape) for o in outs[1:]],
         out_shape=outs,
         scratch_shapes=scratch(micro, full, features, units),
-        compiler_params=pltpu.CompilerParams(vmem_limit_bytes=48 * 2**20),
+        compiler_params=pltpu.CompilerParams(vmem_limit_bytes=52 * 2**20),
         name="lower_backward",
     )(grad, back, *weights, *stash)
 
 
-def unpack_kernel(place_of_layer, *refs):
+def unpack_kernel(bits, *refs):
     sources, refs = refs[:4], refs[4:]
     out, refs = Weights(*refs[: len(Weights._fields)]), refs[len(Weights._fields) :]
     ordered, *staged, in_sems, out_sems = refs
@@ -774,7 +774,7 @@
         load.start()
     sizes = [features] * 4 + [units, units]
     sizes.append(rows - sum(sizes))
-    me = [place_of_layer(layer) for layer in range(2)]
+    me = place_of(bits)
 
     def store(index, layer):
         return pltpu.make_async_copy(staged[index].at[layer], arrays[index].at[layer], out_sems.at[layer, index])
@@ -788,9 +788,8 @@
                 loads[2 * i].wait()
                 loads[2 * i + 1].wait()
 
-        mine = jnp.where(layer == 0, me[0], me[1])
         for index, start, which, offset, take in spans(sizes, rows):
-            at = pl.multiple_of((which ^ mine) * piece, TILE) + offset
+            at = pl.multiple_of((which ^ me) * piece, TILE) + offset
             value = ordered[layer, pl.ds(pl.multiple_of(at, TILE), take), :]
             if index == 4:
                 staged[index][layer, :, start : start + take] = value.T.astype(F32)
@@ -817,7 +816,7 @@
     shapes = Weights(*outs)
     large = squares(shapes) + (shapes.w_up, shapes.w_down)
     return pl.pallas_call(
-        functools.partial(unpack_kernel, lambda layer: place_of(bits[layer])),
+        functools.partial(unpack_kernel, bits),
         in_specs=[pl.BlockSpec(memory_space=pl.ANY)] * 4,
         out_specs=[pl.BlockSpec(memory_space=pl.ANY if len(o.shape) == 3 else pltpu.VMEM) for o in outs],
         out_shape=outs,
@@ -875,27 +874,26 @@
     return jnp.where(high, jnp.concatenate([upper, lower], axis=0), jnp.concatenate([lower, upper], axis=0))
 
 
-def sum_all(lower, upper, lower_bits, upper_bits, rest_bits, others):
-    chains = []
-    for (keep, send), bits in ((lower, lower_bits), (upper, upper_bits)):
-        chains.append((plus(keep, swap(send, bits[0])), bits))
-    for level in (1, 2):
-        sent = [swap(kept[kept.shape[0] // 2 :], bits[level]) for kept, bits in chains]
-        chains = [(plus(kept[: kept.shape[0] // 2], got), bits) for got, (kept, bits) in zip(sent, chains)]
-        if level == 1:
-            others = [with_layout_constraint(jnp.transpose(v, (1, 0, 2)), Layout((0, 1, 2))) for v in others]
-            others, tied = lax.optimization_barrier((others, [kept for kept, _ in chains]))
-            chains = [(kept, bits) for kept, (_, bits) in zip(tied, chains)]
-    size = chains[0][0].shape[0]
-    both = sum_rest(jnp.concatenate([kept for kept, _ in chains], axis=0), rest_bits)
-    chains = [(both[:size], lower_bits), (both[size:], upper_bits)]
-    for level in (2, 1):
-        sent = [swap(kept, bits[level]) for kept, bits in chains]
-        chains = [(jnp.concatenate([kept, got], axis=0), bits) for got, (kept, bits) in zip(sent, chains)]
-    out = []
-    for kept, bits in chains:
-        out += [kept, swap(kept, bits[0])]
-    return out, others
+def sum_all(halves, core, along, across, rest_bits, others):
+    def to(part, j):
+        swaps = [(axis, step) for (axis, step), used in ((across, j % 2), (along, j // 2)) if used]
+        sizes = [lax.axis_size(axis) for axis in (LINE, PAIR)]
+        line = sum(step for axis, step in swaps if axis == LINE)
+        pair = sum(step for axis, step in swaps if axis == PAIR)
+        perm = [(i * sizes[1] + k, (i ^ line) * sizes[1] + (k ^ pair)) for i in range(sizes[0]) for k in range(sizes[1])]
+        return lax.ppermute(part, (LINE, PAIR), perm)
+
+    chains = [plus(keep, swap(send, core)) for keep, send in halves]
+    rows = chains[0].shape[0] // 4
+    for i, kept in enumerate(chains):
+        got = [to(kept[j * rows : (j + 1) * rows], j) for j in (1, 2, 3)]
+        chains[i] = sum([part.astype(F32) for part in got], kept[:rows].astype(F32)).astype(BF16)
+    chains = [sum_rest(kept, rest_bits) for kept in chains]
+    others, chains[0] = lax.optimization_barrier((others, chains[0]))
+    chains = [jnp.concatenate([kept] + [to(kept, j) for j in (1, 2, 3)], axis=0) for kept in chains]
+    others = [with_layout_constraint(jnp.transpose(v, (1, 0, 2)), Layout((0, 1, 2))) for v in others]
+    others, chains[0] = lax.optimization_barrier((others, chains[0]))
+    return [part for kept in chains for part in (kept, swap(kept, core))], others
 
 
 def local(hidden, write_cotangent, targets, positions, counts, *weights):
@@ -905,14 +903,14 @@
     full = -(-rows // TILE) * TILE
     bits = [(axis, 1 << i) for axis in (LINE, PAIR) for i in range(lax.axis_size(axis).bit_length() - 1)]
     core, along, across = (LINE, 1), (LINE, 2), (PAIR, 1)
-    lower_bits, upper_bits = (core, across, along), (core, along, across)
-    rest_bits = [bit for bit in bits if bit not in lower_bits]
+    piece_bits = (core, along, across)
+    rest_bits = [bit for bit in bits if bit not in piece_bits]
 
     hidden_rows = hidden.reshape(micro, rows, features)
     lower_out, sent, stash = lower_forward(hidden_rows, weights, full)
     arrived = from_behind(sent, LINE, 1)
     out, grad, back, *upper = upper_both(
-        upper_bits,
+        piece_bits,
         counts.reshape(micro),
         lower_out,
         arrived,
@@ -923,9 +921,9 @@
         rows,
     )
     returned = from_behind(back, LINE, -1)
-    grad_in, *lower = lower_backward(lower_bits, grad, returned, weights, stash, rows, memory)
-    parts, (out, grad_in) = sum_all(lower, upper, lower_bits, upper_bits, rest_bits, (out, grad_in))
-    grads = unpack((lower_bits, upper_bits), parts, weights)
+    grad_in, *lower = lower_backward(piece_bits, grad, returned, weights, stash, rows, memory)
+    parts, (out, grad_in) = sum_all((lower, upper), core, along, across, rest_bits, (out, grad_in))
+    grads = unpack(piece_bits, parts, weights)
     out, grad_in = (jnp.transpose(v, (1, 0, 2)).reshape(hidden.shape) for v in (out, grad_in))
     return (out, grad_in) + tuple(grads)
 

time: 172 us -> 168 us (0.977)
  waiting for transfers between devices: 41.3 us -> 24.8 us
  starting transfers between devices: 31.4 us -> 42.9 us
  Pallas kernels: 90.1 us -> 92.9 us
    ppermute x12 -> x4, waiting for transfers between devices: 24.4 us -> 2.32 us  [swap(): lax.ppermute(value, axis, [(i, i ^ step) for i in range(lax.axis_size(axi...]
    ppermute x0 -> x12, waiting for transfers between devices: none -> 16.7 us  [to(): return lax.ppermute(part, (LINE, PAIR), perm)]
    ppermute x0 -> x12, starting transfers between devices: none -> 15.2 us  [to(): return lax.ppermute(part, (LINE, PAIR), perm)]
    ppermute x12 -> x4, starting transfers between devices: 19.8 us -> 5.81 us  [swap(): lax.ppermute(value, axis, [(i, i ^ step) for i in range(lax.axis_size(axi...]
    ppermute x6 -> x12, waiting for transfers between devices: 14.1 us -> 2.86 us  [across(): lax.ppermute(part, axis, [(i, i ^ k * step) for i in range(lax.axis_size(...]
    ppermute x6 -> x12, starting transfers between devices: 7.98 us -> 18.3 us  [across(): lax.ppermute(part, axis, [(i, i ^ k * step) for i in range(lax.axis_size(...]
    pallas_call x2 -> x0, local copies, waits for them, and re-layouts: 3.05 us -> none  [the longest x1 1.53 us: lower_backward(): pl.pallas_call(functools.partial(lower_backward_kernel, memory, bits), gr...]
    transpose x0 -> x1, local copies, waits for them, and re-layouts: none -> 2.43 us  [sum_all(): jnp.transpose(v, (1, 0, 2))]
  transfers between devices with their start and end apart: 20 -> 30, of which waited for: 17 -> 13; matrix products, arithmetic and copies ran while one was open for 2% -> 2% of each run, Pallas kernels for 16% -> 17%
where the time goes in v5:
time: 168 us
  Pallas kernels  92.9 us (55%)
  starting transfers between devices  42.9 us (26%)
  waiting for transfers between devices  24.8 us (15%)
  local copies, waits for them, and re-layouts  5.1 us (3%)
    pallas_call x1, Pallas kernels, upper_both(): pl.pallas_call(functools.partial(upper_kernel, rows, micro, bits), grid=(...  39.7 us
    pallas_call x1, Pallas kernels, lower_backward(): pl.pallas_call(functools.partial(lower_backward_kernel, memory, bits), gr...  28.8 us
    pallas_call x1, Pallas kernels, lower_forward(): pl.pallas_call(lower_forward_kernel, grid=(micro,), in_specs=[by_micro(hi...  20.3 us
    ppermute x12, starting transfers between devices, across(): lax.ppermute(part, axis, [(i, i ^ k * step) for i in range(lax.axis_size(...  18.3 us
    ppermute x12, waiting for transfers between devices, to(): return lax.ppermute(part, (LINE, PAIR), perm)  16.7 us
    ppermute x12, starting transfers between devices, to(): return lax.ppermute(part, (LINE, PAIR), perm)  15.2 us
    ppermute x4, starting transfers between devices, swap(): lax.ppermute(value, axis, [(i, i ^ step) for i in range(lax.axis_size(axi...  5.81 us
    pallas_call x1, Pallas kernels, unpack(): pl.pallas_call(functools.partial(unpack_kernel, bits), in_specs=[pl.Block...  4.22 us
  transfers between devices with their start and end apart: 30, of which 13 were waited for; matrix products, arithmetic and copies ran while one was open for 2% of the time, Pallas kernels for 17%

profile of v5, /device:TPU:0, one launch (start us, length us, event | category | flops | bytes accessed | tf_op | source)
XLA Modules:
  0.0 168.1 jit_solution(8129779195477234512)
XLA Ops:
  0.7 2.4 %copy.45 = bf16[4,1,1,522,256]{4,3,0,2,1:T(8,128)(2,1)} copy(bf16[4,1,1,522,256]{4,0,3,2,1:T(4,128)(2,1)} %param.20) | data formatting | bytes 2138112 | tf_op args[0]
  3.2 20.3 %lower_forward.1 = (bf16[4,528,256]{2,1,0:T(8,128)(2,1)}, bf16[4,16,256]{2,1,0:T(8,128)(2,1)}, bf16[4,528,256]{2,1,0:T(8,128)(2,1)}, bf16[4,528,256]{2,1,0:T(8,1...) custom-call(bf16[4,522,256]{2,1,0:T(8,128)(2,1)} %bitcast.23, ...), custom_call_target="tpu_custom_call" | custom-call | tf_op jit(solution)/shard_map/lower_forward/pallas_call | solution.py:577
  23.4 2.4 %collective-permute-start = (bf16[4,16,256]{2,1,0:T(8,128)(2,1)}, bf16[4,16,256]{2,1,0:T(8,128)(2,1)S(1)}, u32[]{:S(2)}, u32[]{:S(2)}) collective-permute-start(bf16[4,16,256]{2,1,0:T(8,128)(2,1)} %get-tuple-element.64), channel_id=1, source_target_pairs={{0,2},{2,4},{4,6},{6,8},{8,10},{10,12},{12,14},{14,16},{16,18},{18... | collective-permute-start | bytes 98312 | tf_op jit(solution)/shard_map/ppermute | solution.py:834
  25.8 1.0 collective-permute-done.arrived_ref
  27.0 39.7 %upper_both.1 = (bf16[4,522,256]{2,1,0:T(8,128)(2,1)}, f32[4,528,256]{2,1,0:T(8,128)}, bf16[4,16,256]{2,1,0:T(8,128)(2,1)S(1)}, bf16[1600,256]{1,0:T(8,128)(2,1)}, bf16[1600,256]{1,0:T(8,128)(2,1)}) custom-call(s32[4]{0:T(128)S(1)} %bitcast.22, bf16[4,528,256]{2,1,0:T(8,128)(2,1)} %get-tuple-element.63.x_ref, ...), custom_call_target="tpu_custom_call" | custom-call | tf_op jit(solution)/shard_map/upper_both/pallas_call | solution.py:699
  66.7 3.0 %collective-permute-start.16 = (bf16[1600,256]{1,0:T(8,128)(2,1)}, bf16[1600,256]{1,0:T(8,128)(2,1)S(1)}, u32[]{:S(2)}, u32[]{:S(2)}) collective-permute-start(bf16[1600,256]{1,0:T(8,128)(2,1)} %get-tuple-element.93), channel_id=1, source_target_pairs={{0,2},{2,0},{4,6},{6,4},{8,10},{10,8},{12,14},{14,12},{16,18},{18,... | collective-permute-start | bytes 2457608 | tf_op jit(solution)/shard_map/ppermute | solution.py:839
  69.6 1.3 collective-permute-start.1
  70.9 1.8 %collective-permute-done.1.back_ref = bf16[4,16,256]{2,1,0:T(8,128)(2,1)S(1)} collective-permute-done((bf16[4,16,256]{2,1,0:T(8,128)(2,1)S(1)}, bf16[4,16,256]{2,1,0:T(8,128)(2,1)S(1)}, u32[]{:S(2)}, u32[]{:S(2)}) %collective-permute-start.1) | collective-permute-done | bytes 32800 | tf_op jit(solution)/shard_map/ppermute | solution.py:834
  72.7 28.8 %lower_backward.1 = (bf16[4,522,256]{2,1,0:T(8,128)(2,1)}, bf16[1600,256]{1,0:T(8,128)(2,1)}, bf16[1600,256]{1,0:T(8,128)(2,1)}) custom-call(f32[4,528,256]{2,1,0:T(8,128)} %get-tuple-element.66.grad_ref, bf16[4,16,256]{2,1,0:T(8,128)(2,1)S(1)} %collective-permute-done.1.back_ref, bf16[2,256,256]{2,1,0:T(8,128)(2,1)S(1)} %copy-done, f32[2,256]{1,0:T(2,128)S(1)} %copy-done.8, ...), custom_call_target="tpu_custom_call" | custom-call | tf_op jit(solution)/shard_map/lower_backward/pallas_call | solution.py:746
  101.5 2.7 %collective-permute-start.2 = (bf16[1600,256]{1,0:T(8,128)(2,1)}, bf16[1600,256]{1,0:T(8,128)(2,1)S(1)}, u32[]{:S(2)}, u32[]{:S(2)}) collective-permute-start(bf16[1600,256]{1,0:T(8,128)(2,1)} %get-tuple-element.85), channel_id=1, source_target_pairs={{0,2},{2,0},{4,6},{6,4},{8,10},{10,8},{12,14},{14,12},{16,18},{18,... | collective-permute-start | bytes 2457608 | tf_op jit(solution)/shard_map/ppermute | solution.py:839
  104.5 4.0 %collective-permute-start.19 = (bf16[400,256]{1,0:T(8,128)(2,1)S(1)}, bf16[400,256]{1,0:T(8,128)(2,1)S(1)}, u32[]{:S(2)}, u32[]{:S(2)}) collective-permute-start(bf16[400,256]{1,0:T(8,128)(2,1)S(1)} %get-tuple-element.110), channel_id=1, source_target_pairs={{0,5},{1,4},{2,7},{3,6},{4,1},{5,0},{6,3},{7,2},{8,13},{9,12},{10,... | collective-permute-start | bytes 614408 | tf_op jit(solution)/shard_map/ppermute | solution.py:884
  109.5 2.9 %collective-permute-start.5 = (bf16[400,256]{1,0:T(8,128)(2,1)S(1)}, bf16[400,256]{1,0:T(8,128)(2,1)S(1)}, u32[]{:S(2)}, u32[]{:S(2)}) collective-permute-start(bf16[400,256]{1,0:T(8,128)(2,1)S(1)} %get-tuple-element.113), channel_id=1, source_target_pairs={{0,5},{1,4},{2,7},{3,6},{4,1},{5,0},{6,3},{7,2},{8,13},{9,12},{10,... | collective-permute-start | bytes 614408 | tf_op jit(solution)/shard_map/ppermute | solution.py:884
  112.4 2.0 %collective-permute-done.19 = bf16[400,256]{1,0:T(8,128)(2,1)S(1)} collective-permute-done((bf16[400,256]{1,0:T(8,128)(2,1)S(1)}, bf16[400,256]{1,0:T(8,128)(2,1)S(1)}, u32[]{:S(2)}, u32[]{:S(2)}) %collective-permute-start.19) | collective-permute-done | bytes 204832 | tf_op jit(solution)/shard_map/ppermute | solution.py:884
  115.0 3.9 %collective-permute-done.18 = bf16[400,256]{1,0:T(8,128)(2,1)S(1)} collective-permute-done((bf16[400,256]{1,0:T(8,128)(2,1)S(1)}, bf16[400,256]{1,0:T(8,128)(2,1)S(1)}, u32[]{:S(2)}, u32[]{:S(2)}) %collective-permute-start.18) | collective-permute-done | bytes 204832 | tf_op jit(solution)/shard_map/ppermute | solution.py:884
  119.6 3.7 %collective-permute-start.22 = (bf16[100,256]{1,0:T(8,128)(2,1)S(1)}, bf16[100,256]{1,0:T(8,128)(2,1)S(1)}, u32[]{:S(2)}, u32[]{:S(2)}) collective-permute-start(bf16[100,256]{1,0:T(8,128)(2,1)S(1)} %get-tuple-element.116), channel_id=1, source_target_pairs={{0,24},{2,26},{4,28},{6,30},{8,16},{10,18},{12,20},{14,22},{16,8},... | collective-permute-start | bytes 153608 | tf_op jit(solution)/shard_map/ppermute | solution.py:858
  123.3 2.1 %collective-permute-start.20 = (bf16[100,256]{1,0:T(8,128)(2,1)S(1)}, bf16[100,256]{1,0:T(8,128)(2,1)S(1)}, u32[]{:S(2)}, u32[]{:S(2)}) collective-permute-start(bf16[100,256]{1,0:T(8,128)(2,1)S(1)} %get-tuple-element.115), channel_id=1, source_target_pairs={{0,8},{2,10},{4,12},{6,14},{8,0},{10,2},{12,4},{14,6},{16,24},{18,... | collective-permute-start | bytes 153608 | tf_op jit(solution)/shard_map/ppermute | solution.py:858
  125.4 1.7 %collective-permute-done.4 = bf16[400,256]{1,0:T(8,128)(2,1)S(1)} collective-permute-done((bf16[400,256]{1,0:T(8,128)(2,1)S(1)}, bf16[400,256]{1,0:T(8,128)(2,1)S(1)}, u32[]{:S(2)}, u32[]{:S(2)}) %collective-permute-start.4) | collective-permute-done | bytes 204832 | tf_op jit(solution)/shard_map/ppermute | solution.py:884
  127.6 3.5 %collective-permute-start.8 = (bf16[100,256]{1,0:T(8,128)(2,1)S(1)}, bf16[100,256]{1,0:T(8,128)(2,1)S(1)}, u32[]{:S(2)}, u32[]{:S(2)}) collective-permute-start(bf16[100,256]{1,0:T(8,128)(2,1)S(1)} %get-tuple-element.119), channel_id=1, source_target_pairs={{0,24},{2,26},{4,28},{6,30},{8,16},{10,18},{12,20},{14,22},{16,8},... | collective-permute-start | bytes 153608 | tf_op jit(solution)/shard_map/ppermute | solution.py:858
  132.1 1.2 collective-permute-start.25
  133.2 2.4 %collective-permute-start.23 = (bf16[100,256]{1,0:T(8,128)(2,1)S(1)}, bf16[100,256]{1,0:T(8,128)(2,1)S(1)}, u32[]{:S(2)}, u32[]{:S(2)}) collective-permute-start(bf16[100,256]{1,0:T(8,128)(2,1)S(1)} %add_convert_fusion.4), channel_id=1, source_target_pairs={{0,24},{2,26},{4,28},{6,30},{8,16},{10,18},{12,20},{14,22},{16,8},... | collective-permute-start | bytes 153608 | tf_op jit(solution)/shard_map/ppermute | solution.py:858
  136.6 1.8 %collective-permute-start.11 = (bf16[100,256]{1,0:T(8,128)(2,1)S(1)}, bf16[100,256]{1,0:T(8,128)(2,1)S(1)}, u32[]{:S(2)}, u32[]{:S(2)}) collective-permute-start(bf16[100,256]{1,0:T(8,128)(2,1)S(1)} %add_convert_fusion.5), channel_id=1, source_target_pairs={{0,8},{2,10},{4,12},{6,14},{8,0},{10,2},{12,4},{14,6},{16,24},{18,... | collective-permute-start | bytes 153608 | tf_op jit(solution)/shard_map/ppermute | solution.py:858
  138.3 1.9 %collective-permute-start.9 = (bf16[100,256]{1,0:T(8,128)(2,1)S(1)}, bf16[100,256]{1,0:T(8,128)(2,1)S(1)}, u32[]{:S(2)}, u32[]{:S(2)}) collective-permute-start(bf16[100,256]{1,0:T(8,128)(2,1)S(1)} %add_convert_fusion.5), channel_id=1, source_target_pairs={{0,24},{2,26},{4,28},{6,30},{8,16},{10,18},{12,20},{14,22},{16,8},... | collective-permute-start | bytes 153608 | tf_op jit(solution)/shard_map/ppermute | solution.py:858
  140.2 2.8 %collective-permute-done.24 = bf16[100,256]{1,0:T(8,128)(2,1)S(1)} collective-permute-done((bf16[100,256]{1,0:T(8,128)(2,1)S(1)}, bf16[100,256]{1,0:T(8,128)(2,1)S(1)}, u32[]{:S(2)}, u32[]{:S(2)}) %collective-permute-start.24) | collective-permute-done | bytes 51232 | tf_op jit(solution)/shard_map/ppermute | solution.py:858
  143.2 1.6 collective-permute-start.28
  145.7 1.0 collective-permute-start.26
  146.9 1.6 collective-permute-start.14
  149.4 2.4 %copy_bitcast_fusion.1 = (bf16[522,4,256]{2,1,0:T(4,128)(2,1)}, bf16[522,4,256]{2,1,0:T(4,128)(2,1)}) fusion(bf16[4,522,256]{2,1,0:T(8,128)(2,1)S(1)} %copy-done.19, bf16[4,522,256]{2,1,0:T(8,128)(2,1)S(1)} %copy-done.18), kind=kLoop, calls=%fused_computation.3 | loop fusion | bytes 4276224 | tf_op jit(solution)/shard_map/transpose | solution.py:894
  153.2 3.8 %collective-permute-done.27 = bf16[400,256]{1,0:T(8,128)(2,1)S(1)} collective-permute-done((bf16[400,256]{1,0:T(8,128)(2,1)S(1)}, bf16[400,256]{1,0:T(8,128)(2,1)S(1)}, u32[]{:S(2)}, u32[]{:S(2)}) %collective-permute-start.27) | collective-permute-done | bytes 204832 | tf_op jit(solution)/shard_map/ppermute | solution.py:884
  157.2 2.0 %collective-permute-done.14 = bf16[400,256]{1,0:T(8,128)(2,1)S(1)} collective-permute-done((bf16[400,256]{1,0:T(8,128)(2,1)S(1)}, bf16[400,256]{1,0:T(8,128)(2,1)S(1)}, u32[]{:S(2)}, u32[]{:S(2)}) %collective-permute-start.14) | collective-permute-done | bytes 204832 | tf_op jit(solution)/shard_map/ppermute | solution.py:884
  159.2 2.0 %collective-permute-done.13 = bf16[400,256]{1,0:T(8,128)(2,1)S(1)} collective-permute-done((bf16[400,256]{1,0:T(8,128)(2,1)S(1)}, bf16[400,256]{1,0:T(8,128)(2,1)S(1)}, u32[]{:S(2)}, u32[]{:S(2)}) %collective-permute-start.13) | collective-permute-done | bytes 204832 | tf_op jit(solution)/shard_map/ppermute | solution.py:884
  161.4 2.3 %collective-permute-done.15.refs_1_ = bf16[1600,256]{1,0:T(8,128)(2,1)S(1)} collective-permute-done((bf16[1600,256]{1,0:T(8,128)(2,1)S(1)}, bf16[1600,256]{1,0:T(8,128)(2,1)S(1)}, u32[]{:S(2)}, u32[]{:S(2)}) %collective-permute-start.15) | collective-permute-done | bytes 819232 | tf_op jit(solution)/shard_map/ppermute | solution.py:839
  163.7 4.2 %unpack.1 = (f32[2,256,256]{2,1,0:T(8,128)}, f32[2,256]{1,0:T(2,128)}, f32[2,256,256]{2,1,0:T(8,128)}, f32[2,256,256]{2,1,0:T(8,128)}, f32[2,256]{1,0:T(2,128)},...) custom-call(bf16[1600,256]{1,0:T(8,128)(2,1)S(1)} %pad_maximum_fusio, ...), custom_call_target="tpu_custom_call" | custom-call | tf_op jit(solution)/shard_map/unpack/pallas_call | solution.py:818
  (99 shorter events, 8.6 us)
Async XLA Ops:
  23.4 3.4 %collective-permute-start = (bf16[4,16,256]{2,1,0:T(8,128)(2,1)}, bf16[4,16,256]{2,1,0:T(8,128)(2,1)S(1)}, u32[]{:S(2)}, u32[]{:S(2)}) collective-permute-start(bf16[4,16,256]{2,1,0:T(8,128)(2,1)} %get-tuple-element.64), channel_id=1, source_target_pairs={{0,2},{2,4},{4,6},{6,8},{8,10},{10,12},{12,14},{14,16},{16,18},{18... | collective-permute-start | bytes 98312 | tf_op jit(solution)/shard_map/ppermute | solution.py:834
  27.0 45.7 %copy-start.4 = (bf16[4,528,64]{2,1,0:T(8,128)(2,1)S(1)}, bf16[4,528,64]{2,1,0:T(8,128)(2,1)}, u32[]{:S(2)}) copy-start(bf16[4,528,64]{2,1,0:T(8,128)(2,1)} %get-tuple-element.73.refs_20_) | copy-start | bytes 811012
  27.0 45.7 %copy-start.7 = (f32[4,4,512]{2,1,0:T(4,128)S(1)}, f32[4,4,512]{2,1,0:T(4,128)}, u32[]{:S(2)}) copy-start(f32[4,4,512]{2,1,0:T(4,128)} %get-tuple-element.74.refs_21_) | copy-start | bytes 98308
  66.7 37.6 %collective-permute-start.16 = (bf16[1600,256]{1,0:T(8,128)(2,1)}, bf16[1600,256]{1,0:T(8,128)(2,1)S(1)}, u32[]{:S(2)}, u32[]{:S(2)}) collective-permute-start(bf16[1600,256]{1,0:T(8,128)(2,1)} %get-tuple-element.93), channel_id=1, source_target_pairs={{0,2},{2,0},{4,6},{6,4},{8,10},{10,8},{12,14},{14,12},{16,18},{18,... | collective-permute-start | bytes 2457608 | tf_op jit(solution)/shard_map/ppermute | solution.py:839
  69.6 3.1 %collective-permute-start.1 = (bf16[4,16,256]{2,1,0:T(8,128)(2,1)S(1)}, bf16[4,16,256]{2,1,0:T(8,128)(2,1)S(1)}, u32[]{:S(2)}, u32[]{:S(2)}) collective-permute-start(bf16[4,16,256]{2,1,0:T(8,128)(2,1)S(1)} %get-tuple-element.67), channel_id=1, source_target_pairs={{2,0},{4,2},{6,4},{8,6},{10,8},{12,10},{14,12},{16,14},{18,16},{20... | collective-permute-start | bytes 98312 | tf_op jit(solution)/shard_map/ppermute | solution.py:834
  101.5 7.6 %collective-permute-start.2 = (bf16[1600,256]{1,0:T(8,128)(2,1)}, bf16[1600,256]{1,0:T(8,128)(2,1)S(1)}, u32[]{:S(2)}, u32[]{:S(2)}) collective-permute-start(bf16[1600,256]{1,0:T(8,128)(2,1)} %get-tuple-element.85), channel_id=1, source_target_pairs={{0,2},{2,0},{4,6},{6,4},{8,10},{10,8},{12,14},{14,12},{16,18},{18,... | collective-permute-start | bytes 2457608 | tf_op jit(solution)/shard_map/ppermute | solution.py:839
  104.5 9.9 %collective-permute-start.19 = (bf16[400,256]{1,0:T(8,128)(2,1)S(1)}, bf16[400,256]{1,0:T(8,128)(2,1)S(1)}, u32[]{:S(2)}, u32[]{:S(2)}) collective-permute-start(bf16[400,256]{1,0:T(8,128)(2,1)S(1)} %get-tuple-element.110), channel_id=1, source_target_pairs={{0,5},{1,4},{2,7},{3,6},{4,1},{5,0},{6,3},{7,2},{8,13},{9,12},{10,... | collective-permute-start | bytes 614408 | tf_op jit(solution)/shard_map/ppermute | solution.py:884
  108.5 10.4 %collective-permute-start.18 = (bf16[400,256]{1,0:T(8,128)(2,1)S(1)}, bf16[400,256]{1,0:T(8,128)(2,1)S(1)}, u32[]{:S(2)}, u32[]{:S(2)}) collective-permute-start(bf16[400,256]{1,0:T(8,128)(2,1)S(1)} %get-tuple-element.111), channel_id=1, source_target_pairs={{0,4},{1,5},{2,6},{3,7},{4,0},{5,1},{6,2},{7,3},{8,12},{9,13},{10,... | collective-permute-start | bytes 614408 | tf_op jit(solution)/shard_map/ppermute | solution.py:884
  108.5 10.9 %collective-permute-start.17 = (bf16[400,256]{1,0:T(8,128)(2,1)S(1)}, bf16[400,256]{1,0:T(8,128)(2,1)S(1)}, u32[]{:S(2)}, u32[]{:S(2)}) collective-permute-start(bf16[400,256]{1,0:T(8,128)(2,1)S(1)} %get-tuple-element.109), channel_id=1, source_target_pairs={{0,1},{1,0},{2,3},{3,2},{4,5},{5,4},{6,7},{7,6},{8,9},{9,8},{10,11... | collective-permute-start | bytes 614408 | tf_op jit(solution)/shard_map/ppermute | solution.py:884
  109.5 13.8 %collective-permute-start.5 = (bf16[400,256]{1,0:T(8,128)(2,1)S(1)}, bf16[400,256]{1,0:T(8,128)(2,1)S(1)}, u32[]{:S(2)}, u32[]{:S(2)}) collective-permute-start(bf16[400,256]{1,0:T(8,128)(2,1)S(1)} %get-tuple-element.113), channel_id=1, source_target_pairs={{0,5},{1,4},{2,7},{3,6},{4,1},{5,0},{6,3},{7,2},{8,13},{9,12},{10,... | collective-permute-start | bytes 614408 | tf_op jit(solution)/shard_map/ppermute | solution.py:884
  112.4 14.7 %collective-permute-start.4 = (bf16[400,256]{1,0:T(8,128)(2,1)S(1)}, bf16[400,256]{1,0:T(8,128)(2,1)S(1)}, u32[]{:S(2)}, u32[]{:S(2)}) collective-permute-start(bf16[400,256]{1,0:T(8,128)(2,1)S(1)} %get-tuple-element.114), channel_id=1, source_target_pairs={{0,4},{1,5},{2,6},{3,7},{4,0},{5,1},{6,2},{7,3},{8,12},{9,13},{10,... | collective-permute-start | bytes 614408 | tf_op jit(solution)/shard_map/ppermute | solution.py:884
  114.4 12.9 %collective-permute-start.3 = (bf16[400,256]{1,0:T(8,128)(2,1)S(1)}, bf16[400,256]{1,0:T(8,128)(2,1)S(1)}, u32[]{:S(2)}, u32[]{:S(2)}) collective-permute-start(bf16[400,256]{1,0:T(8,128)(2,1)S(1)} %get-tuple-element.112), channel_id=1, source_target_pairs={{0,1},{1,0},{2,3},{3,2},{4,5},{5,4},{6,7},{7,6},{8,9},{9,8},{10,11... | collective-permute-start | bytes 614408 | tf_op jit(solution)/shard_map/ppermute | solution.py:884
  119.6 11.5 %collective-permute-start.22 = (bf16[100,256]{1,0:T(8,128)(2,1)S(1)}, bf16[100,256]{1,0:T(8,128)(2,1)S(1)}, u32[]{:S(2)}, u32[]{:S(2)}) collective-permute-start(bf16[100,256]{1,0:T(8,128)(2,1)S(1)} %get-tuple-element.116), channel_id=1, source_target_pairs={{0,24},{2,26},{4,28},{6,30},{8,16},{10,18},{12,20},{14,22},{16,8},... | collective-permute-start | bytes 153608 | tf_op jit(solution)/shard_map/ppermute | solution.py:858
  123.2 8.8 %collective-permute-start.21 = (bf16[100,256]{1,0:T(8,128)(2,1)S(1)}, bf16[100,256]{1,0:T(8,128)(2,1)S(1)}, u32[]{:S(2)}, u32[]{:S(2)}) collective-permute-start(bf16[100,256]{1,0:T(8,128)(2,1)S(1)} %get-tuple-element.117), channel_id=1, source_target_pairs={{0,16},{2,18},{4,20},{6,22},{8,24},{10,26},{12,28},{14,30},{16,0},... | collective-permute-start | bytes 153608 | tf_op jit(solution)/shard_map/ppermute | solution.py:858
  123.3 8.8 %collective-permute-start.20 = (bf16[100,256]{1,0:T(8,128)(2,1)S(1)}, bf16[100,256]{1,0:T(8,128)(2,1)S(1)}, u32[]{:S(2)}, u32[]{:S(2)}) collective-permute-start(bf16[100,256]{1,0:T(8,128)(2,1)S(1)} %get-tuple-element.115), channel_id=1, source_target_pairs={{0,8},{2,10},{4,12},{6,14},{8,0},{10,2},{12,4},{14,6},{16,24},{18,... | collective-permute-start | bytes 153608 | tf_op jit(solution)/shard_map/ppermute | solution.py:858
  127.6 8.1 %collective-permute-start.8 = (bf16[100,256]{1,0:T(8,128)(2,1)S(1)}, bf16[100,256]{1,0:T(8,128)(2,1)S(1)}, u32[]{:S(2)}, u32[]{:S(2)}) collective-permute-start(bf16[100,256]{1,0:T(8,128)(2,1)S(1)} %get-tuple-element.119), channel_id=1, source_target_pairs={{0,24},{2,26},{4,28},{6,30},{8,16},{10,18},{12,20},{14,22},{16,8},... | collective-permute-start | bytes 153608 | tf_op jit(solution)/shard_map/ppermute | solution.py:858
  131.1 5.4 %collective-permute-start.7 = (bf16[100,256]{1,0:T(8,128)(2,1)S(1)}, bf16[100,256]{1,0:T(8,128)(2,1)S(1)}, u32[]{:S(2)}, u32[]{:S(2)}) collective-permute-start(bf16[100,256]{1,0:T(8,128)(2,1)S(1)} %get-tuple-element.120), channel_id=1, source_target_pairs={{0,16},{2,18},{4,20},{6,22},{8,24},{10,26},{12,28},{14,30},{16,0},... | collective-permute-start | bytes 153608 | tf_op jit(solution)/shard_map/ppermute | solution.py:858
  131.1 5.4 %collective-permute-start.6 = (bf16[100,256]{1,0:T(8,128)(2,1)S(1)}, bf16[100,256]{1,0:T(8,128)(2,1)S(1)}, u32[]{:S(2)}, u32[]{:S(2)}) collective-permute-start(bf16[100,256]{1,0:T(8,128)(2,1)S(1)} %get-tuple-element.118), channel_id=1, source_target_pairs={{0,8},{2,10},{4,12},{6,14},{8,0},{10,2},{12,4},{14,6},{16,24},{18,... | collective-permute-start | bytes 153608 | tf_op jit(solution)/shard_map/ppermute | solution.py:858
  132.1 8.1 %collective-permute-start.25 = (bf16[100,256]{1,0:T(8,128)(2,1)S(1)}, bf16[100,256]{1,0:T(8,128)(2,1)S(1)}, u32[]{:S(2)}, u32[]{:S(2)}) collective-permute-start(bf16[100,256]{1,0:T(8,128)(2,1)S(1)} %add_convert_fusion.4), channel_id=1, source_target_pairs={{0,8},{2,10},{4,12},{6,14},{8,0},{10,2},{12,4},{14,6},{16,24},{18,... | collective-permute-start | bytes 153608 | tf_op jit(solution)/shard_map/ppermute | solution.py:858
  133.2 7.0 %collective-permute-start.23 = (bf16[100,256]{1,0:T(8,128)(2,1)S(1)}, bf16[100,256]{1,0:T(8,128)(2,1)S(1)}, u32[]{:S(2)}, u32[]{:S(2)}) collective-permute-start(bf16[100,256]{1,0:T(8,128)(2,1)S(1)} %add_convert_fusion.4), channel_id=1, source_target_pairs={{0,24},{2,26},{4,28},{6,30},{8,16},{10,18},{12,20},{14,22},{16,8},... | collective-permute-start | bytes 153608 | tf_op jit(solution)/shard_map/ppermute | solution.py:858
  135.7 7.4 %collective-permute-start.24 = (bf16[100,256]{1,0:T(8,128)(2,1)S(1)}, bf16[100,256]{1,0:T(8,128)(2,1)S(1)}, u32[]{:S(2)}, u32[]{:S(2)}) collective-permute-start(bf16[100,256]{1,0:T(8,128)(2,1)S(1)} %add_convert_fusion.4), channel_id=1, source_target_pairs={{0,16},{2,18},{4,20},{6,22},{8,24},{10,26},{12,28},{14,30},{16,0},... | collective-permute-start | bytes 153608 | tf_op jit(solution)/shard_map/ppermute | solution.py:858
  136.6 9.2 %collective-permute-start.11 = (bf16[100,256]{1,0:T(8,128)(2,1)S(1)}, bf16[100,256]{1,0:T(8,128)(2,1)S(1)}, u32[]{:S(2)}, u32[]{:S(2)}) collective-permute-start(bf16[100,256]{1,0:T(8,128)(2,1)S(1)} %add_convert_fusion.5), channel_id=1, source_target_pairs={{0,8},{2,10},{4,12},{6,14},{8,0},{10,2},{12,4},{14,6},{16,24},{18,... | collective-permute-start | bytes 153608 | tf_op jit(solution)/shard_map/ppermute | solution.py:858
  138.3 8.4 %collective-permute-start.9 = (bf16[100,256]{1,0:T(8,128)(2,1)S(1)}, bf16[100,256]{1,0:T(8,128)(2,1)S(1)}, u32[]{:S(2)}, u32[]{:S(2)}) collective-permute-start(bf16[100,256]{1,0:T(8,128)(2,1)S(1)} %add_convert_fusion.5), channel_id=1, source_target_pairs={{0,24},{2,26},{4,28},{6,30},{8,16},{10,18},{12,20},{14,22},{16,8},... | collective-permute-start | bytes 153608 | tf_op jit(solution)/shard_map/ppermute | solution.py:858
  140.2 6.6 %collective-permute-start.10 = (bf16[100,256]{1,0:T(8,128)(2,1)S(1)}, bf16[100,256]{1,0:T(8,128)(2,1)S(1)}, u32[]{:S(2)}, u32[]{:S(2)}) collective-permute-start(bf16[100,256]{1,0:T(8,128)(2,1)S(1)} %add_convert_fusion.5), channel_id=1, source_target_pairs={{0,16},{2,18},{4,20},{6,22},{8,24},{10,26},{12,28},{14,30},{16,0},... | collective-permute-start | bytes 153608 | tf_op jit(solution)/shard_map/ppermute | solution.py:858
  143.2 9.1 %collective-permute-start.28 = (bf16[400,256]{1,0:T(8,128)(2,1)S(1)}, bf16[400,256]{1,0:T(8,128)(2,1)S(1)}, u32[]{:S(2)}, u32[]{:S(2)}) collective-permute-start(bf16[400,256]{1,0:T(8,128)(2,1)S(1)} %maximum_select_fusion.1), channel_id=1, source_target_pairs={{0,5},{1,4},{2,7},{3,6},{4,1},{5,0},{6,3},{7,2},{8,13},{9,12},{10,... | collective-permute-start | bytes 614408 | tf_op jit(solution)/shard_map/ppermute | solution.py:884
  144.8 12.3 %collective-permute-start.27 = (bf16[400,256]{1,0:T(8,128)(2,1)S(1)}, bf16[400,256]{1,0:T(8,128)(2,1)S(1)}, u32[]{:S(2)}, u32[]{:S(2)}) collective-permute-start(bf16[400,256]{1,0:T(8,128)(2,1)S(1)} %maximum_select_fusion.1), channel_id=1, source_target_pairs={{0,4},{1,5},{2,6},{3,7},{4,0},{5,1},{6,2},{7,3},{8,12},{9,13},{10,... | collective-permute-start | bytes 614408 | tf_op jit(solution)/shard_map/ppermute | solution.py:884
  145.7 11.3 %collective-permute-start.26 = (bf16[400,256]{1,0:T(8,128)(2,1)S(1)}, bf16[400,256]{1,0:T(8,128)(2,1)S(1)}, u32[]{:S(2)}, u32[]{:S(2)}) collective-permute-start(bf16[400,256]{1,0:T(8,128)(2,1)S(1)} %maximum_select_fusion.1), channel_id=1, source_target_pairs={{0,1},{1,0},{2,3},{3,2},{4,5},{5,4},{6,7},{7,6},{8,9},{9,8},{10,11... | collective-permute-start | bytes 614408 | tf_op jit(solution)/shard_map/ppermute | solution.py:884
  146.9 12.3 %collective-permute-start.14 = (bf16[400,256]{1,0:T(8,128)(2,1)S(1)}, bf16[400,256]{1,0:T(8,128)(2,1)S(1)}, u32[]{:S(2)}, u32[]{:S(2)}) collective-permute-start(bf16[400,256]{1,0:T(8,128)(2,1)S(1)} %maximum_select_fusion), channel_id=1, source_target_pairs={{0,5},{1,4},{2,7},{3,6},{4,1},{5,0},{6,3},{7,2},{8,13},{9,12},{10,... | collective-permute-start | bytes 614408 | tf_op jit(solution)/shard_map/ppermute | solution.py:884
  148.5 12.7 %collective-permute-start.13 = (bf16[400,256]{1,0:T(8,128)(2,1)S(1)}, bf16[400,256]{1,0:T(8,128)(2,1)S(1)}, u32[]{:S(2)}, u32[]{:S(2)}) collective-permute-start(bf16[400,256]{1,0:T(8,128)(2,1)S(1)} %maximum_select_fusion), channel_id=1, source_target_pairs={{0,4},{1,5},{2,6},{3,7},{4,0},{5,1},{6,2},{7,3},{8,12},{9,13},{10,... | collective-permute-start | bytes 614408 | tf_op jit(solution)/shard_map/ppermute | solution.py:884
  152.3 9.0 %collective-permute-start.12 = (bf16[400,256]{1,0:T(8,128)(2,1)S(1)}, bf16[400,256]{1,0:T(8,128)(2,1)S(1)}, u32[]{:S(2)}, u32[]{:S(2)}) collective-permute-start(bf16[400,256]{1,0:T(8,128)(2,1)S(1)} %maximum_select_fusion), channel_id=1, source_target_pairs={{0,1},{1,0},{2,3},{3,2},{4,5},{5,4},{6,7},{7,6},{8,9},{9,8},{10,11... | collective-permute-start | bytes 614408 | tf_op jit(solution)/shard_map/ppermute | solution.py:884
  157.1 4.2 %collective-permute-start.29 = (bf16[1600,256]{1,0:T(8,128)(2,1)S(1)}, bf16[1600,256]{1,0:T(8,128)(2,1)S(1)}, u32[]{:S(2)}, u32[]{:S(2)}) collective-permute-start(bf16[1600,256]{1,0:T(8,128)(2,1)S(1)} %pad_maximum_fusion.1.refs_2_), channel_id=1, source_target_pairs={{0,2},{2,0},{4,6},{6,4},{8,10},{10,8},{12,14},{14,12},{16,18},{18,... | collective-permute-start | bytes 2457608 | tf_op jit(solution)/shard_map/ppermute | solution.py:839
  161.3 2.4 %collective-permute-start.15 = (bf16[1600,256]{1,0:T(8,128)(2,1)S(1)}, bf16[1600,256]{1,0:T(8,128)(2,1)S(1)}, u32[]{:S(2)}, u32[]{:S(2)}) collective-permute-start(bf16[1600,256]{1,0:T(8,128)(2,1)S(1)} %pad_maximum_fusion.refs_0_), channel_id=1, source_target_pairs={{0,2},{2,0},{4,6},{6,4},{8,10},{10,8},{12,14},{14,12},{16,18},{18,... | collective-permute-start | bytes 2457608 | tf_op jit(solution)/shard_map/ppermute | solution.py:839
  (21 other events, 493.0 us)

commit v6 on v5

--- a/solution.py
+++ b/solution.py
@@ -581,7 +581,7 @@
         out_specs=[by_micro(o.shape) for o in outs],
         out_shape=outs,
         scratch_shapes=[pltpu.VMEM((full, features), BF16)],
-        compiler_params=pltpu.CompilerParams(vmem_limit_bytes=60 * 2**20),
+        compiler_params=pltpu.CompilerParams(vmem_limit_bytes=56 * 2**20),
         name="lower_forward",
     )(hidden, *weights)
     return out, sent, Stash(*stash)
@@ -760,12 +760,14 @@
 def unpack_kernel(bits, *refs):
     sources, refs = refs[:4], refs[4:]
     out, refs = Weights(*refs[: len(Weights._fields)]), refs[len(Weights._fields) :]
-    ordered, *staged, in_sems, out_sems = refs
+    ordered, *staged, in_sems, out_sems, line_sems = refs
     features, units = out.w_up.shape[1:]
     chunks = units // features
     half = sources[0].shape[0]
     rows, piece = 2 * half, 2 * half // PIECES
     arrays = squares(out) + (out.w_up, out.w_down)
+    names = lines(out) + (out.b_up,)
+    short = staged[len(arrays) :]
     loads = [
         pltpu.make_async_copy(source, ordered.at[i // 2, (i % 2) * half : (i % 2 + 1) * half], in_sems.at[i])
         for i, source in enumerate(sources)
@@ -797,32 +799,37 @@
                 staged[index][layer, start : start + take, :] = value.astype(F32)
             else:
                 value = value.astype(F32)
-                names = lines(out)
-                for i, ref in enumerate(names):
+                for i, ref in enumerate(short[:-1]):
                     ref[pl.ds(layer, 1), :] = value[i : i + 1]
                 for c in range(chunks):
-                    i = len(names) + c
-                    out.b_up[pl.ds(layer, 1), c * features : (c + 1) * features] = value[i : i + 1]
+                    i = len(short) - 1 + c
+                    short[-1][pl.ds(layer, 1), c * features : (c + 1) * features] = value[i : i + 1]
             if index < 6 and start + take == sizes[index]:
                 store(index, layer).start()
 
+    line_stores = [pltpu.make_async_copy(near, far, line_sems.at[i]) for i, (near, far) in enumerate(zip(short, names))]
+    for copy in line_stores:
+        copy.start()
     for layer in range(2):
         for index in range(6):
             store(index, layer).wait()
+    for copy in line_stores:
+        copy.wait()
 
 
 def unpack(bits, parts, weights):
     outs = [jax.ShapeDtypeStruct(weight.shape, F32) for weight in weights]
     shapes = Weights(*outs)
     large = squares(shapes) + (shapes.w_up, shapes.w_down)
+    short = lines(shapes) + (shapes.b_up,)
     return pl.pallas_call(
         functools.partial(unpack_kernel, bits),
         in_specs=[pl.BlockSpec(memory_space=pl.ANY)] * 4,
-        out_specs=[pl.BlockSpec(memory_space=pl.ANY if len(o.shape) == 3 else pltpu.VMEM) for o in outs],
+        out_specs=[pl.BlockSpec(memory_space=pl.ANY) for _ in outs],
         out_shape=outs,
         scratch_shapes=[pltpu.VMEM((2, 2 * parts[0].shape[0], parts[0].shape[1]), BF16)]
-        + [pltpu.VMEM(o.shape, F32) for o in large]
-        + [pltpu.SemaphoreType.DMA((4,)), pltpu.SemaphoreType.DMA((2, 6))],
+        + [pltpu.VMEM(o.shape, F32) for o in large + short]
+        + [pltpu.SemaphoreType.DMA((4,)), pltpu.SemaphoreType.DMA((2, 6)), pltpu.SemaphoreType.DMA((len(short),))],
         compiler_params=pltpu.CompilerParams(vmem_limit_bytes=20 * 2**20),
         name="unpack",
     )(*parts)
@@ -886,7 +893,7 @@
     chains = [plus(keep, swap(send, core)) for keep, send in halves]
     rows = chains[0].shape[0] // 4
     for i, kept in enumerate(chains):
-        got = [to(kept[j * rows : (j + 1) * rows], j) for j in (1, 2, 3)]
+        got = [to(kept[j * rows : (j + 1) * rows], j) for j in (3, 1, 2)]
         chains[i] = sum([part.astype(F32) for part in got], kept[:rows].astype(F32)).astype(BF16)
     chains = [sum_rest(kept, rest_bits) for kept in chains]
     others, chains[0] = lax.optimization_barrier((others, chains[0]))

time: 168 us -> 167 us (level)
  waiting for transfers between devices: 24.8 us -> 21 us
  starting transfers between devices: 42.9 us -> 46.3 us
    ppermute x12, starting transfers between devices: 15.2 us -> 19.7 us  [to(): return lax.ppermute(part, (LINE, PAIR), perm)]
    ppermute x12, waiting for transfers between devices: 16.7 us -> 13 us  [to(): return lax.ppermute(part, (LINE, PAIR), perm)]
  transfers between devices with their start and end apart: 30 -> 30, of which waited for: 13 -> 12; matrix products, arithmetic and copies ran while one was open for 2% -> 2% of each run, Pallas kernels for 17% -> 17%
where the time goes in v6:
time: 167 us
  Pallas kernels  92.4 us (55%)
  starting transfers between devices  46.3 us (28%)
  waiting for transfers between devices  21 us (13%)
  local copies, waits for them, and re-layouts  5.1 us (3%)
    pallas_call x1, Pallas kernels, upper_both(): pl.pallas_call(functools.partial(upper_kernel, rows, micro, bits), grid=(...  39.7 us
    pallas_call x1, Pallas kernels, lower_backward(): pl.pallas_call(functools.partial(lower_backward_kernel, memory, bits), gr...  28.8 us
    pallas_call x1, Pallas kernels, lower_forward(): pl.pallas_call(lower_forward_kernel, grid=(micro,), in_specs=[by_micro(hi...  20.3 us
    ppermute x12, starting transfers between devices, to(): return lax.ppermute(part, (LINE, PAIR), perm)  19.7 us
    ppermute x12, starting transfers between devices, across(): lax.ppermute(part, axis, [(i, i ^ k * step) for i in range(lax.axis_size(...  17.2 us
    ppermute x12, waiting for transfers between devices, to(): return lax.ppermute(part, (LINE, PAIR), perm)  13 us
    ppermute x4, starting transfers between devices, swap(): lax.ppermute(value, axis, [(i, i ^ step) for i in range(lax.axis_size(axi...  5.81 us
    pallas_call x1, Pallas kernels, unpack(): pl.pallas_call(functools.partial(unpack_kernel, bits), in_specs=[pl.Block...  3.72 us
  transfers between devices with their start and end apart: 30, of which 12 were waited for; matrix products, arithmetic and copies ran while one was open for 2% of the time, Pallas kernels for 17%

profile of v6, /device:TPU:0, one launch (start us, length us, event | category | flops | bytes accessed | tf_op | source)
XLA Modules:
  0.0 167.3 jit_solution(9174907116434288503)
XLA Ops:
  0.7 2.4 %copy.45 = bf16[4,1,1,522,256]{4,3,0,2,1:T(8,128)(2,1)} copy(bf16[4,1,1,522,256]{4,0,3,2,1:T(4,128)(2,1)} %param.20) | data formatting | bytes 2138112 | tf_op args[0]
  3.2 20.3 %lower_forward.1 = (bf16[4,528,256]{2,1,0:T(8,128)(2,1)}, bf16[4,16,256]{2,1,0:T(8,128)(2,1)}, bf16[4,528,256]{2,1,0:T(8,128)(2,1)}, bf16[4,528,256]{2,1,0:T(8,1...) custom-call(bf16[4,522,256]{2,1,0:T(8,128)(2,1)} %bitcast.23, ...), custom_call_target="tpu_custom_call" | custom-call | tf_op jit(solution)/shard_map/lower_forward/pallas_call | solution.py:577
  23.4 2.4 %collective-permute-start = (bf16[4,16,256]{2,1,0:T(8,128)(2,1)}, bf16[4,16,256]{2,1,0:T(8,128)(2,1)S(1)}, u32[]{:S(2)}, u32[]{:S(2)}) collective-permute-start(bf16[4,16,256]{2,1,0:T(8,128)(2,1)} %get-tuple-element.64), channel_id=1, source_target_pairs={{0,2},{2,4},{4,6},{6,8},{8,10},{10,12},{12,14},{14,16},{16,18},{18... | collective-permute-start | bytes 98312 | tf_op jit(solution)/shard_map/ppermute | solution.py:841
  27.0 39.7 %upper_both.1 = (bf16[4,522,256]{2,1,0:T(8,128)(2,1)}, f32[4,528,256]{2,1,0:T(8,128)}, bf16[4,16,256]{2,1,0:T(8,128)(2,1)S(1)}, bf16[1600,256]{1,0:T(8,128)(2,1)}, bf16[1600,256]{1,0:T(8,128)(2,1)}) custom-call(s32[4]{0:T(128)S(1)} %bitcast.22, bf16[4,528,256]{2,1,0:T(8,128)(2,1)} %get-tuple-element.63.x_ref, ...), custom_call_target="tpu_custom_call" | custom-call | tf_op jit(solution)/shard_map/upper_both/pallas_call | solution.py:699
  66.7 3.0 %collective-permute-start.16 = (bf16[1600,256]{1,0:T(8,128)(2,1)}, bf16[1600,256]{1,0:T(8,128)(2,1)S(1)}, u32[]{:S(2)}, u32[]{:S(2)}) collective-permute-start(bf16[1600,256]{1,0:T(8,128)(2,1)} %get-tuple-element.93), channel_id=1, source_target_pairs={{0,2},{2,0},{4,6},{6,4},{8,10},{10,8},{12,14},{14,12},{16,18},{18,... | collective-permute-start | bytes 2457608 | tf_op jit(solution)/shard_map/ppermute | solution.py:846
  69.6 1.3 collective-permute-start.1
  70.9 1.8 %collective-permute-done.1.back_ref = bf16[4,16,256]{2,1,0:T(8,128)(2,1)S(1)} collective-permute-done((bf16[4,16,256]{2,1,0:T(8,128)(2,1)S(1)}, bf16[4,16,256]{2,1,0:T(8,128)(2,1)S(1)}, u32[]{:S(2)}, u32[]{:S(2)}) %collective-permute-start.1) | collective-permute-done | bytes 32800 | tf_op jit(solution)/shard_map/ppermute | solution.py:841
  72.7 28.8 %lower_backward.1 = (bf16[4,522,256]{2,1,0:T(8,128)(2,1)}, bf16[1600,256]{1,0:T(8,128)(2,1)}, bf16[1600,256]{1,0:T(8,128)(2,1)}) custom-call(f32[4,528,256]{2,1,0:T(8,128)} %get-tuple-element.66.grad_ref, bf16[4,16,256]{2,1,0:T(8,128)(2,1)S(1)} %collective-permute-done.1.back_ref, bf16[2,256,256]{2,1,0:T(8,128)(2,1)S(1)} %copy-done, f32[2,256]{1,0:T(2,128)S(1)} %copy-done.8, ...), custom_call_target="tpu_custom_call" | custom-call | tf_op jit(solution)/shard_map/lower_backward/pallas_call | solution.py:746
  101.5 2.7 %collective-permute-start.2 = (bf16[1600,256]{1,0:T(8,128)(2,1)}, bf16[1600,256]{1,0:T(8,128)(2,1)S(1)}, u32[]{:S(2)}, u32[]{:S(2)}) collective-permute-start(bf16[1600,256]{1,0:T(8,128)(2,1)} %get-tuple-element.85), channel_id=1, source_target_pairs={{0,2},{2,0},{4,6},{6,4},{8,10},{10,8},{12,14},{14,12},{16,18},{18,... | collective-permute-start | bytes 2457608 | tf_op jit(solution)/shard_map/ppermute | solution.py:846
  104.5 3.1 %collective-permute-start.19 = (bf16[400,256]{1,0:T(8,128)(2,1)S(1)}, bf16[400,256]{1,0:T(8,128)(2,1)S(1)}, u32[]{:S(2)}, u32[]{:S(2)}) collective-permute-start(bf16[400,256]{1,0:T(8,128)(2,1)S(1)} %get-tuple-element.110), channel_id=1, source_target_pairs={{0,4},{1,5},{2,6},{3,7},{4,0},{5,1},{6,2},{7,3},{8,12},{9,13},{10,... | collective-permute-start | bytes 614408 | tf_op jit(solution)/shard_map/ppermute | solution.py:891
  107.6 1.5 collective-permute-start.18
  109.4 2.0 %collective-permute-start.5 = (bf16[400,256]{1,0:T(8,128)(2,1)S(1)}, bf16[400,256]{1,0:T(8,128)(2,1)S(1)}, u32[]{:S(2)}, u32[]{:S(2)}) collective-permute-start(bf16[400,256]{1,0:T(8,128)(2,1)S(1)} %get-tuple-element.113), channel_id=1, source_target_pairs={{0,4},{1,5},{2,6},{3,7},{4,0},{5,1},{6,2},{7,3},{8,12},{9,13},{10,... | collective-permute-start | bytes 614408 | tf_op jit(solution)/shard_map/ppermute | solution.py:891
  111.4 1.5 collective-permute-start.4
  113.5 3.7 %collective-permute-start.3 = (bf16[400,256]{1,0:T(8,128)(2,1)S(1)}, bf16[400,256]{1,0:T(8,128)(2,1)S(1)}, u32[]{:S(2)}, u32[]{:S(2)}) collective-permute-start(bf16[400,256]{1,0:T(8,128)(2,1)S(1)} %get-tuple-element.112), channel_id=1, source_target_pairs={{0,5},{1,4},{2,7},{3,6},{4,1},{5,0},{6,3},{7,2},{8,13},{9,12},{10,... | collective-permute-start | bytes 614408 | tf_op jit(solution)/shard_map/ppermute | solution.py:891
  117.2 2.2 %collective-permute-done.17 = bf16[400,256]{1,0:T(8,128)(2,1)S(1)} collective-permute-done((bf16[400,256]{1,0:T(8,128)(2,1)S(1)}, bf16[400,256]{1,0:T(8,128)(2,1)S(1)}, u32[]{:S(2)}, u32[]{:S(2)}) %collective-permute-start.17) | collective-permute-done | bytes 204832 | tf_op jit(solution)/shard_map/ppermute | solution.py:891
  119.6 4.1 %collective-permute-start.22 = (bf16[100,256]{1,0:T(8,128)(2,1)S(1)}, bf16[100,256]{1,0:T(8,128)(2,1)S(1)}, u32[]{:S(2)}, u32[]{:S(2)}) collective-permute-start(bf16[100,256]{1,0:T(8,128)(2,1)S(1)} %get-tuple-element.116), channel_id=1, source_target_pairs={{0,24},{2,26},{4,28},{6,30},{8,16},{10,18},{12,20},{14,22},{16,8},... | collective-permute-start | bytes 153608 | tf_op jit(solution)/shard_map/ppermute | solution.py:865
  124.4 3.0 %collective-permute-done.3 = bf16[400,256]{1,0:T(8,128)(2,1)S(1)} collective-permute-done((bf16[400,256]{1,0:T(8,128)(2,1)S(1)}, bf16[400,256]{1,0:T(8,128)(2,1)S(1)}, u32[]{:S(2)}, u32[]{:S(2)}) %collective-permute-start.3) | collective-permute-done | bytes 204832 | tf_op jit(solution)/shard_map/ppermute | solution.py:891
  127.6 3.8 %collective-permute-start.8 = (bf16[100,256]{1,0:T(8,128)(2,1)S(1)}, bf16[100,256]{1,0:T(8,128)(2,1)S(1)}, u32[]{:S(2)}, u32[]{:S(2)}) collective-permute-start(bf16[100,256]{1,0:T(8,128)(2,1)S(1)} %get-tuple-element.119), channel_id=1, source_target_pairs={{0,24},{2,26},{4,28},{6,30},{8,16},{10,18},{12,20},{14,22},{16,8},... | collective-permute-start | bytes 153608 | tf_op jit(solution)/shard_map/ppermute | solution.py:865
  132.1 1.5 collective-permute-start.25
  133.6 2.4 %collective-permute-start.23 = (bf16[100,256]{1,0:T(8,128)(2,1)S(1)}, bf16[100,256]{1,0:T(8,128)(2,1)S(1)}, u32[]{:S(2)}, u32[]{:S(2)}) collective-permute-start(bf16[100,256]{1,0:T(8,128)(2,1)S(1)} %add_convert_fusion.4), channel_id=1, source_target_pairs={{0,24},{2,26},{4,28},{6,30},{8,16},{10,18},{12,20},{14,22},{16,8},... | collective-permute-start | bytes 153608 | tf_op jit(solution)/shard_map/ppermute | solution.py:865
  138.4 2.1 %collective-permute-start.9 = (bf16[100,256]{1,0:T(8,128)(2,1)S(1)}, bf16[100,256]{1,0:T(8,128)(2,1)S(1)}, u32[]{:S(2)}, u32[]{:S(2)}) collective-permute-start(bf16[100,256]{1,0:T(8,128)(2,1)S(1)} %add_convert_fusion.5), channel_id=1, source_target_pairs={{0,24},{2,26},{4,28},{6,30},{8,16},{10,18},{12,20},{14,22},{16,8},... | collective-permute-start | bytes 153608 | tf_op jit(solution)/shard_map/ppermute | solution.py:865
  141.0 2.0 %collective-permute-done.24 = bf16[100,256]{1,0:T(8,128)(2,1)S(1)} collective-permute-done((bf16[100,256]{1,0:T(8,128)(2,1)S(1)}, bf16[100,256]{1,0:T(8,128)(2,1)S(1)}, u32[]{:S(2)}, u32[]{:S(2)}) %collective-permute-start.24) | collective-permute-done | bytes 51232 | tf_op jit(solution)/shard_map/ppermute | solution.py:865
  143.1 1.8 %collective-permute-start.28 = (bf16[400,256]{1,0:T(8,128)(2,1)S(1)}, bf16[400,256]{1,0:T(8,128)(2,1)S(1)}, u32[]{:S(2)}, u32[]{:S(2)}) collective-permute-start(bf16[400,256]{1,0:T(8,128)(2,1)S(1)} %maximum_select_fusion.1), channel_id=1, source_target_pairs={{0,5},{1,4},{2,7},{3,6},{4,1},{5,0},{6,3},{7,2},{8,13},{9,12},{10,... | collective-permute-start | bytes 614408 | tf_op jit(solution)/shard_map/ppermute | solution.py:891
  144.9 1.2 collective-permute-start.27
  146.8 1.8 %collective-permute-start.14 = (bf16[400,256]{1,0:T(8,128)(2,1)S(1)}, bf16[400,256]{1,0:T(8,128)(2,1)S(1)}, u32[]{:S(2)}, u32[]{:S(2)}) collective-permute-start(bf16[400,256]{1,0:T(8,128)(2,1)S(1)} %maximum_select_fusion), channel_id=1, source_target_pairs={{0,5},{1,4},{2,7},{3,6},{4,1},{5,0},{6,3},{7,2},{8,13},{9,12},{10,... | collective-permute-start | bytes 614408 | tf_op jit(solution)/shard_map/ppermute | solution.py:891
  149.8 2.4 %copy_bitcast_fusion.1 = (bf16[522,4,256]{2,1,0:T(4,128)(2,1)}, bf16[522,4,256]{2,1,0:T(4,128)(2,1)}) fusion(bf16[4,522,256]{2,1,0:T(8,128)(2,1)S(1)} %copy-done.19, bf16[4,522,256]{2,1,0:T(8,128)(2,1)S(1)} %copy-done.18), kind=kLoop, calls=%fused_computation.3 | loop fusion | bytes 4276224 | tf_op jit(solution)/shard_map/transpose | solution.py:901
  152.3 1.4 collective-permute-start.12
  153.6 2.7 %collective-permute-done.27 = bf16[400,256]{1,0:T(8,128)(2,1)S(1)} collective-permute-done((bf16[400,256]{1,0:T(8,128)(2,1)S(1)}, bf16[400,256]{1,0:T(8,128)(2,1)S(1)}, u32[]{:S(2)}, u32[]{:S(2)}) %collective-permute-start.27) | collective-permute-done | bytes 204832 | tf_op jit(solution)/shard_map/ppermute | solution.py:891
  156.4 2.5 %collective-permute-done.14 = bf16[400,256]{1,0:T(8,128)(2,1)S(1)} collective-permute-done((bf16[400,256]{1,0:T(8,128)(2,1)S(1)}, bf16[400,256]{1,0:T(8,128)(2,1)S(1)}, u32[]{:S(2)}, u32[]{:S(2)}) %collective-permute-start.14) | collective-permute-done | bytes 204832 | tf_op jit(solution)/shard_map/ppermute | solution.py:891
  158.9 1.7 %collective-permute-done.13 = bf16[400,256]{1,0:T(8,128)(2,1)S(1)} collective-permute-done((bf16[400,256]{1,0:T(8,128)(2,1)S(1)}, bf16[400,256]{1,0:T(8,128)(2,1)S(1)}, u32[]{:S(2)}, u32[]{:S(2)}) %collective-permute-start.13) | collective-permute-done | bytes 204832 | tf_op jit(solution)/shard_map/ppermute | solution.py:891
  161.1 2.3 %collective-permute-done.15.refs_1_ = bf16[1600,256]{1,0:T(8,128)(2,1)S(1)} collective-permute-done((bf16[1600,256]{1,0:T(8,128)(2,1)S(1)}, bf16[1600,256]{1,0:T(8,128)(2,1)S(1)}, u32[]{:S(2)}, u32[]{:S(2)}) %collective-permute-start.15) | collective-permute-done | bytes 819232 | tf_op jit(solution)/shard_map/ppermute | solution.py:846
  163.4 3.7 %unpack.1 = (f32[2,256,256]{2,1,0:T(8,128)}, f32[2,256]{1,0:T(2,128)}, f32[2,256,256]{2,1,0:T(8,128)}, f32[2,256,256]{2,1,0:T(8,128)}, f32[2,256]{1,0:T(2,128)},...) custom-call(bf16[1600,256]{1,0:T(8,128)(2,1)S(1)} %pad_maximum_fusio, ...), custom_call_target="tpu_custom_call" | custom-call | tf_op jit(solution)/shard_map/unpack/pallas_call | solution.py:825
  (99 shorter events, 9.4 us)
Async XLA Ops:
  23.4 3.4 %collective-permute-start = (bf16[4,16,256]{2,1,0:T(8,128)(2,1)}, bf16[4,16,256]{2,1,0:T(8,128)(2,1)S(1)}, u32[]{:S(2)}, u32[]{:S(2)}) collective-permute-start(bf16[4,16,256]{2,1,0:T(8,128)(2,1)} %get-tuple-element.64), channel_id=1, source_target_pairs={{0,2},{2,4},{4,6},{6,8},{8,10},{10,12},{12,14},{14,16},{16,18},{18... | collective-permute-start | bytes 98312 | tf_op jit(solution)/shard_map/ppermute | solution.py:841
  27.0 45.7 %copy-start.4 = (bf16[4,528,64]{2,1,0:T(8,128)(2,1)S(1)}, bf16[4,528,64]{2,1,0:T(8,128)(2,1)}, u32[]{:S(2)}) copy-start(bf16[4,528,64]{2,1,0:T(8,128)(2,1)} %get-tuple-element.73.refs_20_) | copy-start | bytes 811012
  27.0 45.7 %copy-start.7 = (f32[4,4,512]{2,1,0:T(4,128)S(1)}, f32[4,4,512]{2,1,0:T(4,128)}, u32[]{:S(2)}) copy-start(f32[4,4,512]{2,1,0:T(4,128)} %get-tuple-element.74.refs_21_) | copy-start | bytes 98308
  66.7 37.6 %collective-permute-start.16 = (bf16[1600,256]{1,0:T(8,128)(2,1)}, bf16[1600,256]{1,0:T(8,128)(2,1)S(1)}, u32[]{:S(2)}, u32[]{:S(2)}) collective-permute-start(bf16[1600,256]{1,0:T(8,128)(2,1)} %get-tuple-element.93), channel_id=1, source_target_pairs={{0,2},{2,0},{4,6},{6,4},{8,10},{10,8},{12,14},{14,12},{16,18},{18,... | collective-permute-start | bytes 2457608 | tf_op jit(solution)/shard_map/ppermute | solution.py:846
  69.6 3.1 %collective-permute-start.1 = (bf16[4,16,256]{2,1,0:T(8,128)(2,1)S(1)}, bf16[4,16,256]{2,1,0:T(8,128)(2,1)S(1)}, u32[]{:S(2)}, u32[]{:S(2)}) collective-permute-start(bf16[4,16,256]{2,1,0:T(8,128)(2,1)S(1)} %get-tuple-element.67), channel_id=1, source_target_pairs={{2,0},{4,2},{6,4},{8,6},{10,8},{12,10},{14,12},{16,14},{18,16},{20... | collective-permute-start | bytes 98312 | tf_op jit(solution)/shard_map/ppermute | solution.py:841
  101.5 7.6 %collective-permute-start.2 = (bf16[1600,256]{1,0:T(8,128)(2,1)}, bf16[1600,256]{1,0:T(8,128)(2,1)S(1)}, u32[]{:S(2)}, u32[]{:S(2)}) collective-permute-start(bf16[1600,256]{1,0:T(8,128)(2,1)} %get-tuple-element.85), channel_id=1, source_target_pairs={{0,2},{2,0},{4,6},{6,4},{8,10},{10,8},{12,14},{14,12},{16,18},{18,... | collective-permute-start | bytes 2457608 | tf_op jit(solution)/shard_map/ppermute | solution.py:846
  104.5 9.0 %collective-permute-start.19 = (bf16[400,256]{1,0:T(8,128)(2,1)S(1)}, bf16[400,256]{1,0:T(8,128)(2,1)S(1)}, u32[]{:S(2)}, u32[]{:S(2)}) collective-permute-start(bf16[400,256]{1,0:T(8,128)(2,1)S(1)} %get-tuple-element.110), channel_id=1, source_target_pairs={{0,4},{1,5},{2,6},{3,7},{4,0},{5,1},{6,2},{7,3},{8,12},{9,13},{10,... | collective-permute-start | bytes 614408 | tf_op jit(solution)/shard_map/ppermute | solution.py:891
  107.6 9.7 %collective-permute-start.18 = (bf16[400,256]{1,0:T(8,128)(2,1)S(1)}, bf16[400,256]{1,0:T(8,128)(2,1)S(1)}, u32[]{:S(2)}, u32[]{:S(2)}) collective-permute-start(bf16[400,256]{1,0:T(8,128)(2,1)S(1)} %get-tuple-element.111), channel_id=1, source_target_pairs={{0,1},{1,0},{2,3},{3,2},{4,5},{5,4},{6,7},{7,6},{8,9},{9,8},{10,11... | collective-permute-start | bytes 614408 | tf_op jit(solution)/shard_map/ppermute | solution.py:891
  109.1 10.4 %collective-permute-start.17 = (bf16[400,256]{1,0:T(8,128)(2,1)S(1)}, bf16[400,256]{1,0:T(8,128)(2,1)S(1)}, u32[]{:S(2)}, u32[]{:S(2)}) collective-permute-start(bf16[400,256]{1,0:T(8,128)(2,1)S(1)} %get-tuple-element.109), channel_id=1, source_target_pairs={{0,5},{1,4},{2,7},{3,6},{4,1},{5,0},{6,3},{7,2},{8,13},{9,12},{10,... | collective-permute-start | bytes 614408 | tf_op jit(solution)/shard_map/ppermute | solution.py:891
  109.4 14.4 %collective-permute-start.5 = (bf16[400,256]{1,0:T(8,128)(2,1)S(1)}, bf16[400,256]{1,0:T(8,128)(2,1)S(1)}, u32[]{:S(2)}, u32[]{:S(2)}) collective-permute-start(bf16[400,256]{1,0:T(8,128)(2,1)S(1)} %get-tuple-element.113), channel_id=1, source_target_pairs={{0,4},{1,5},{2,6},{3,7},{4,0},{5,1},{6,2},{7,3},{8,12},{9,13},{10,... | collective-permute-start | bytes 614408 | tf_op jit(solution)/shard_map/ppermute | solution.py:891
  111.4 13.0 %collective-permute-start.4 = (bf16[400,256]{1,0:T(8,128)(2,1)S(1)}, bf16[400,256]{1,0:T(8,128)(2,1)S(1)}, u32[]{:S(2)}, u32[]{:S(2)}) collective-permute-start(bf16[400,256]{1,0:T(8,128)(2,1)S(1)} %get-tuple-element.114), channel_id=1, source_target_pairs={{0,1},{1,0},{2,3},{3,2},{4,5},{5,4},{6,7},{7,6},{8,9},{9,8},{10,11... | collective-permute-start | bytes 614408 | tf_op jit(solution)/shard_map/ppermute | solution.py:891
  113.5 13.9 %collective-permute-start.3 = (bf16[400,256]{1,0:T(8,128)(2,1)S(1)}, bf16[400,256]{1,0:T(8,128)(2,1)S(1)}, u32[]{:S(2)}, u32[]{:S(2)}) collective-permute-start(bf16[400,256]{1,0:T(8,128)(2,1)S(1)} %get-tuple-element.112), channel_id=1, source_target_pairs={{0,5},{1,4},{2,7},{3,6},{4,1},{5,0},{6,3},{7,2},{8,13},{9,12},{10,... | collective-permute-start | bytes 614408 | tf_op jit(solution)/shard_map/ppermute | solution.py:891
  119.6 11.8 %collective-permute-start.22 = (bf16[100,256]{1,0:T(8,128)(2,1)S(1)}, bf16[100,256]{1,0:T(8,128)(2,1)S(1)}, u32[]{:S(2)}, u32[]{:S(2)}) collective-permute-start(bf16[100,256]{1,0:T(8,128)(2,1)S(1)} %get-tuple-element.116), channel_id=1, source_target_pairs={{0,24},{2,26},{4,28},{6,30},{8,16},{10,18},{12,20},{14,22},{16,8},... | collective-permute-start | bytes 153608 | tf_op jit(solution)/shard_map/ppermute | solution.py:865
  123.8 8.3 %collective-permute-start.21 = (bf16[100,256]{1,0:T(8,128)(2,1)S(1)}, bf16[100,256]{1,0:T(8,128)(2,1)S(1)}, u32[]{:S(2)}, u32[]{:S(2)}) collective-permute-start(bf16[100,256]{1,0:T(8,128)(2,1)S(1)} %get-tuple-element.117), channel_id=1, source_target_pairs={{0,16},{2,18},{4,20},{6,22},{8,24},{10,26},{12,28},{14,30},{16,0},... | collective-permute-start | bytes 153608 | tf_op jit(solution)/shard_map/ppermute | solution.py:865
  123.8 8.3 %collective-permute-start.20 = (bf16[100,256]{1,0:T(8,128)(2,1)S(1)}, bf16[100,256]{1,0:T(8,128)(2,1)S(1)}, u32[]{:S(2)}, u32[]{:S(2)}) collective-permute-start(bf16[100,256]{1,0:T(8,128)(2,1)S(1)} %get-tuple-element.115), channel_id=1, source_target_pairs={{0,8},{2,10},{4,12},{6,14},{8,0},{10,2},{12,4},{14,6},{16,24},{18,... | collective-permute-start | bytes 153608 | tf_op jit(solution)/shard_map/ppermute | solution.py:865
  127.6 8.4 %collective-permute-start.8 = (bf16[100,256]{1,0:T(8,128)(2,1)S(1)}, bf16[100,256]{1,0:T(8,128)(2,1)S(1)}, u32[]{:S(2)}, u32[]{:S(2)}) collective-permute-start(bf16[100,256]{1,0:T(8,128)(2,1)S(1)} %get-tuple-element.119), channel_id=1, source_target_pairs={{0,24},{2,26},{4,28},{6,30},{8,16},{10,18},{12,20},{14,22},{16,8},... | collective-permute-start | bytes 153608 | tf_op jit(solution)/shard_map/ppermute | solution.py:865
  131.4 6.0 %collective-permute-start.7 = (bf16[100,256]{1,0:T(8,128)(2,1)S(1)}, bf16[100,256]{1,0:T(8,128)(2,1)S(1)}, u32[]{:S(2)}, u32[]{:S(2)}) collective-permute-start(bf16[100,256]{1,0:T(8,128)(2,1)S(1)} %get-tuple-element.120), channel_id=1, source_target_pairs={{0,16},{2,18},{4,20},{6,22},{8,24},{10,26},{12,28},{14,30},{16,0},... | collective-permute-start | bytes 153608 | tf_op jit(solution)/shard_map/ppermute | solution.py:865
  131.4 6.0 %collective-permute-start.6 = (bf16[100,256]{1,0:T(8,128)(2,1)S(1)}, bf16[100,256]{1,0:T(8,128)(2,1)S(1)}, u32[]{:S(2)}, u32[]{:S(2)}) collective-permute-start(bf16[100,256]{1,0:T(8,128)(2,1)S(1)} %get-tuple-element.118), channel_id=1, source_target_pairs={{0,8},{2,10},{4,12},{6,14},{8,0},{10,2},{12,4},{14,6},{16,24},{18,... | collective-permute-start | bytes 153608 | tf_op jit(solution)/shard_map/ppermute | solution.py:865
  132.1 8.4 %collective-permute-start.25 = (bf16[100,256]{1,0:T(8,128)(2,1)S(1)}, bf16[100,256]{1,0:T(8,128)(2,1)S(1)}, u32[]{:S(2)}, u32[]{:S(2)}) collective-permute-start(bf16[100,256]{1,0:T(8,128)(2,1)S(1)} %add_convert_fusion.4), channel_id=1, source_target_pairs={{0,8},{2,10},{4,12},{6,14},{8,0},{10,2},{12,4},{14,6},{16,24},{18,... | collective-permute-start | bytes 153608 | tf_op jit(solution)/shard_map/ppermute | solution.py:865
  133.6 7.5 %collective-permute-start.23 = (bf16[100,256]{1,0:T(8,128)(2,1)S(1)}, bf16[100,256]{1,0:T(8,128)(2,1)S(1)}, u32[]{:S(2)}, u32[]{:S(2)}) collective-permute-start(bf16[100,256]{1,0:T(8,128)(2,1)S(1)} %add_convert_fusion.4), channel_id=1, source_target_pairs={{0,24},{2,26},{4,28},{6,30},{8,16},{10,18},{12,20},{14,22},{16,8},... | collective-permute-start | bytes 153608 | tf_op jit(solution)/shard_map/ppermute | solution.py:865
  136.0 7.0 %collective-permute-start.24 = (bf16[100,256]{1,0:T(8,128)(2,1)S(1)}, bf16[100,256]{1,0:T(8,128)(2,1)S(1)}, u32[]{:S(2)}, u32[]{:S(2)}) collective-permute-start(bf16[100,256]{1,0:T(8,128)(2,1)S(1)} %add_convert_fusion.4), channel_id=1, source_target_pairs={{0,16},{2,18},{4,20},{6,22},{8,24},{10,26},{12,28},{14,30},{16,0},... | collective-permute-start | bytes 153608 | tf_op jit(solution)/shard_map/ppermute | solution.py:865
  137.5 8.7 %collective-permute-start.11 = (bf16[100,256]{1,0:T(8,128)(2,1)S(1)}, bf16[100,256]{1,0:T(8,128)(2,1)S(1)}, u32[]{:S(2)}, u32[]{:S(2)}) collective-permute-start(bf16[100,256]{1,0:T(8,128)(2,1)S(1)} %add_convert_fusion.5), channel_id=1, source_target_pairs={{0,8},{2,10},{4,12},{6,14},{8,0},{10,2},{12,4},{14,6},{16,24},{18,... | collective-permute-start | bytes 153608 | tf_op jit(solution)/shard_map/ppermute | solution.py:865
  138.4 8.3 %collective-permute-start.9 = (bf16[100,256]{1,0:T(8,128)(2,1)S(1)}, bf16[100,256]{1,0:T(8,128)(2,1)S(1)}, u32[]{:S(2)}, u32[]{:S(2)}) collective-permute-start(bf16[100,256]{1,0:T(8,128)(2,1)S(1)} %add_convert_fusion.5), channel_id=1, source_target_pairs={{0,24},{2,26},{4,28},{6,30},{8,16},{10,18},{12,20},{14,22},{16,8},... | collective-permute-start | bytes 153608 | tf_op jit(solution)/shard_map/ppermute | solution.py:865
  140.5 6.2 %collective-permute-start.10 = (bf16[100,256]{1,0:T(8,128)(2,1)S(1)}, bf16[100,256]{1,0:T(8,128)(2,1)S(1)}, u32[]{:S(2)}, u32[]{:S(2)}) collective-permute-start(bf16[100,256]{1,0:T(8,128)(2,1)S(1)} %add_convert_fusion.5), channel_id=1, source_target_pairs={{0,16},{2,18},{4,20},{6,22},{8,24},{10,26},{12,28},{14,30},{16,0},... | collective-permute-start | bytes 153608 | tf_op jit(solution)/shard_map/ppermute | solution.py:865
  143.1 9.2 %collective-permute-start.28 = (bf16[400,256]{1,0:T(8,128)(2,1)S(1)}, bf16[400,256]{1,0:T(8,128)(2,1)S(1)}, u32[]{:S(2)}, u32[]{:S(2)}) collective-permute-start(bf16[400,256]{1,0:T(8,128)(2,1)S(1)} %maximum_select_fusion.1), channel_id=1, source_target_pairs={{0,5},{1,4},{2,7},{3,6},{4,1},{5,0},{6,3},{7,2},{8,13},{9,12},{10,... | collective-permute-start | bytes 614408 | tf_op jit(solution)/shard_map/ppermute | solution.py:891
  144.9 11.4 %collective-permute-start.27 = (bf16[400,256]{1,0:T(8,128)(2,1)S(1)}, bf16[400,256]{1,0:T(8,128)(2,1)S(1)}, u32[]{:S(2)}, u32[]{:S(2)}) collective-permute-start(bf16[400,256]{1,0:T(8,128)(2,1)S(1)} %maximum_select_fusion.1), channel_id=1, source_target_pairs={{0,4},{1,5},{2,6},{3,7},{4,0},{5,1},{6,2},{7,3},{8,12},{9,13},{10,... | collective-permute-start | bytes 614408 | tf_op jit(solution)/shard_map/ppermute | solution.py:891
  146.1 10.2 %collective-permute-start.26 = (bf16[400,256]{1,0:T(8,128)(2,1)S(1)}, bf16[400,256]{1,0:T(8,128)(2,1)S(1)}, u32[]{:S(2)}, u32[]{:S(2)}) collective-permute-start(bf16[400,256]{1,0:T(8,128)(2,1)S(1)} %maximum_select_fusion.1), channel_id=1, source_target_pairs={{0,1},{1,0},{2,3},{3,2},{4,5},{5,4},{6,7},{7,6},{8,9},{9,8},{10,11... | collective-permute-start | bytes 614408 | tf_op jit(solution)/shard_map/ppermute | solution.py:891
  146.8 12.1 %collective-permute-start.14 = (bf16[400,256]{1,0:T(8,128)(2,1)S(1)}, bf16[400,256]{1,0:T(8,128)(2,1)S(1)}, u32[]{:S(2)}, u32[]{:S(2)}) collective-permute-start(bf16[400,256]{1,0:T(8,128)(2,1)S(1)} %maximum_select_fusion), channel_id=1, source_target_pairs={{0,5},{1,4},{2,7},{3,6},{4,1},{5,0},{6,3},{7,2},{8,13},{9,12},{10,... | collective-permute-start | bytes 614408 | tf_op jit(solution)/shard_map/ppermute | solution.py:891
  148.6 12.1 %collective-permute-start.13 = (bf16[400,256]{1,0:T(8,128)(2,1)S(1)}, bf16[400,256]{1,0:T(8,128)(2,1)S(1)}, u32[]{:S(2)}, u32[]{:S(2)}) collective-permute-start(bf16[400,256]{1,0:T(8,128)(2,1)S(1)} %maximum_select_fusion), channel_id=1, source_target_pairs={{0,4},{1,5},{2,6},{3,7},{4,0},{5,1},{6,2},{7,3},{8,12},{9,13},{10,... | collective-permute-start | bytes 614408 | tf_op jit(solution)/shard_map/ppermute | solution.py:891
  152.3 8.6 %collective-permute-start.12 = (bf16[400,256]{1,0:T(8,128)(2,1)S(1)}, bf16[400,256]{1,0:T(8,128)(2,1)S(1)}, u32[]{:S(2)}, u32[]{:S(2)}) collective-permute-start(bf16[400,256]{1,0:T(8,128)(2,1)S(1)} %maximum_select_fusion), channel_id=1, source_target_pairs={{0,1},{1,0},{2,3},{3,2},{4,5},{5,4},{6,7},{7,6},{8,9},{9,8},{10,11... | collective-permute-start | bytes 614408 | tf_op jit(solution)/shard_map/ppermute | solution.py:891
  156.3 4.7 %collective-permute-start.29 = (bf16[1600,256]{1,0:T(8,128)(2,1)S(1)}, bf16[1600,256]{1,0:T(8,128)(2,1)S(1)}, u32[]{:S(2)}, u32[]{:S(2)}) collective-permute-start(bf16[1600,256]{1,0:T(8,128)(2,1)S(1)} %pad_maximum_fusion.1.refs_2_), channel_id=1, source_target_pairs={{0,2},{2,0},{4,6},{6,4},{8,10},{10,8},{12,14},{14,12},{16,18},{18,... | collective-permute-start | bytes 2457608 | tf_op jit(solution)/shard_map/ppermute | solution.py:846
  161.0 2.4 %collective-permute-start.15 = (bf16[1600,256]{1,0:T(8,128)(2,1)S(1)}, bf16[1600,256]{1,0:T(8,128)(2,1)S(1)}, u32[]{:S(2)}, u32[]{:S(2)}) collective-permute-start(bf16[1600,256]{1,0:T(8,128)(2,1)S(1)} %pad_maximum_fusion.refs_0_), channel_id=1, source_target_pairs={{0,2},{2,0},{4,6},{6,4},{8,10},{10,8},{12,14},{14,12},{16,18},{18,... | collective-permute-start | bytes 2457608 | tf_op jit(solution)/shard_map/ppermute | solution.py:846
  (21 other events, 492.7 us)

commit v7 on v6

--- a/solution.py
+++ b/solution.py
@@ -13,6 +13,7 @@
 DENSITY = 0.3989422804014327
 ROOT_HALF = 0.7071067811865476
 BELL = -0.7213475204444817
+LOG2_E = 1.4426950408889634
 HEADS = 4
 TILE = 16
 STRIP = 64
@@ -127,9 +128,9 @@
     top, bottom = s[:main], jnp.where(live_rest, s[main:], LOW)
     peak = jnp.maximum(jnp.max(top, axis=0, keepdims=True), jnp.max(bottom, axis=0, keepdims=True))
     yield 120
-    top = jnp.exp(top - peak).astype(BF16)
+    top = jnp.exp2(top - peak).astype(BF16)
     yield 220
-    return top, jnp.exp(bottom - peak).astype(BF16)
+    return top, jnp.exp2(bottom - peak).astype(BF16)
 
 
 def woven(*tasks):
@@ -162,7 +163,7 @@
         return ref[layer : layer + 1, :]
 
     st.x[...] = x
-    q = ((dot(x, w.w_query[at(w, layer)]) + row(w.b_query)) * 0.125).astype(BF16)
+    q = ((dot(x, w.w_query[at(w, layer)]) + row(w.b_query)) * (0.125 * LOG2_E)).astype(BF16)
     yield 150
     k = dot(x, w.w_key[at(w, layer)]).astype(BF16)
     yield 150
@@ -373,7 +374,7 @@
     yield from woven((last_rows(at_last), 500), (first_rows(), 3000))
     grad_v, grad_k, grad_q_rest = at_last
     grad_v = (grad_v + jnp.concatenate(v_parts, axis=1)).astype(BF16)
-    grad_k = (grad_k + jnp.concatenate(k_parts, axis=1)).astype(BF16)
+    grad_k = ((grad_k + jnp.concatenate(k_parts, axis=1)) * (1.0 / LOG2_E)).astype(BF16)
     grad_q_t = jnp.concatenate(q_parts, axis=0)
     grad_q_t = grad_q_t + dot_tn(spread_heads(k[main:], width), jnp.concatenate(bottoms, axis=0))
     grad_q = jnp.concatenate([grad_q_t.astype(BF16).T, grad_q_rest], axis=0) * BF16(0.125)

time: 167 us -> 166 us (level)
  no operation moved by 1% of the time
where the time goes in v7:
time: 166 us
  Pallas kernels  91.1 us (55%)
  starting transfers between devices  46.3 us (28%)
  waiting for transfers between devices  21 us (13%)
  local copies, waits for them, and re-layouts  5.1 us (3%)
    pallas_call x1, Pallas kernels, upper_both(): pl.pallas_call(functools.partial(upper_kernel, rows, micro, bits), grid=(...  39 us
    pallas_call x1, Pallas kernels, lower_backward(): pl.pallas_call(functools.partial(lower_backward_kernel, memory, bits), gr...  28.8 us
    ppermute x12, starting transfers between devices, to(): return lax.ppermute(part, (LINE, PAIR), perm)  19.7 us
    pallas_call x1, Pallas kernels, lower_forward(): pl.pallas_call(lower_forward_kernel, grid=(micro,), in_specs=[by_micro(hi...  19.6 us
    ppermute x12, starting transfers between devices, across(): lax.ppermute(part, axis, [(i, i ^ k * step) for i in range(lax.axis_size(...  17.2 us
    ppermute x12, waiting for transfers between devices, to(): return lax.ppermute(part, (LINE, PAIR), perm)  13 us
    ppermute x4, starting transfers between devices, swap(): lax.ppermute(value, axis, [(i, i ^ step) for i in range(lax.axis_size(axi...  5.81 us
    pallas_call x1, Pallas kernels, unpack(): pl.pallas_call(functools.partial(unpack_kernel, bits), in_specs=[pl.Block...  3.72 us
  transfers between devices with their start and end apart: 30, of which 12 were waited for; matrix products, arithmetic and copies ran while one was open for 2% of the time, Pallas kernels for 17%

profile of v7, /device:TPU:0, one launch (start us, length us, event | category | flops | bytes accessed | tf_op | source)
XLA Modules:
  0.0 166.0 jit_solution(13411626262342338883)
XLA Ops:
  0.7 2.4 %copy.45 = bf16[4,1,1,522,256]{4,3,0,2,1:T(8,128)(2,1)} copy(bf16[4,1,1,522,256]{4,0,3,2,1:T(4,128)(2,1)} %param.20) | data formatting | bytes 2138112 | tf_op args[0]
  3.2 19.6 %lower_forward.1 = (bf16[4,528,256]{2,1,0:T(8,128)(2,1)}, bf16[4,16,256]{2,1,0:T(8,128)(2,1)}, bf16[4,528,256]{2,1,0:T(8,128)(2,1)}, bf16[4,528,256]{2,1,0:T(8,1...) custom-call(bf16[4,522,256]{2,1,0:T(8,128)(2,1)} %bitcast.23, ...), custom_call_target="tpu_custom_call" | custom-call | tf_op jit(solution)/shard_map/lower_forward/pallas_call | solution.py:578
  22.8 2.4 %collective-permute-start = (bf16[4,16,256]{2,1,0:T(8,128)(2,1)}, bf16[4,16,256]{2,1,0:T(8,128)(2,1)S(1)}, u32[]{:S(2)}, u32[]{:S(2)}) collective-permute-start(bf16[4,16,256]{2,1,0:T(8,128)(2,1)} %get-tuple-element.64), channel_id=1, source_target_pairs={{0,2},{2,4},{4,6},{6,8},{8,10},{10,12},{12,14},{14,16},{16,18},{18... | collective-permute-start | bytes 98312 | tf_op jit(solution)/shard_map/ppermute | solution.py:842
  26.4 39.0 %upper_both.1 = (bf16[4,522,256]{2,1,0:T(8,128)(2,1)}, f32[4,528,256]{2,1,0:T(8,128)}, bf16[4,16,256]{2,1,0:T(8,128)(2,1)S(1)}, bf16[1600,256]{1,0:T(8,128)(2,1)}, bf16[1600,256]{1,0:T(8,128)(2,1)}) custom-call(s32[4]{0:T(128)S(1)} %bitcast.22, bf16[4,528,256]{2,1,0:T(8,128)(2,1)} %get-tuple-element.63.x_ref, ...), custom_call_target="tpu_custom_call" | custom-call | tf_op jit(solution)/shard_map/upper_both/pallas_call | solution.py:700
  65.4 3.0 %collective-permute-start.16 = (bf16[1600,256]{1,0:T(8,128)(2,1)}, bf16[1600,256]{1,0:T(8,128)(2,1)S(1)}, u32[]{:S(2)}, u32[]{:S(2)}) collective-permute-start(bf16[1600,256]{1,0:T(8,128)(2,1)} %get-tuple-element.93), channel_id=1, source_target_pairs={{0,2},{2,0},{4,6},{6,4},{8,10},{10,8},{12,14},{14,12},{16,18},{18,... | collective-permute-start | bytes 2457608 | tf_op jit(solution)/shard_map/ppermute | solution.py:847
  68.4 1.3 collective-permute-start.1
  69.7 1.8 %collective-permute-done.1.back_ref = bf16[4,16,256]{2,1,0:T(8,128)(2,1)S(1)} collective-permute-done((bf16[4,16,256]{2,1,0:T(8,128)(2,1)S(1)}, bf16[4,16,256]{2,1,0:T(8,128)(2,1)S(1)}, u32[]{:S(2)}, u32[]{:S(2)}) %collective-permute-start.1) | collective-permute-done | bytes 32800 | tf_op jit(solution)/shard_map/ppermute | solution.py:842
  71.5 28.8 %lower_backward.1 = (bf16[4,522,256]{2,1,0:T(8,128)(2,1)}, bf16[1600,256]{1,0:T(8,128)(2,1)}, bf16[1600,256]{1,0:T(8,128)(2,1)}) custom-call(f32[4,528,256]{2,1,0:T(8,128)} %get-tuple-element.66.grad_ref, bf16[4,16,256]{2,1,0:T(8,128)(2,1)S(1)} %collective-permute-done.1.back_ref, bf16[2,256,256]{2,1,0:T(8,128)(2,1)S(1)} %copy-done, f32[2,256]{1,0:T(2,128)S(1)} %copy-done.8, ...), custom_call_target="tpu_custom_call" | custom-call | tf_op jit(solution)/shard_map/lower_backward/pallas_call | solution.py:747
  100.3 2.7 %collective-permute-start.2 = (bf16[1600,256]{1,0:T(8,128)(2,1)}, bf16[1600,256]{1,0:T(8,128)(2,1)S(1)}, u32[]{:S(2)}, u32[]{:S(2)}) collective-permute-start(bf16[1600,256]{1,0:T(8,128)(2,1)} %get-tuple-element.85), channel_id=1, source_target_pairs={{0,2},{2,0},{4,6},{6,4},{8,10},{10,8},{12,14},{14,12},{16,18},{18,... | collective-permute-start | bytes 2457608 | tf_op jit(solution)/shard_map/ppermute | solution.py:847
  103.2 3.1 %collective-permute-start.19 = (bf16[400,256]{1,0:T(8,128)(2,1)S(1)}, bf16[400,256]{1,0:T(8,128)(2,1)S(1)}, u32[]{:S(2)}, u32[]{:S(2)}) collective-permute-start(bf16[400,256]{1,0:T(8,128)(2,1)S(1)} %get-tuple-element.110), channel_id=1, source_target_pairs={{0,4},{1,5},{2,6},{3,7},{4,0},{5,1},{6,2},{7,3},{8,12},{9,13},{10,... | collective-permute-start | bytes 614408 | tf_op jit(solution)/shard_map/ppermute | solution.py:892
  106.3 1.5 collective-permute-start.18
  108.1 2.0 %collective-permute-start.5 = (bf16[400,256]{1,0:T(8,128)(2,1)S(1)}, bf16[400,256]{1,0:T(8,128)(2,1)S(1)}, u32[]{:S(2)}, u32[]{:S(2)}) collective-permute-start(bf16[400,256]{1,0:T(8,128)(2,1)S(1)} %get-tuple-element.113), channel_id=1, source_target_pairs={{0,4},{1,5},{2,6},{3,7},{4,0},{5,1},{6,2},{7,3},{8,12},{9,13},{10,... | collective-permute-start | bytes 614408 | tf_op jit(solution)/shard_map/ppermute | solution.py:892
  110.1 1.5 collective-permute-start.4
  112.3 3.7 %collective-permute-start.3 = (bf16[400,256]{1,0:T(8,128)(2,1)S(1)}, bf16[400,256]{1,0:T(8,128)(2,1)S(1)}, u32[]{:S(2)}, u32[]{:S(2)}) collective-permute-start(bf16[400,256]{1,0:T(8,128)(2,1)S(1)} %get-tuple-element.112), channel_id=1, source_target_pairs={{0,5},{1,4},{2,7},{3,6},{4,1},{5,0},{6,3},{7,2},{8,13},{9,12},{10,... | collective-permute-start | bytes 614408 | tf_op jit(solution)/shard_map/ppermute | solution.py:892
  116.0 2.2 %collective-permute-done.17 = bf16[400,256]{1,0:T(8,128)(2,1)S(1)} collective-permute-done((bf16[400,256]{1,0:T(8,128)(2,1)S(1)}, bf16[400,256]{1,0:T(8,128)(2,1)S(1)}, u32[]{:S(2)}, u32[]{:S(2)}) %collective-permute-start.17) | collective-permute-done | bytes 204832 | tf_op jit(solution)/shard_map/ppermute | solution.py:892
  118.4 4.1 %collective-permute-start.22 = (bf16[100,256]{1,0:T(8,128)(2,1)S(1)}, bf16[100,256]{1,0:T(8,128)(2,1)S(1)}, u32[]{:S(2)}, u32[]{:S(2)}) collective-permute-start(bf16[100,256]{1,0:T(8,128)(2,1)S(1)} %get-tuple-element.116), channel_id=1, source_target_pairs={{0,24},{2,26},{4,28},{6,30},{8,16},{10,18},{12,20},{14,22},{16,8},... | collective-permute-start | bytes 153608 | tf_op jit(solution)/shard_map/ppermute | solution.py:866
  123.1 3.0 %collective-permute-done.3 = bf16[400,256]{1,0:T(8,128)(2,1)S(1)} collective-permute-done((bf16[400,256]{1,0:T(8,128)(2,1)S(1)}, bf16[400,256]{1,0:T(8,128)(2,1)S(1)}, u32[]{:S(2)}, u32[]{:S(2)}) %collective-permute-start.3) | collective-permute-done | bytes 204832 | tf_op jit(solution)/shard_map/ppermute | solution.py:892
  126.3 3.8 %collective-permute-start.8 = (bf16[100,256]{1,0:T(8,128)(2,1)S(1)}, bf16[100,256]{1,0:T(8,128)(2,1)S(1)}, u32[]{:S(2)}, u32[]{:S(2)}) collective-permute-start(bf16[100,256]{1,0:T(8,128)(2,1)S(1)} %get-tuple-element.119), channel_id=1, source_target_pairs={{0,24},{2,26},{4,28},{6,30},{8,16},{10,18},{12,20},{14,22},{16,8},... | collective-permute-start | bytes 153608 | tf_op jit(solution)/shard_map/ppermute | solution.py:866
  130.8 1.5 collective-permute-start.25
  132.3 2.4 %collective-permute-start.23 = (bf16[100,256]{1,0:T(8,128)(2,1)S(1)}, bf16[100,256]{1,0:T(8,128)(2,1)S(1)}, u32[]{:S(2)}, u32[]{:S(2)}) collective-permute-start(bf16[100,256]{1,0:T(8,128)(2,1)S(1)} %add_convert_fusion.4), channel_id=1, source_target_pairs={{0,24},{2,26},{4,28},{6,30},{8,16},{10,18},{12,20},{14,22},{16,8},... | collective-permute-start | bytes 153608 | tf_op jit(solution)/shard_map/ppermute | solution.py:866
  137.1 2.1 %collective-permute-start.9 = (bf16[100,256]{1,0:T(8,128)(2,1)S(1)}, bf16[100,256]{1,0:T(8,128)(2,1)S(1)}, u32[]{:S(2)}, u32[]{:S(2)}) collective-permute-start(bf16[100,256]{1,0:T(8,128)(2,1)S(1)} %add_convert_fusion.5), channel_id=1, source_target_pairs={{0,24},{2,26},{4,28},{6,30},{8,16},{10,18},{12,20},{14,22},{16,8},... | collective-permute-start | bytes 153608 | tf_op jit(solution)/shard_map/ppermute | solution.py:866
  139.8 2.0 %collective-permute-done.24 = bf16[100,256]{1,0:T(8,128)(2,1)S(1)} collective-permute-done((bf16[100,256]{1,0:T(8,128)(2,1)S(1)}, bf16[100,256]{1,0:T(8,128)(2,1)S(1)}, u32[]{:S(2)}, u32[]{:S(2)}) %collective-permute-start.24) | collective-permute-done | bytes 51232 | tf_op jit(solution)/shard_map/ppermute | solution.py:866
  141.8 1.8 %collective-permute-start.28 = (bf16[400,256]{1,0:T(8,128)(2,1)S(1)}, bf16[400,256]{1,0:T(8,128)(2,1)S(1)}, u32[]{:S(2)}, u32[]{:S(2)}) collective-permute-start(bf16[400,256]{1,0:T(8,128)(2,1)S(1)} %maximum_select_fusion.1), channel_id=1, source_target_pairs={{0,5},{1,4},{2,7},{3,6},{4,1},{5,0},{6,3},{7,2},{8,13},{9,12},{10,... | collective-permute-start | bytes 614408 | tf_op jit(solution)/shard_map/ppermute | solution.py:892
  143.6 1.2 collective-permute-start.27
  145.5 1.8 %collective-permute-start.14 = (bf16[400,256]{1,0:T(8,128)(2,1)S(1)}, bf16[400,256]{1,0:T(8,128)(2,1)S(1)}, u32[]{:S(2)}, u32[]{:S(2)}) collective-permute-start(bf16[400,256]{1,0:T(8,128)(2,1)S(1)} %maximum_select_fusion), channel_id=1, source_target_pairs={{0,5},{1,4},{2,7},{3,6},{4,1},{5,0},{6,3},{7,2},{8,13},{9,12},{10,... | collective-permute-start | bytes 614408 | tf_op jit(solution)/shard_map/ppermute | solution.py:892
  148.5 2.4 %copy_bitcast_fusion.1 = (bf16[522,4,256]{2,1,0:T(4,128)(2,1)}, bf16[522,4,256]{2,1,0:T(4,128)(2,1)}) fusion(bf16[4,522,256]{2,1,0:T(8,128)(2,1)S(1)} %copy-done.19, bf16[4,522,256]{2,1,0:T(8,128)(2,1)S(1)} %copy-done.18), kind=kLoop, calls=%fused_computation.3 | loop fusion | bytes 4276224 | tf_op jit(solution)/shard_map/transpose | solution.py:902
  151.0 1.4 collective-permute-start.12
  152.3 2.7 %collective-permute-done.27 = bf16[400,256]{1,0:T(8,128)(2,1)S(1)} collective-permute-done((bf16[400,256]{1,0:T(8,128)(2,1)S(1)}, bf16[400,256]{1,0:T(8,128)(2,1)S(1)}, u32[]{:S(2)}, u32[]{:S(2)}) %collective-permute-start.27) | collective-permute-done | bytes 204832 | tf_op jit(solution)/shard_map/ppermute | solution.py:892
  155.1 2.5 %collective-permute-done.14 = bf16[400,256]{1,0:T(8,128)(2,1)S(1)} collective-permute-done((bf16[400,256]{1,0:T(8,128)(2,1)S(1)}, bf16[400,256]{1,0:T(8,128)(2,1)S(1)}, u32[]{:S(2)}, u32[]{:S(2)}) %collective-permute-start.14) | collective-permute-done | bytes 204832 | tf_op jit(solution)/shard_map/ppermute | solution.py:892
  157.7 1.7 %collective-permute-done.13 = bf16[400,256]{1,0:T(8,128)(2,1)S(1)} collective-permute-done((bf16[400,256]{1,0:T(8,128)(2,1)S(1)}, bf16[400,256]{1,0:T(8,128)(2,1)S(1)}, u32[]{:S(2)}, u32[]{:S(2)}) %collective-permute-start.13) | collective-permute-done | bytes 204832 | tf_op jit(solution)/shard_map/ppermute | solution.py:892
  159.8 2.3 %collective-permute-done.15.refs_1_ = bf16[1600,256]{1,0:T(8,128)(2,1)S(1)} collective-permute-done((bf16[1600,256]{1,0:T(8,128)(2,1)S(1)}, bf16[1600,256]{1,0:T(8,128)(2,1)S(1)}, u32[]{:S(2)}, u32[]{:S(2)}) %collective-permute-start.15) | collective-permute-done | bytes 819232 | tf_op jit(solution)/shard_map/ppermute | solution.py:847
  162.1 3.7 %unpack.1 = (f32[2,256,256]{2,1,0:T(8,128)}, f32[2,256]{1,0:T(2,128)}, f32[2,256,256]{2,1,0:T(8,128)}, f32[2,256,256]{2,1,0:T(8,128)}, f32[2,256]{1,0:T(2,128)},...) custom-call(bf16[1600,256]{1,0:T(8,128)(2,1)S(1)} %pad_maximum_fusio, ...), custom_call_target="tpu_custom_call" | custom-call | tf_op jit(solution)/shard_map/unpack/pallas_call | solution.py:826
  (99 shorter events, 9.4 us)
Async XLA Ops:
  22.8 3.4 %collective-permute-start = (bf16[4,16,256]{2,1,0:T(8,128)(2,1)}, bf16[4,16,256]{2,1,0:T(8,128)(2,1)S(1)}, u32[]{:S(2)}, u32[]{:S(2)}) collective-permute-start(bf16[4,16,256]{2,1,0:T(8,128)(2,1)} %get-tuple-element.64), channel_id=1, source_target_pairs={{0,2},{2,4},{4,6},{6,8},{8,10},{10,12},{12,14},{14,16},{16,18},{18... | collective-permute-start | bytes 98312 | tf_op jit(solution)/shard_map/ppermute | solution.py:842
  26.3 45.1 %copy-start.4 = (bf16[4,528,64]{2,1,0:T(8,128)(2,1)S(1)}, bf16[4,528,64]{2,1,0:T(8,128)(2,1)}, u32[]{:S(2)}) copy-start(bf16[4,528,64]{2,1,0:T(8,128)(2,1)} %get-tuple-element.73.refs_20_) | copy-start | bytes 811012
  26.3 45.1 %copy-start.7 = (f32[4,4,512]{2,1,0:T(4,128)S(1)}, f32[4,4,512]{2,1,0:T(4,128)}, u32[]{:S(2)}) copy-start(f32[4,4,512]{2,1,0:T(4,128)} %get-tuple-element.74.refs_21_) | copy-start | bytes 98308
  65.4 37.6 %collective-permute-start.16 = (bf16[1600,256]{1,0:T(8,128)(2,1)}, bf16[1600,256]{1,0:T(8,128)(2,1)S(1)}, u32[]{:S(2)}, u32[]{:S(2)}) collective-permute-start(bf16[1600,256]{1,0:T(8,128)(2,1)} %get-tuple-element.93), channel_id=1, source_target_pairs={{0,2},{2,0},{4,6},{6,4},{8,10},{10,8},{12,14},{14,12},{16,18},{18,... | collective-permute-start | bytes 2457608 | tf_op jit(solution)/shard_map/ppermute | solution.py:847
  68.4 3.1 %collective-permute-start.1 = (bf16[4,16,256]{2,1,0:T(8,128)(2,1)S(1)}, bf16[4,16,256]{2,1,0:T(8,128)(2,1)S(1)}, u32[]{:S(2)}, u32[]{:S(2)}) collective-permute-start(bf16[4,16,256]{2,1,0:T(8,128)(2,1)S(1)} %get-tuple-element.67), channel_id=1, source_target_pairs={{2,0},{4,2},{6,4},{8,6},{10,8},{12,10},{14,12},{16,14},{18,16},{20... | collective-permute-start | bytes 98312 | tf_op jit(solution)/shard_map/ppermute | solution.py:842
  100.3 7.6 %collective-permute-start.2 = (bf16[1600,256]{1,0:T(8,128)(2,1)}, bf16[1600,256]{1,0:T(8,128)(2,1)S(1)}, u32[]{:S(2)}, u32[]{:S(2)}) collective-permute-start(bf16[1600,256]{1,0:T(8,128)(2,1)} %get-tuple-element.85), channel_id=1, source_target_pairs={{0,2},{2,0},{4,6},{6,4},{8,10},{10,8},{12,14},{14,12},{16,18},{18,... | collective-permute-start | bytes 2457608 | tf_op jit(solution)/shard_map/ppermute | solution.py:847
  103.2 9.0 %collective-permute-start.19 = (bf16[400,256]{1,0:T(8,128)(2,1)S(1)}, bf16[400,256]{1,0:T(8,128)(2,1)S(1)}, u32[]{:S(2)}, u32[]{:S(2)}) collective-permute-start(bf16[400,256]{1,0:T(8,128)(2,1)S(1)} %get-tuple-element.110), channel_id=1, source_target_pairs={{0,4},{1,5},{2,6},{3,7},{4,0},{5,1},{6,2},{7,3},{8,12},{9,13},{10,... | collective-permute-start | bytes 614408 | tf_op jit(solution)/shard_map/ppermute | solution.py:892
  106.3 9.7 %collective-permute-start.18 = (bf16[400,256]{1,0:T(8,128)(2,1)S(1)}, bf16[400,256]{1,0:T(8,128)(2,1)S(1)}, u32[]{:S(2)}, u32[]{:S(2)}) collective-permute-start(bf16[400,256]{1,0:T(8,128)(2,1)S(1)} %get-tuple-element.111), channel_id=1, source_target_pairs={{0,1},{1,0},{2,3},{3,2},{4,5},{5,4},{6,7},{7,6},{8,9},{9,8},{10,11... | collective-permute-start | bytes 614408 | tf_op jit(solution)/shard_map/ppermute | solution.py:892
  107.8 10.4 %collective-permute-start.17 = (bf16[400,256]{1,0:T(8,128)(2,1)S(1)}, bf16[400,256]{1,0:T(8,128)(2,1)S(1)}, u32[]{:S(2)}, u32[]{:S(2)}) collective-permute-start(bf16[400,256]{1,0:T(8,128)(2,1)S(1)} %get-tuple-element.109), channel_id=1, source_target_pairs={{0,5},{1,4},{2,7},{3,6},{4,1},{5,0},{6,3},{7,2},{8,13},{9,12},{10,... | collective-permute-start | bytes 614408 | tf_op jit(solution)/shard_map/ppermute | solution.py:892
  108.1 14.4 %collective-permute-start.5 = (bf16[400,256]{1,0:T(8,128)(2,1)S(1)}, bf16[400,256]{1,0:T(8,128)(2,1)S(1)}, u32[]{:S(2)}, u32[]{:S(2)}) collective-permute-start(bf16[400,256]{1,0:T(8,128)(2,1)S(1)} %get-tuple-element.113), channel_id=1, source_target_pairs={{0,4},{1,5},{2,6},{3,7},{4,0},{5,1},{6,2},{7,3},{8,12},{9,13},{10,... | collective-permute-start | bytes 614408 | tf_op jit(solution)/shard_map/ppermute | solution.py:892
  110.1 13.0 %collective-permute-start.4 = (bf16[400,256]{1,0:T(8,128)(2,1)S(1)}, bf16[400,256]{1,0:T(8,128)(2,1)S(1)}, u32[]{:S(2)}, u32[]{:S(2)}) collective-permute-start(bf16[400,256]{1,0:T(8,128)(2,1)S(1)} %get-tuple-element.114), channel_id=1, source_target_pairs={{0,1},{1,0},{2,3},{3,2},{4,5},{5,4},{6,7},{7,6},{8,9},{9,8},{10,11... | collective-permute-start | bytes 614408 | tf_op jit(solution)/shard_map/ppermute | solution.py:892
  112.3 13.9 %collective-permute-start.3 = (bf16[400,256]{1,0:T(8,128)(2,1)S(1)}, bf16[400,256]{1,0:T(8,128)(2,1)S(1)}, u32[]{:S(2)}, u32[]{:S(2)}) collective-permute-start(bf16[400,256]{1,0:T(8,128)(2,1)S(1)} %get-tuple-element.112), channel_id=1, source_target_pairs={{0,5},{1,4},{2,7},{3,6},{4,1},{5,0},{6,3},{7,2},{8,13},{9,12},{10,... | collective-permute-start | bytes 614408 | tf_op jit(solution)/shard_map/ppermute | solution.py:892
  118.4 11.8 %collective-permute-start.22 = (bf16[100,256]{1,0:T(8,128)(2,1)S(1)}, bf16[100,256]{1,0:T(8,128)(2,1)S(1)}, u32[]{:S(2)}, u32[]{:S(2)}) collective-permute-start(bf16[100,256]{1,0:T(8,128)(2,1)S(1)} %get-tuple-element.116), channel_id=1, source_target_pairs={{0,24},{2,26},{4,28},{6,30},{8,16},{10,18},{12,20},{14,22},{16,8},... | collective-permute-start | bytes 153608 | tf_op jit(solution)/shard_map/ppermute | solution.py:866
  122.5 8.3 %collective-permute-start.21 = (bf16[100,256]{1,0:T(8,128)(2,1)S(1)}, bf16[100,256]{1,0:T(8,128)(2,1)S(1)}, u32[]{:S(2)}, u32[]{:S(2)}) collective-permute-start(bf16[100,256]{1,0:T(8,128)(2,1)S(1)} %get-tuple-element.117), channel_id=1, source_target_pairs={{0,16},{2,18},{4,20},{6,22},{8,24},{10,26},{12,28},{14,30},{16,0},... | collective-permute-start | bytes 153608 | tf_op jit(solution)/shard_map/ppermute | solution.py:866
  122.5 8.3 %collective-permute-start.20 = (bf16[100,256]{1,0:T(8,128)(2,1)S(1)}, bf16[100,256]{1,0:T(8,128)(2,1)S(1)}, u32[]{:S(2)}, u32[]{:S(2)}) collective-permute-start(bf16[100,256]{1,0:T(8,128)(2,1)S(1)} %get-tuple-element.115), channel_id=1, source_target_pairs={{0,8},{2,10},{4,12},{6,14},{8,0},{10,2},{12,4},{14,6},{16,24},{18,... | collective-permute-start | bytes 153608 | tf_op jit(solution)/shard_map/ppermute | solution.py:866
  126.3 8.4 %collective-permute-start.8 = (bf16[100,256]{1,0:T(8,128)(2,1)S(1)}, bf16[100,256]{1,0:T(8,128)(2,1)S(1)}, u32[]{:S(2)}, u32[]{:S(2)}) collective-permute-start(bf16[100,256]{1,0:T(8,128)(2,1)S(1)} %get-tuple-element.119), channel_id=1, source_target_pairs={{0,24},{2,26},{4,28},{6,30},{8,16},{10,18},{12,20},{14,22},{16,8},... | collective-permute-start | bytes 153608 | tf_op jit(solution)/shard_map/ppermute | solution.py:866
  130.1 6.0 %collective-permute-start.7 = (bf16[100,256]{1,0:T(8,128)(2,1)S(1)}, bf16[100,256]{1,0:T(8,128)(2,1)S(1)}, u32[]{:S(2)}, u32[]{:S(2)}) collective-permute-start(bf16[100,256]{1,0:T(8,128)(2,1)S(1)} %get-tuple-element.120), channel_id=1, source_target_pairs={{0,16},{2,18},{4,20},{6,22},{8,24},{10,26},{12,28},{14,30},{16,0},... | collective-permute-start | bytes 153608 | tf_op jit(solution)/shard_map/ppermute | solution.py:866
  130.1 6.0 %collective-permute-start.6 = (bf16[100,256]{1,0:T(8,128)(2,1)S(1)}, bf16[100,256]{1,0:T(8,128)(2,1)S(1)}, u32[]{:S(2)}, u32[]{:S(2)}) collective-permute-start(bf16[100,256]{1,0:T(8,128)(2,1)S(1)} %get-tuple-element.118), channel_id=1, source_target_pairs={{0,8},{2,10},{4,12},{6,14},{8,0},{10,2},{12,4},{14,6},{16,24},{18,... | collective-permute-start | bytes 153608 | tf_op jit(solution)/shard_map/ppermute | solution.py:866
  130.8 8.4 %collective-permute-start.25 = (bf16[100,256]{1,0:T(8,128)(2,1)S(1)}, bf16[100,256]{1,0:T(8,128)(2,1)S(1)}, u32[]{:S(2)}, u32[]{:S(2)}) collective-permute-start(bf16[100,256]{1,0:T(8,128)(2,1)S(1)} %add_convert_fusion.4), channel_id=1, source_target_pairs={{0,8},{2,10},{4,12},{6,14},{8,0},{10,2},{12,4},{14,6},{16,24},{18,... | collective-permute-start | bytes 153608 | tf_op jit(solution)/shard_map/ppermute | solution.py:866
  132.3 7.5 %collective-permute-start.23 = (bf16[100,256]{1,0:T(8,128)(2,1)S(1)}, bf16[100,256]{1,0:T(8,128)(2,1)S(1)}, u32[]{:S(2)}, u32[]{:S(2)}) collective-permute-start(bf16[100,256]{1,0:T(8,128)(2,1)S(1)} %add_convert_fusion.4), channel_id=1, source_target_pairs={{0,24},{2,26},{4,28},{6,30},{8,16},{10,18},{12,20},{14,22},{16,8},... | collective-permute-start | bytes 153608 | tf_op jit(solution)/shard_map/ppermute | solution.py:866
  134.7 7.0 %collective-permute-start.24 = (bf16[100,256]{1,0:T(8,128)(2,1)S(1)}, bf16[100,256]{1,0:T(8,128)(2,1)S(1)}, u32[]{:S(2)}, u32[]{:S(2)}) collective-permute-start(bf16[100,256]{1,0:T(8,128)(2,1)S(1)} %add_convert_fusion.4), channel_id=1, source_target_pairs={{0,16},{2,18},{4,20},{6,22},{8,24},{10,26},{12,28},{14,30},{16,0},... | collective-permute-start | bytes 153608 | tf_op jit(solution)/shard_map/ppermute | solution.py:866
  136.2 8.7 %collective-permute-start.11 = (bf16[100,256]{1,0:T(8,128)(2,1)S(1)}, bf16[100,256]{1,0:T(8,128)(2,1)S(1)}, u32[]{:S(2)}, u32[]{:S(2)}) collective-permute-start(bf16[100,256]{1,0:T(8,128)(2,1)S(1)} %add_convert_fusion.5), channel_id=1, source_target_pairs={{0,8},{2,10},{4,12},{6,14},{8,0},{10,2},{12,4},{14,6},{16,24},{18,... | collective-permute-start | bytes 153608 | tf_op jit(solution)/shard_map/ppermute | solution.py:866
  137.1 8.3 %collective-permute-start.9 = (bf16[100,256]{1,0:T(8,128)(2,1)S(1)}, bf16[100,256]{1,0:T(8,128)(2,1)S(1)}, u32[]{:S(2)}, u32[]{:S(2)}) collective-permute-start(bf16[100,256]{1,0:T(8,128)(2,1)S(1)} %add_convert_fusion.5), channel_id=1, source_target_pairs={{0,24},{2,26},{4,28},{6,30},{8,16},{10,18},{12,20},{14,22},{16,8},... | collective-permute-start | bytes 153608 | tf_op jit(solution)/shard_map/ppermute | solution.py:866
  139.2 6.2 %collective-permute-start.10 = (bf16[100,256]{1,0:T(8,128)(2,1)S(1)}, bf16[100,256]{1,0:T(8,128)(2,1)S(1)}, u32[]{:S(2)}, u32[]{:S(2)}) collective-permute-start(bf16[100,256]{1,0:T(8,128)(2,1)S(1)} %add_convert_fusion.5), channel_id=1, source_target_pairs={{0,16},{2,18},{4,20},{6,22},{8,24},{10,26},{12,28},{14,30},{16,0},... | collective-permute-start | bytes 153608 | tf_op jit(solution)/shard_map/ppermute | solution.py:866
  141.8 9.2 %collective-permute-start.28 = (bf16[400,256]{1,0:T(8,128)(2,1)S(1)}, bf16[400,256]{1,0:T(8,128)(2,1)S(1)}, u32[]{:S(2)}, u32[]{:S(2)}) collective-permute-start(bf16[400,256]{1,0:T(8,128)(2,1)S(1)} %maximum_select_fusion.1), channel_id=1, source_target_pairs={{0,5},{1,4},{2,7},{3,6},{4,1},{5,0},{6,3},{7,2},{8,13},{9,12},{10,... | collective-permute-start | bytes 614408 | tf_op jit(solution)/shard_map/ppermute | solution.py:892
  143.6 11.4 %collective-permute-start.27 = (bf16[400,256]{1,0:T(8,128)(2,1)S(1)}, bf16[400,256]{1,0:T(8,128)(2,1)S(1)}, u32[]{:S(2)}, u32[]{:S(2)}) collective-permute-start(bf16[400,256]{1,0:T(8,128)(2,1)S(1)} %maximum_select_fusion.1), channel_id=1, source_target_pairs={{0,4},{1,5},{2,6},{3,7},{4,0},{5,1},{6,2},{7,3},{8,12},{9,13},{10,... | collective-permute-start | bytes 614408 | tf_op jit(solution)/shard_map/ppermute | solution.py:892
  144.8 10.2 %collective-permute-start.26 = (bf16[400,256]{1,0:T(8,128)(2,1)S(1)}, bf16[400,256]{1,0:T(8,128)(2,1)S(1)}, u32[]{:S(2)}, u32[]{:S(2)}) collective-permute-start(bf16[400,256]{1,0:T(8,128)(2,1)S(1)} %maximum_select_fusion.1), channel_id=1, source_target_pairs={{0,1},{1,0},{2,3},{3,2},{4,5},{5,4},{6,7},{7,6},{8,9},{9,8},{10,11... | collective-permute-start | bytes 614408 | tf_op jit(solution)/shard_map/ppermute | solution.py:892
  145.5 12.1 %collective-permute-start.14 = (bf16[400,256]{1,0:T(8,128)(2,1)S(1)}, bf16[400,256]{1,0:T(8,128)(2,1)S(1)}, u32[]{:S(2)}, u32[]{:S(2)}) collective-permute-start(bf16[400,256]{1,0:T(8,128)(2,1)S(1)} %maximum_select_fusion), channel_id=1, source_target_pairs={{0,5},{1,4},{2,7},{3,6},{4,1},{5,0},{6,3},{7,2},{8,13},{9,12},{10,... | collective-permute-start | bytes 614408 | tf_op jit(solution)/shard_map/ppermute | solution.py:892
  147.3 12.1 %collective-permute-start.13 = (bf16[400,256]{1,0:T(8,128)(2,1)S(1)}, bf16[400,256]{1,0:T(8,128)(2,1)S(1)}, u32[]{:S(2)}, u32[]{:S(2)}) collective-permute-start(bf16[400,256]{1,0:T(8,128)(2,1)S(1)} %maximum_select_fusion), channel_id=1, source_target_pairs={{0,4},{1,5},{2,6},{3,7},{4,0},{5,1},{6,2},{7,3},{8,12},{9,13},{10,... | collective-permute-start | bytes 614408 | tf_op jit(solution)/shard_map/ppermute | solution.py:892
  151.0 8.6 %collective-permute-start.12 = (bf16[400,256]{1,0:T(8,128)(2,1)S(1)}, bf16[400,256]{1,0:T(8,128)(2,1)S(1)}, u32[]{:S(2)}, u32[]{:S(2)}) collective-permute-start(bf16[400,256]{1,0:T(8,128)(2,1)S(1)} %maximum_select_fusion), channel_id=1, source_target_pairs={{0,1},{1,0},{2,3},{3,2},{4,5},{5,4},{6,7},{7,6},{8,9},{9,8},{10,11... | collective-permute-start | bytes 614408 | tf_op jit(solution)/shard_map/ppermute | solution.py:892
  155.1 4.7 %collective-permute-start.29 = (bf16[1600,256]{1,0:T(8,128)(2,1)S(1)}, bf16[1600,256]{1,0:T(8,128)(2,1)S(1)}, u32[]{:S(2)}, u32[]{:S(2)}) collective-permute-start(bf16[1600,256]{1,0:T(8,128)(2,1)S(1)} %pad_maximum_fusion.1.refs_2_), channel_id=1, source_target_pairs={{0,2},{2,0},{4,6},{6,4},{8,10},{10,8},{12,14},{14,12},{16,18},{18,... | collective-permute-start | bytes 2457608 | tf_op jit(solution)/shard_map/ppermute | solution.py:847
  159.7 2.4 %collective-permute-start.15 = (bf16[1600,256]{1,0:T(8,128)(2,1)S(1)}, bf16[1600,256]{1,0:T(8,128)(2,1)S(1)}, u32[]{:S(2)}, u32[]{:S(2)}) collective-permute-start(bf16[1600,256]{1,0:T(8,128)(2,1)S(1)} %pad_maximum_fusion.refs_0_), channel_id=1, source_target_pairs={{0,2},{2,0},{4,6},{6,4},{8,10},{10,8},{12,14},{14,12},{16,18},{18,... | collective-permute-start | bytes 2457608 | tf_op jit(solution)/shard_map/ppermute | solution.py:847
  (21 other events, 481.4 us)
